TPU v7x, 256 devices: a whole 4x4x8 slice. The times are simulated.
256 devices in a mesh: replica: 32 (over x, z_hi, core), fsdp: 8 (over y, z_lo).
Axes of the slice: x: 4, y: 4, z: 8 (z_hi: 4, z_lo: 2; z = z_hi * 2 + z_lo), core: 2. Of those that a mesh axis runs over, the one named last changes fastest.
Arguments:
- local_frag: bfloat16 [32, 2048, 8192], P('replica', 'fsdp'), may hold values from -6 to 6
- master: float32 [2048, 8192], P('fsdp', 'replica'), may hold values from -6 to 6
- momentum: float32 [2048, 8192], P('fsdp', 'replica'), may hold values from -3 to 3
- counts: int32 [32], P('replica'), may hold values from 1024 to 3072, as said below
- inputs: bfloat16 [32768, 8192], P(('replica', 'fsdp')), may hold values from -6 to 6
- inner_weight: bfloat16 [32, 512, 8192], P('replica', 'fsdp'), may hold values from -0.0625 to 0.0625
- cotangent: bfloat16 [32768, 512], P(('replica', 'fsdp')), may hold values from -6 to 6
Outputs:
- new_master: float32 [2048, 8192], P('fsdp', 'replica')
- new_momentum: float32 [2048, 8192], P('fsdp', 'replica')
- projected: bfloat16 [32768, 512], P(('replica', 'fsdp'))
- input_grad: bfloat16 [32768, 8192], P(('replica', 'fsdp'))
- weight_grad: bfloat16 [32, 512, 8192], P('replica', 'fsdp')
Inputs may be any that keep to these rules, and one draw needn't show every extreme that they name: `counts`: one count a replica; the first replica has the least and the last the most.
All inputs are finite; a program needn't handle non-finite values.
Results may differ from a plain program's by a relative error of at most 0.017.
Values may be sent and summed in bfloat16 or wider, within the bound.
No kernel may reach another device: no remote copies, remote signals or barrier semaphores. Data moves between devices by JAX's collectives and lax.ppermute only.
A program may use at most 128 MiB of HBM per device.

v0:
```python
import jax
import jax.numpy as jnp
from jax import lax
from jax.sharding import PartitionSpec as P

momentum_decay = 0.9
outer_rate = 0.7


def local(local_frag, master, momentum, counts, inputs, inner_weight, cotangent):
    count_value = counts.astype(jnp.float32)
    count_sum = lax.psum(jnp.sum(count_value), "replica")
    factor = count_value[0] / count_sum
    shares = lax.psum_scatter(
        local_frag[0].astype(jnp.float32) * factor, "replica", scatter_dimension=1, tiled=True
    )
    pseudo_grad = master - shares
    new_momentum = momentum_decay * momentum + pseudo_grad
    new_master = master - outer_rate * (pseudo_grad + momentum_decay * new_momentum)
    weight_shard = inner_weight[0]
    token_rows = inputs.shape[0]
    contract_rows = (((1,), (1,)), ((), ()))
    gathered = lax.all_gather(weight_shard, "fsdp", axis=0, tiled=True)
    keys_full = lax.dot_general(inputs, gathered, contract_rows, preferred_element_type=jnp.float32)
    back_full = jnp.dot(cotangent, gathered, preferred_element_type=jnp.float32)
    grad_scale = 1.0 / (token_rows * lax.axis_size("fsdp"))
    product = lax.dot_general(
        cotangent, inputs, (((0,), (0,)), ((), ())), preferred_element_type=jnp.float32
    )
    grads = lax.psum_scatter(
        (product * grad_scale).astype(jnp.bfloat16), "fsdp", scatter_dimension=0, tiled=True
    )
    return (
        new_master,
        new_momentum,
        keys_full.astype(jnp.bfloat16),
        back_full.astype(jnp.bfloat16),
        grads[None],
    )


def solution(mesh):
    placed = (
        P("replica", "fsdp", None),
        P("fsdp", "replica"),
        P("fsdp", "replica"),
        P("replica"),
        P(("replica", "fsdp"), None),
        P("replica", "fsdp", None),
        P(("replica", "fsdp"), None),
    )
    return jax.shard_map(
        local,
        mesh=mesh,
        in_specs=placed,
        out_specs=(
            P("fsdp", "replica"),
            P("fsdp", "replica"),
            P(("replica", "fsdp"), None),
            P(("replica", "fsdp"), None),
            P("replica", "fsdp", None),
        ),
        check_vma=False,
    )
```

profile of v0, /device:TPU:8, one launch (start us, length us, event | category | flops | bytes accessed | tf_op | source)
XLA Modules:
  0.0 490.4 jit_solution(4147943977009235217)
XLA Ops:
  8.0 0.0 copy-start
  8.0 0.0 reduce-scatter.3.cloned.1.call-start
  8.8 78.9 %psum.7 = f32[]{:T(128)} all-reduce(f32[]{:T(128)} %bitcast), channel_id=1, replica_groups=mesh['replica'=32,'fsdp'=8] {'replica'}, use_global_device_ids=true, to_apply=%region_0.0 | all-reduce | flops 1 | bytes 8 | tf_op jit(solution)/shard_map/psum | solution.py:12
  88.4 0.0 copy-start.2
  88.4 6.5 %multiply_bitcast_fusion = f32[256,8192]{1,0:T(8,128)} fusion(bf16[1,256,8192]{2,1,0:T(8,128)(2,1)} %param.7, f32[]{:T(128)S(6)} %div.3), kind=kLoop, calls=%fused_computation.5 | loop fusion | flops 4194304 | bytes 12582916 | tf_op jit(solution)/shard_map/mul | solution.py:15
  94.9 0.0 reduce-scatter.3.cloned.1.call-update
  94.9 0.0 all-gather.3.cloned.1.call-start
  94.9 0.5 all-gather.3.cloned.1.call-update
  95.5 0.0 copy-start.3
  95.5 0.0 copy-start.4
  95.5 0.0 reduce-scatter.5.cloned.1.call-start
  95.5 0.0 copy-done
  95.6 0.0 copy-done.2
  95.6 5.6 %multiply_convert_fusion = bf16[512,8192]{1,0:T(8,128)(2,1)} fusion(bf16[128,512]{1,0:T(8,128)(2,1)S(1)} %copy-done.2, bf16[128,8192]{1,0:T(8,128)(2,1)S(1)} %copy-done), kind=kOutput, calls=%fused_computation | convolution fusion | flops 1082130432 | bytes 10616832 | tf_op jit(solution)/shard_map/dot_general | solution.py:27
  101.2 0.0 reduce-scatter.5.cloned.1.call-update
  101.2 208.8 %reduce-scatter.3.cloned.1.call-done = f32[256,256]{1,0:T(8,128)} async-done(((f32[256,8192]{1,0:T(8,128)}), f32[256,256]{1,0:T(8,128)}) %reduce-scatter.3.cloned.1.call-update) | async-done | bytes 262160 | tf_op jit(solution)/shard_map/reduce_scatter | solution.py:14
  310.0 0.0 copy-done.3
  310.0 0.0 copy-done.4
  310.0 1.8 multiply_subtract_fusion
  311.8 0.0 all-gather.3.cloned.1.call-done
  311.8 0.0 copy-start.1
  311.8 6.1 %convolution_convert_fusion = bf16[128,8192]{1,0:T(8,128)(2,1)} fusion(bf16[128,512]{1,0:T(8,128)(2,1)S(1)} %copy-done.2, bf16[1,512,8192]{2,1,0:T(8,128)(2,1)} %all-gather.3.cloned.1.call-done), kind=kOutput, calls=%fused_computation.1 | convolution fusion | flops 1074790400 | bytes 10616832 | tf_op jit(solution)/shard_map/dot_general | solution.py:25
  317.9 0.0 copy-done.1
  317.9 3.6 fusion.3
  321.5 161.5 %reduce-scatter.5.cloned.1.call-done = bf16[64,8192]{1,0:T(8,128)(2,1)} async-done(((bf16[512,8192]{1,0:T(8,128)(2,1)}), bf16[64,8192]{1,0:T(8,128)(2,1)}) %reduce-scatter.5.cloned.1.call-update) | async-done | bytes 1048592 | tf_op jit(solution)/shard_map/reduce_scatter | solution.py:30
Async XLA Ops:
  8.0 87.5 %copy-start = (bf16[128,8192]{1,0:T(8,128)(2,1)S(1)}, bf16[128,8192]{1,0:T(8,128)(2,1)}, u32[]{:S(2)}) copy-start(bf16[128,8192]{1,0:T(8,128)(2,1)} %param.11) | copy-start | bytes 6291460
  8.0 302.0 %reduce-scatter.3.cloned.1.call-start = ((), (), s32[]{:S(2)}) async-start(), calls=%async_computation.2 | async-start | bytes 8650752 | tf_op jit(solution)/shard_map/reduce_scatter | solution.py:14
  88.4 7.2 %copy-start.2 = (bf16[128,512]{1,0:T(8,128)(2,1)S(1)}, bf16[128,512]{1,0:T(8,128)(2,1)}, u32[]{:S(2)}) copy-start(bf16[128,512]{1,0:T(8,128)(2,1)} %param.13) | copy-start | bytes 393220
  94.9 216.9 %all-gather.3.cloned.1.call-start = ((), (), s32[]{:S(2)}) async-start(), calls=%async_computation.4 | async-start | bytes 9437184 | tf_op jit(solution)/shard_map/all_gather | solution.py:23
  95.5 214.5 %copy-start.3 = (f32[256,256]{1,0:T(8,128)S(1)}, f32[256,256]{1,0:T(8,128)}, u32[]{:S(2)}) copy-start(f32[256,256]{1,0:T(8,128)} %param.8) | copy-start | bytes 786436
  95.5 214.5 %copy-start.4 = (f32[256,256]{1,0:T(8,128)S(1)}, f32[256,256]{1,0:T(8,128)}, u32[]{:S(2)}) copy-start(f32[256,256]{1,0:T(8,128)} %param.9) | copy-start | bytes 786436
  95.5 387.5 %reduce-scatter.5.cloned.1.call-start = ((), (), s32[]{:S(2)}) async-start(), calls=%async_computation.3 | async-start | bytes 9437184 | tf_op jit(solution)/shard_map/reduce_scatter | solution.py:30
  311.8 6.1 %copy-start.1 = (bf16[1,512,8192]{2,1,0:T(8,128)(2,1)S(1)}, bf16[1,512,8192]{2,1,0:T(8,128)(2,1)}, u32[]{:S(2)}) copy-start(bf16[1,512,8192]{2,1,0:T(8,128)(2,1)} %all-gather.3.cloned.1.call-done) | copy-start | bytes 25165828
Sparse Core Ops, SparseCore 0:
  95.0 214.9 reduce-scatter.2
  313.3 169.6 reduce-scatter.4
Sparse Core Ops, SparseCore 1:
  97.3 203.4 all-gather.2
where the time goes:
time: 492 us; the launch traced here: 490 us
  waiting for transfers between devices  371 us (75%)
  blocking collectives  78.9 us (16%)
  between operations  17 us (3%)
  matrix products  15.3 us (3%)
  other arithmetic  8.26 us (2%)
    reduce_scatter x1, waiting for transfers between devices, local(): lax.psum_scatter(local_frag[0].astype(jnp.float32) * factor, 'replica', s...  209 us
    reduce_scatter x1, waiting for transfers between devices, local(): lax.psum_scatter((product * grad_scale).astype(jnp.bfloat16), 'fsdp', sca...  161 us
    psum x1, blocking collectives, local(): count_sum = lax.psum(jnp.sum(count_value), 'replica')  78.9 us
  transfers between devices with their start and end apart: 3, of which 2 were waited for; matrix products, arithmetic and copies ran while one was open for 3% of the time, Pallas kernels for 0%

commit v1 on v0

v1 whole, which is shorter than its diff:
```python
import functools

import jax
import jax.numpy as jnp
from jax import lax
from jax.experimental import pallas as pl
from jax.experimental.pallas import tpu as pltpu
from jax.sharding import PartitionSpec as P

momentum_decay = 0.9
outer_rate = 0.7

F32, BF16 = jnp.float32, jnp.bfloat16
ANY = pl.BlockSpec(memory_space=pl.ANY)
VMEM = pl.BlockSpec(memory_space=pltpu.VMEM)
SMEM = pl.BlockSpec(memory_space=pltpu.SMEM)

SEG = 2048
ROWS = 64
TOK = 128
KVI = 512


def y_shift(k):
    return [(f, (f + 2 * k) % 8) for f in range(8)]


Z_SWAP = [(f, f ^ 1) for f in range(8)]
CORE_SWAP = [(r, r ^ 1) for r in range(32)]


def x_shift(k):
    return [(r, (r + 8 * k) % 32) for r in range(32)]


def zh_shift(k):
    return [(r, r // 8 * 8 + (r + 2 * k) % 8) for r in range(32)]


def call(kernel, name, ins, outs, scratch=(), limit=24, flops=0):
    arrays = [a for _, a in ins]
    moved = sum(a.size * a.dtype.itemsize for a in arrays) + sum(
        int(jnp.dtype(o.dtype).itemsize) * o.size for _, o in outs
    )
    return pl.pallas_call(
        kernel,
        name=name,
        in_specs=[s for s, _ in ins],
        out_specs=[s for s, _ in outs],
        out_shape=[o for _, o in outs],
        scratch_shapes=list(scratch),
        compiler_params=pltpu.CompilerParams(vmem_limit_bytes=limit << 20),
        cost_estimate=pl.CostEstimate(flops=flops, bytes_accessed=moved, transcendentals=0),
    )(*arrays)


def shape(*dims, dtype=BF16):
    return jax.ShapeDtypeStruct(dims, dtype)


def here():
    f = lax.axis_index("fsdp")
    return f // 2, f % 2


def run_all(copies):
    for c in copies:
        c.start()
    for c in copies:
        c.wait()


def pack_weight(w, cot, *rest):
    outs, sems = rest[:4], rest[4]
    y, _ = here()
    copies = []
    for k in range(4):
        start = pl.multiple_of((y + k) % 4 * SEG, SEG)
        copies.append((w.at[:, pl.ds(start, SEG)], outs[k].at[pl.ds(0, ROWS)]))
        for j in range(4):
            copies.append((cot.at[pl.ds(32 * j, 32)], outs[k].at[pl.ds(ROWS, 32), pl.ds(KVI * j, KVI)]))
    run_all([pltpu.make_async_copy(s, d, sems.at[i]) for i, (s, d) in enumerate(copies)])


def pack_inputs(x, *rest):
    outs, sems = rest[:4], rest[4]
    y, _ = here()
    copies = []
    for k in range(4):
        start = pl.multiple_of((y + k) % 4 * SEG, SEG)
        copies.append(pltpu.make_async_copy(x.at[:, pl.ds(start, SEG)], outs[k], sems.at[k]))
    run_all(copies)


def unpack_columns(*refs):
    parts, out, sems = refs[:4], refs[4], refs[5]
    y, _ = here()
    copies = []
    for k in range(4):
        start = pl.multiple_of((y + k) % 4 * SEG, SEG)
        copies.append(pltpu.make_async_copy(parts[k], out.at[:, pl.ds(start, SEG)], sems.at[k]))
    run_all(copies)


def grad_to_inputs(*refs):
    got, other, outs, w, cots = refs[:4], refs[4:8], refs[8:12], refs[12], refs[13]
    y, z = here()
    for k in range(4):
        owner = (y + 4 - k) % 4
        w[pl.ds(pl.multiple_of((owner * 2 + z) * ROWS, ROWS), ROWS), :] = got[k][0:ROWS, :]
        w[pl.ds(pl.multiple_of((owner * 2 + 1 - z) * ROWS, ROWS), ROWS), :] = other[k][...]
        for j in range(4):
            cots[TOK * k + 32 * j : TOK * k + 32 * j + 32, :] = got[k][ROWS : ROWS + 32, KVI * j : KVI * j + KVI]
    for c in range(0, SEG, 512):
        part = jnp.dot(cots[...], w[:, c : c + 512], preferred_element_type=F32).astype(BF16)
        for k in range(4):
            outs[k][:, c : c + 512] = part[TOK * k : TOK * k + TOK]


def weight_grad(scale, *refs):
    xs, cots, mine, other, whole = refs[:4], refs[4], refs[5], refs[6], refs[7]
    y, z = here()
    for c in range(0, SEG, 256):
        total = None
        for k in range(4):
            term = lax.dot_general(
                cots[TOK * k : TOK * k + TOK, :],
                xs[k][:, c : c + 256],
                (((0,), (0,)), ((), ())),
                preferred_element_type=F32,
            )
            total = term if total is None else total + term
        whole[:, c : c + 256] = (total * scale).astype(BF16)
    for j in range(4):
        to = (y + j) % 4 * 2
        rows = slice(ROWS * j, ROWS * j + ROWS)
        mine[rows, :] = whole[pl.ds(pl.multiple_of((to + z) * ROWS, ROWS), ROWS), :]
        other[rows, :] = whole[pl.ds(pl.multiple_of((to + 1 - z) * ROWS, ROWS), ROWS), :]


def project(*refs):
    xs, w, outs = refs[:4], refs[4], refs[5:9]
    for k in range(4):
        outs[k][...] = lax.dot_general(
            xs[k][...], w[...], (((1,), (1,)), ((), ())), preferred_element_type=F32
        ).astype(BF16)


def join_grads(mine, recv, *refs):
    parts, outs = refs[:4], refs[4:8]
    for j in range(4):
        rows = slice(ROWS * j, ROWS * j + ROWS)
        outs[j][0:ROWS, :] = (mine[rows, :].astype(F32) + recv[rows, :].astype(F32)).astype(BF16)
        for i in range(4):
            outs[j][ROWS : ROWS + 32, KVI * i : KVI * i + KVI] = parts[(4 - j) % 4][32 * i : 32 * i + 32, :]


def finish(*refs):
    got, grads, keys = refs[:4], refs[4], refs[5]
    y, _ = here()
    for j in range(4):
        owner = (y + 4 - j) % 4
        grads[:, pl.ds(pl.multiple_of(owner * SEG, SEG), SEG)] = got[j][0:ROWS, :]
    for i in range(4):
        total = None
        for j in range(4):
            term = got[j][ROWS : ROWS + 32, KVI * i : KVI * i + KVI].astype(F32)
            total = term if total is None else total + term
        keys[32 * i : 32 * i + 32, :] = total.astype(BF16)


def weigh(counts, mine, other, *outs):
    r = lax.axis_index("replica")
    x, core = r // 8, r % 2
    own, theirs = counts[0], counts[1]
    for k in range(4):
        for h in range(4):
            start = pl.multiple_of((x + k) % 4 * 2048 + h * 512 + core * 256, 256)
            cols = pl.ds(start, 256)
            total = own * mine[:, cols].astype(F32) + theirs * other[:, cols].astype(F32)
            outs[k][:, 256 * h : 256 * h + 256] = total.astype(BF16)


def weigh_grid(frag, frag_other, counts):
    step = 64
    spec_in = pl.BlockSpec((step, 8192), lambda i: (i, 0))
    spec_out = pl.BlockSpec((step, 1024), lambda i: (i, 0))
    return pl.pallas_call(
        weigh,
        name="weigh",
        grid=(256 // step,),
        in_specs=[SMEM, spec_in, spec_in],
        out_specs=[spec_out] * 4,
        out_shape=[shape(256, 1024)] * 4,
        compiler_params=pltpu.CompilerParams(vmem_limit_bytes=24 << 20),
        cost_estimate=pl.CostEstimate(flops=0, bytes_accessed=10 << 20, transcendentals=0),
    )(counts, frag, frag_other)


def sum_blocks(*refs):
    parts, outs = refs[:4], refs[4:8]
    zh = lax.axis_index("replica") // 2 % 4
    for j in range(4):
        cols = pl.ds(pl.multiple_of((zh + j) % 4 * 256, 256), 256)
        total = parts[0][:, cols].astype(F32)
        for p in parts[1:]:
            total = total + p[:, cols].astype(F32)
        outs[j][...] = total.astype(BF16)


def after(value, *others):
    return lax.optimization_barrier((value, *others))[0]


def local(local_frag, master, momentum, counts, inputs, inner_weight, cotangent):
    frag = local_frag[0]
    count = counts.astype(F32)
    frag_other = lax.ppermute(frag, "replica", CORE_SWAP)
    count_other = lax.ppermute(count, "replica", CORE_SWAP)

    dma = pltpu.SemaphoreType.DMA
    sent = call(
        pack_weight,
        "pack_weight",
        [(ANY, inner_weight[0]), (ANY, cotangent)],
        [(ANY, shape(ROWS + 32, SEG))] * 4,
        [dma((20,))],
    )
    got = [sent[0]] + [lax.ppermute(sent[k], "fsdp", y_shift(k)) for k in (1, 2, 3)]
    packed = call(pack_inputs, "pack_inputs", [(ANY, inputs)], [(ANY, shape(TOK, SEG))] * 4, [dma((4,))])
    packed = lax.optimization_barrier((*packed, *got))[:4]
    xs = [packed[0]] + [lax.ppermute(packed[k], "fsdp", y_shift(k)) for k in (1, 2, 3)]
    crossed = [lax.ppermute(g[:ROWS], "fsdp", Z_SWAP) for g in got]

    weights = jnp.concatenate([count, count_other])
    parts = weigh_grid(frag, frag_other, weights)
    pair = count + count_other
    parts = [parts[0]] + [lax.ppermute(parts[k], "replica", x_shift(k)) for k in (1, 2, 3)]
    quad = pair + sum(lax.ppermute(pair, "replica", x_shift(k)) for k in (1, 2, 3))

    flops = 2 * TOK * KVI * 8192
    *back, w_full, cots = call(
        grad_to_inputs,
        "input_grad",
        [(VMEM, a) for a in (*got, *crossed)],
        [(VMEM, shape(TOK, SEG))] * 4 + [(VMEM, shape(KVI, SEG)), (VMEM, shape(4 * TOK, KVI))],
        flops=flops,
    )
    back = [back[0]] + [lax.ppermute(back[k], "fsdp", y_shift(-k)) for k in (1, 2, 3)]

    mine, other = call(
        functools.partial(weight_grad, 1.0 / (TOK * lax.axis_size("fsdp"))),
        "weight_grad",
        [(VMEM, a) for a in (*xs, cots)],
        [(VMEM, shape(4 * ROWS, SEG))] * 2,
        [pltpu.VMEM((KVI, SEG), BF16)],
        flops=flops,
    )
    recv = lax.ppermute(other, "fsdp", Z_SWAP)
    keys = call(
        project,
        "project",
        [(VMEM, a) for a in (*xs, w_full)],
        [(VMEM, shape(TOK, KVI))] * 4,
        flops=flops,
    )

    blocks = call(sum_blocks, "sum_blocks", [(VMEM, a) for a in parts], [(VMEM, shape(256, 256))] * 4)
    blocks = lax.optimization_barrier((*blocks, recv))
    recv = blocks[4]
    shares = [blocks[0]] + [lax.ppermute(blocks[j], "replica", zh_shift(j)) for j in (1, 2, 3)]
    count_sum = quad + sum(lax.ppermute(quad, "replica", zh_shift(j)) for j in (1, 2, 3))

    joined = call(
        join_grads,
        "join_grads",
        [(VMEM, a) for a in (mine, recv, *keys)],
        [(VMEM, shape(ROWS + 32, SEG))] * 4,
    )
    joined = [joined[0]] + [lax.ppermute(joined[j], "fsdp", y_shift(j)) for j in (1, 2, 3)]

    (back_full,) = call(
        unpack_columns, "unpack_input_grad", [(ANY, a) for a in back], [(ANY, shape(TOK, 8192))], [dma((4,))]
    )

    total = shares[0].astype(F32)
    for s in shares[1:]:
        total = total + s.astype(F32)
    pseudo_grad = master - total / count_sum[0]
    new_momentum = momentum_decay * momentum + pseudo_grad
    new_master = master - outer_rate * (pseudo_grad + momentum_decay * new_momentum)

    grads, projected = call(
        finish, "finish", [(VMEM, a) for a in joined], [(VMEM, shape(ROWS, 8192)), (VMEM, shape(TOK, KVI))]
    )
    return new_master, new_momentum, projected, back_full, grads[None]


def solution(mesh):
    placed = (
        P("replica", "fsdp", None),
        P("fsdp", "replica"),
        P("fsdp", "replica"),
        P("replica"),
        P(("replica", "fsdp"), None),
        P("replica", "fsdp", None),
        P(("replica", "fsdp"), None),
    )
    return jax.shard_map(
        local,
        mesh=mesh,
        in_specs=placed,
        out_specs=(
            P("fsdp", "replica"),
            P("fsdp", "replica"),
            P(("replica", "fsdp"), None),
            P(("replica", "fsdp"), None),
            P("replica", "fsdp", None),
        ),
        check_vma=False,
    )
```

time: 492 us -> 151 us (0.31)
  waiting for transfers between devices: 371 us -> 70.2 us
  blocking collectives: 78.9 us -> 0 us
  starting transfers between devices: 0.12 us -> 59.7 us
  matrix products: 15.3 us -> 0 us
  Pallas kernels: 0 us -> 12 us
  between operations: 17 us -> 5.52 us
  other arithmetic: 8.26 us -> 1.54 us
    reduce_scatter x2 -> x0, waiting for transfers between devices: 370 us -> none  [the longest x1 209 us: local(): lax.psum_scatter(local_frag[0].astype(jnp.float32) * factor, 'replica', s...]
    psum x1 -> x0, blocking collectives: 78.9 us -> none  [local(): count_sum = lax.psum(jnp.sum(count_value), 'replica')]
    ppermute x0 -> x31, waiting for transfers between devices: none -> 70.2 us  [the longest x3 18.6 us: local(): lax.ppermute(parts[k], 'replica', x_shift(k))]
    ppermute x0 -> x31, starting transfers between devices: none -> 59.7 us  [the longest x3 9.35 us: local(): lax.ppermute(blocks[j], 'replica', zh_shift(j))]
    dot_general x3 -> x0, matrix products: 15.3 us -> none  [the longest x1 6.12 us: local(): back_full = jnp.dot(cotangent, gathered, preferred_element_type=jnp.float32)]
    pallas_call x0 -> x10, Pallas kernels: none -> 12 us  [the longest x9 10.5 us: call(): pl.pallas_call(kernel, name=name, in_specs=[s for s, _ in ins], out_specs...]
    mul x1 -> x0, other arithmetic: 6.45 us -> none  [local(): local_frag[0].astype(jnp.float32) * factor]
  transfers between devices with their start and end apart: 3 -> 31, of which waited for: 2 -> 17; matrix products, arithmetic and copies ran while one was open for 3% -> 1% of each run, Pallas kernels for 0% -> 7%
where the time goes in v1:
time: 151 us
  waiting for transfers between devices  70.2 us (46%)
  starting transfers between devices  59.7 us (40%)
  Pallas kernels  12 us (8%)
  between operations  5.52 us (4%)
  local copies, waits for them, and re-layouts  2.34 us (2%)
  other arithmetic  1.54 us (1%)
    ppermute x3, waiting for transfers between devices, local(): lax.ppermute(parts[k], 'replica', x_shift(k))  18.6 us
    ppermute x3, waiting for transfers between devices, local(): lax.ppermute(quad, 'replica', zh_shift(j))  12.1 us
    ppermute x3, waiting for transfers between devices, local(): lax.ppermute(sent[k], 'fsdp', y_shift(k))  11.6 us
    ppermute x3, waiting for transfers between devices, local(): lax.ppermute(packed[k], 'fsdp', y_shift(k))  10.7 us
    pallas_call x9, Pallas kernels, call(): pl.pallas_call(kernel, name=name, in_specs=[s for s, _ in ins], out_specs...  10.5 us
    ppermute x3, starting transfers between devices, local(): lax.ppermute(blocks[j], 'replica', zh_shift(j))  9.35 us
    ppermute x3, starting transfers between devices, local(): lax.ppermute(packed[k], 'fsdp', y_shift(k))  8.14 us
    ppermute x4, starting transfers between devices, local(): crossed = [lax.ppermute(g[:ROWS], 'fsdp', Z_SWAP) for g in got]  7.63 us
  transfers between devices with their start and end apart: 31, of which 17 were waited for; matrix products, arithmetic and copies ran while one was open for 1% of the time, Pallas kernels for 7%

profile of v1, /device:TPU:8, one launch (start us, length us, event | category | flops | bytes accessed | tf_op | source)
XLA Modules:
  0.0 151.2 jit_solution(6508834445424140621)
XLA Ops:
  0.6 0.1 collective-permute-start.1
  0.8 1.3 copy-done.2
  2.1 0.9 copy-done.3
  3.0 0.5 pack_weight.1
  3.5 1.7 %collective-permute-start.5 = (bf16[96,2048]{1,0:T(8,128)(2,1)S(1)}, bf16[96,2048]{1,0:T(8,128)(2,1)S(1)}, u32[]{:S(2)}, u32[]{:S(2)}) collective-permute-start(bf16[96,2048]{1,0:T(8,128)(2,1)S(1)} %get-tuple-element.61), channel_id=1, source_target_pairs={{0,2},{1,3},{2,4},{3,5},{4,6},{5,7},{6,0},{7,1},{8,10},{9,11},{10,... | collective-permute-start | bytes 1179656 | tf_op jit(solution)/shard_map/ppermute | solution.py:229
  5.1 2.7 %collective-permute-start.6 = (bf16[96,2048]{1,0:T(8,128)(2,1)S(1)}, bf16[96,2048]{1,0:T(8,128)(2,1)S(1)}, u32[]{:S(2)}, u32[]{:S(2)}) collective-permute-start(bf16[96,2048]{1,0:T(8,128)(2,1)S(1)} %get-tuple-element.62), channel_id=1, source_target_pairs={{0,4},{1,5},{2,6},{3,7},{4,0},{5,1},{6,2},{7,3},{8,12},{9,13},{10,... | collective-permute-start | bytes 1179656 | tf_op jit(solution)/shard_map/ppermute | solution.py:229
  7.8 0.7 collective-permute-start.7
  8.5 2.0 %collective-permute-start.11 = (bf16[64,2048]{1,0:T(8,128)(2,1)S(1)}, bf16[64,2048]{1,0:T(8,128)(2,1)S(1)}, u32[]{:S(2)}, u32[]{:S(2)}) collective-permute-start(bf16[64,2048]{1,0:T(8,128)(2,1)S(1)} %slice.12), channel_id=1, source_target_pairs={{0,1},{1,0},{2,3},{3,2},{4,5},{5,4},{6,7},{7,6},{8,9},{9,8},{10,11... | collective-permute-start | bytes 786440 | tf_op jit(solution)/shard_map/ppermute | solution.py:233
  10.5 5.2 %collective-permute-done.5.refs_1_ = bf16[96,2048]{1,0:T(8,128)(2,1)S(1)} collective-permute-done((bf16[96,2048]{1,0:T(8,128)(2,1)S(1)}, bf16[96,2048]{1,0:T(8,128)(2,1)S(1)}, u32[]{:S(2)}, u32[]{:S(2)}) %collective-permute-start.5) | collective-permute-done | bytes 393248 | tf_op jit(solution)/shard_map/ppermute | solution.py:229
  15.7 1.8 %collective-permute-start.12 = (bf16[64,2048]{1,0:T(8,128)(2,1)S(1)}, bf16[64,2048]{1,0:T(8,128)(2,1)S(1)}, u32[]{:S(2)}, u32[]{:S(2)}) collective-permute-start(bf16[64,2048]{1,0:T(8,128)(2,1)S(1)} %slice.16), channel_id=1, source_target_pairs={{0,1},{1,0},{2,3},{3,2},{4,5},{5,4},{6,7},{7,6},{8,9},{9,8},{10,11... | collective-permute-start | bytes 786440 | tf_op jit(solution)/shard_map/ppermute | solution.py:233
  17.5 1.1 collective-permute-done.6.refs_2_
  18.7 2.0 %collective-permute-start.13 = (bf16[64,2048]{1,0:T(8,128)(2,1)S(1)}, bf16[64,2048]{1,0:T(8,128)(2,1)S(1)}, u32[]{:S(2)}, u32[]{:S(2)}) collective-permute-start(bf16[64,2048]{1,0:T(8,128)(2,1)S(1)} %slice.17), channel_id=1, source_target_pairs={{0,1},{1,0},{2,3},{3,2},{4,5},{5,4},{6,7},{7,6},{8,9},{9,8},{10,11... | collective-permute-start | bytes 786440 | tf_op jit(solution)/shard_map/ppermute | solution.py:233
  20.7 0.2 pack_inputs.1
  20.9 5.3 %collective-permute-done.7.refs_3_ = bf16[96,2048]{1,0:T(8,128)(2,1)S(1)} collective-permute-done((bf16[96,2048]{1,0:T(8,128)(2,1)S(1)}, bf16[96,2048]{1,0:T(8,128)(2,1)S(1)}, u32[]{:S(2)}, u32[]{:S(2)}) %collective-permute-start.7) | collective-permute-done | bytes 393248 | tf_op jit(solution)/shard_map/ppermute | solution.py:229
  26.2 1.2 collective-permute-start.8
  27.4 3.9 %collective-permute-start.9 = (bf16[128,2048]{1,0:T(8,128)(2,1)S(1)}, bf16[128,2048]{1,0:T(8,128)(2,1)S(1)}, u32[]{:S(2)}, u32[]{:S(2)}) collective-permute-start(bf16[128,2048]{1,0:T(8,128)(2,1)S(1)} %get-tuple-element.66), channel_id=1, source_target_pairs={{0,4},{1,5},{2,6},{3,7},{4,0},{5,1},{6,2},{7,3},{8,12},{9,13},{10,... | collective-permute-start | bytes 1572872 | tf_op jit(solution)/shard_map/ppermute | solution.py:232
  31.4 2.9 %collective-permute-start.10 = (bf16[128,2048]{1,0:T(8,128)(2,1)S(1)}, bf16[128,2048]{1,0:T(8,128)(2,1)S(1)}, u32[]{:S(2)}, u32[]{:S(2)}) collective-permute-start(bf16[128,2048]{1,0:T(8,128)(2,1)S(1)} %get-tuple-element.67), channel_id=1, source_target_pairs={{0,6},{1,7},{2,0},{3,1},{4,2},{5,3},{6,4},{7,5},{8,14},{9,15},{10,... | collective-permute-start | bytes 1572872 | tf_op jit(solution)/shard_map/ppermute | solution.py:232
  34.3 1.8 %collective-permute-start.14 = (bf16[64,2048]{1,0:T(8,128)(2,1)S(1)}, bf16[64,2048]{1,0:T(8,128)(2,1)S(1)}, u32[]{:S(2)}, u32[]{:S(2)}) collective-permute-start(bf16[64,2048]{1,0:T(8,128)(2,1)S(1)} %slice.18), channel_id=1, source_target_pairs={{0,1},{1,0},{2,3},{3,2},{4,5},{5,4},{6,7},{7,6},{8,9},{9,8},{10,11... | collective-permute-start | bytes 786440 | tf_op jit(solution)/shard_map/ppermute | solution.py:233
  36.2 4.6 %collective-permute-done.14.refs_7_ = bf16[64,2048]{1,0:T(8,128)(2,1)S(1)} collective-permute-done((bf16[64,2048]{1,0:T(8,128)(2,1)S(1)}, bf16[64,2048]{1,0:T(8,128)(2,1)S(1)}, u32[]{:S(2)}, u32[]{:S(2)}) %collective-permute-start.14) | collective-permute-done | bytes 262176 | tf_op jit(solution)/shard_map/ppermute | solution.py:233
  40.8 1.4 input_grad.1
  42.2 2.0 %collective-permute-done.9.refs_2_ = bf16[128,2048]{1,0:T(8,128)(2,1)S(1)} collective-permute-done((bf16[128,2048]{1,0:T(8,128)(2,1)S(1)}, bf16[128,2048]{1,0:T(8,128)(2,1)S(1)}, u32[]{:S(2)}, u32[]{:S(2)}) %collective-permute-start.9) | collective-permute-done | bytes 524320 | tf_op jit(solution)/shard_map/ppermute | solution.py:232
  44.2 8.7 %collective-permute-done.10.refs_3_ = bf16[128,2048]{1,0:T(8,128)(2,1)S(1)} collective-permute-done((bf16[128,2048]{1,0:T(8,128)(2,1)S(1)}, bf16[128,2048]{1,0:T(8,128)(2,1)S(1)}, u32[]{:S(2)}, u32[]{:S(2)}) %collective-permute-start.10) | collective-permute-done | bytes 524320 | tf_op jit(solution)/shard_map/ppermute | solution.py:232
  52.9 2.5 %weight_grad.1 = (bf16[256,2048]{1,0:T(8,128)(2,1)S(1)}, bf16[256,2048]{1,0:T(8,128)(2,1)S(1)}) custom-call(bf16[128,2048]{1,0:T(8,128)(2,1)S(1)} %get-tuple-element.64.refs_0_, bf16[128,2048]{1,0:T(8,128)(2,1)S(1)} %collective-permute-done.8.refs_1_, bf16[128,2048]{1,0:T(8,128)(2,1)S(1)} %collective-permute-done.9.refs_2_, ...), custom_call_target="tpu_custom_call" | custom-call | flops 1073741824 | bytes 4718592 | tf_op jit(solution)/shard_map/weight_grad/pallas_call | solution.py:45
  55.5 1.3 collective-permute-start.15
  57.4 1.0 collective-permute-start
  58.5 0.3 collective-permute-done
  58.8 0.6 pad_maximum_fusion.counts
  59.4 1.5 weigh.1
  60.9 1.8 %collective-permute-start.2 = (bf16[256,1024]{1,0:T(8,128)(2,1)S(1)}, bf16[256,1024]{1,0:T(8,128)(2,1)S(1)}, u32[]{:S(2)}, u32[]{:S(2)}) collective-permute-start(bf16[256,1024]{1,0:T(8,128)(2,1)S(1)} %get-tuple-element.49), channel_id=1, source_target_pairs={{0,64},{8,72},{16,80},{24,88},{32,96},{40,104},{48,112},{56,120},{... | collective-permute-start | bytes 1572872 | tf_op jit(solution)/shard_map/ppermute | solution.py:238
  62.6 2.7 %collective-permute-start.3 = (bf16[256,1024]{1,0:T(8,128)(2,1)S(1)}, bf16[256,1024]{1,0:T(8,128)(2,1)S(1)}, u32[]{:S(2)}, u32[]{:S(2)}) collective-permute-start(bf16[256,1024]{1,0:T(8,128)(2,1)S(1)} %get-tuple-element.50), channel_id=1, source_target_pairs={{0,128},{8,136},{16,144},{24,152},{32,160},{40,168},{48,176},{56,1... | collective-permute-start | bytes 1572872 | tf_op jit(solution)/shard_map/ppermute | solution.py:238
  65.4 1.4 collective-permute-start.4
  66.8 0.9 collective-permute-start.28
  67.7 8.7 %collective-permute-done.2.refs_1_ = bf16[256,1024]{1,0:T(8,128)(2,1)S(1)} collective-permute-done((bf16[256,1024]{1,0:T(8,128)(2,1)S(1)}, bf16[256,1024]{1,0:T(8,128)(2,1)S(1)}, u32[]{:S(2)}, u32[]{:S(2)}) %collective-permute-start.2) | collective-permute-done | bytes 524320 | tf_op jit(solution)/shard_map/ppermute | solution.py:238
  76.4 2.3 %collective-permute-start.29 = (bf16[128,2048]{1,0:T(8,128)(2,1)S(1)}, bf16[128,2048]{1,0:T(8,128)(2,1)S(1)}, u32[]{:S(2)}, u32[]{:S(2)}) collective-permute-start(bf16[128,2048]{1,0:T(8,128)(2,1)S(1)} %get-tuple-element.88), channel_id=1, source_target_pairs={{0,4},{1,5},{2,6},{3,7},{4,0},{5,1},{6,2},{7,3},{8,12},{9,13},{10,... | collective-permute-start | bytes 1572872 | tf_op jit(solution)/shard_map/ppermute | solution.py:249
  78.7 9.9 %collective-permute-done.3.refs_2_ = bf16[256,1024]{1,0:T(8,128)(2,1)S(1)} collective-permute-done((bf16[256,1024]{1,0:T(8,128)(2,1)S(1)}, bf16[256,1024]{1,0:T(8,128)(2,1)S(1)}, u32[]{:S(2)}, u32[]{:S(2)}) %collective-permute-start.3) | collective-permute-done | bytes 524320 | tf_op jit(solution)/shard_map/ppermute | solution.py:238
  88.6 0.6 collective-permute-start.30
  89.2 0.3 sum_blocks.1
  89.5 5.5 %collective-permute-start.18 = (bf16[256,256]{1,0:T(8,128)(2,1)S(1)}, bf16[256,256]{1,0:T(8,128)(2,1)S(1)}, u32[]{:S(2)}, u32[]{:S(2)}) collective-permute-start(bf16[256,256]{1,0:T(8,128)(2,1)S(1)} %get-tuple-element.73), channel_id=1, source_target_pairs={{0,48},{8,56},{16,0},{24,8},{32,16},{40,24},{48,32},{56,40},{64,11... | collective-permute-start | bytes 393224 | tf_op jit(solution)/shard_map/ppermute | solution.py:271
  95.5 2.1 %collective-permute-start.19 = (f32[1]{0:T(128)}, f32[1]{0:T(128)}, u32[]{:S(2)}, u32[]{:S(2)}) collective-permute-start(f32[1]{0:T(128)} %add.39), channel_id=1, source_target_pairs={{0,64},{8,72},{16,80},{24,88},{32,96},{40,104},{48,112},{56,120},{... | collective-permute-start | bytes 20 | tf_op jit(solution)/shard_map/ppermute | solution.py:239
  97.6 2.8 %collective-permute-done.19 = f32[1]{0:T(128)} collective-permute-done((f32[1]{0:T(128)}, f32[1]{0:T(128)}, u32[]{:S(2)}, u32[]{:S(2)}) %collective-permute-start.19) | collective-permute-done | bytes 36 | tf_op jit(solution)/shard_map/ppermute | solution.py:239
  100.5 2.1 %collective-permute-start.20 = (f32[1]{0:T(128)}, f32[1]{0:T(128)}, u32[]{:S(2)}, u32[]{:S(2)}) collective-permute-start(f32[1]{0:T(128)} %add.39), channel_id=1, source_target_pairs={{0,128},{8,136},{16,144},{24,152},{32,160},{40,168},{48,176},{56,1... | collective-permute-start | bytes 20 | tf_op jit(solution)/shard_map/ppermute | solution.py:239
  102.6 2.9 %collective-permute-done.20 = f32[1]{0:T(128)} collective-permute-done((f32[1]{0:T(128)}, f32[1]{0:T(128)}, u32[]{:S(2)}, u32[]{:S(2)}) %collective-permute-start.20) | collective-permute-done | bytes 36 | tf_op jit(solution)/shard_map/ppermute | solution.py:239
  105.5 1.7 %collective-permute-start.21 = (f32[1]{0:T(128)}, f32[1]{0:T(128)}, u32[]{:S(2)}, u32[]{:S(2)}) collective-permute-start(f32[1]{0:T(128)} %add.39), channel_id=1, source_target_pairs={{0,192},{8,200},{16,208},{24,216},{32,224},{40,232},{48,240},{56,2... | collective-permute-start | bytes 20 | tf_op jit(solution)/shard_map/ppermute | solution.py:239
  108.4 0.7 collective-permute-done.21
  109.7 1.4 collective-permute-start.22
  111.1 4.5 %collective-permute-done.22 = f32[1]{0:T(128)} collective-permute-done((f32[1]{0:T(128)}, f32[1]{0:T(128)}, u32[]{:S(2)}, u32[]{:S(2)}) %collective-permute-start.22) | collective-permute-done | bytes 36 | tf_op jit(solution)/shard_map/ppermute | solution.py:272
  115.5 2.7 %collective-permute-start.23 = (f32[1]{0:T(128)}, f32[1]{0:T(128)}, u32[]{:S(2)}, u32[]{:S(2)}) collective-permute-start(f32[1]{0:T(128)} %add.42), channel_id=1, source_target_pairs={{0,32},{8,40},{16,48},{24,56},{32,0},{40,8},{48,16},{56,24},{64,96... | collective-permute-start | bytes 20 | tf_op jit(solution)/shard_map/ppermute | solution.py:272
  118.2 4.7 %collective-permute-done.23 = f32[1]{0:T(128)} collective-permute-done((f32[1]{0:T(128)}, f32[1]{0:T(128)}, u32[]{:S(2)}, u32[]{:S(2)}) %collective-permute-start.23) | collective-permute-done | bytes 36 | tf_op jit(solution)/shard_map/ppermute | solution.py:272
  122.9 1.5 %collective-permute-start.24 = (f32[1]{0:T(128)}, f32[1]{0:T(128)}, u32[]{:S(2)}, u32[]{:S(2)}) collective-permute-start(f32[1]{0:T(128)} %add.42), channel_id=1, source_target_pairs={{0,48},{8,56},{16,0},{24,8},{32,16},{40,24},{48,32},{56,40},{64,11... | collective-permute-start | bytes 20 | tf_op jit(solution)/shard_map/ppermute | solution.py:272
  124.5 3.0 %collective-permute-done.24 = f32[1]{0:T(128)} collective-permute-done((f32[1]{0:T(128)}, f32[1]{0:T(128)}, u32[]{:S(2)}, u32[]{:S(2)}) %collective-permute-start.24) | collective-permute-done | bytes 36 | tf_op jit(solution)/shard_map/ppermute | solution.py:272
  127.5 1.5 collective-permute-start.17
  129.0 2.4 %collective-permute-start.16 = (bf16[256,256]{1,0:T(8,128)(2,1)S(1)}, bf16[256,256]{1,0:T(8,128)(2,1)S(1)}, u32[]{:S(2)}, u32[]{:S(2)}) collective-permute-start(bf16[256,256]{1,0:T(8,128)(2,1)S(1)} %get-tuple-element.71), channel_id=1, source_target_pairs={{0,16},{8,24},{16,32},{24,40},{32,48},{40,56},{48,0},{56,8},{64,80... | collective-permute-start | bytes 393224 | tf_op jit(solution)/shard_map/ppermute | solution.py:271
  131.3 2.9 %project.1 = (bf16[128,512]{1,0:T(8,128)(2,1)S(1)}, bf16[128,512]{1,0:T(8,128)(2,1)S(1)}, bf16[128,512]{1,0:T(8,128)(2,1)S(1)}, bf16[128,512]{1,0:T(8,128)(2,1)S(1)}) custom-call(bf16[128,2048]{1,0:T(8,128)(2,1)S(1)} %get-tuple-element.64.refs_0_, bf16[128,2048]{1,0:T(8,128)(2,1)S(1)} %collective-permute-done.8.refs_1_, ...), custom_call_target="tpu_custom_call" | custom-call | flops 1073741824 | bytes 4718592 | tf_op jit(solution)/shard_map/project/pallas_call | solution.py:45
  134.3 0.3 join_grads.1
  134.6 3.0 %collective-permute-start.25 = (bf16[96,2048]{1,0:T(8,128)(2,1)S(1)}, bf16[96,2048]{1,0:T(8,128)(2,1)S(1)}, u32[]{:S(2)}, u32[]{:S(2)}) collective-permute-start(bf16[96,2048]{1,0:T(8,128)(2,1)S(1)} %get-tuple-element.82), channel_id=1, source_target_pairs={{0,2},{1,3},{2,4},{3,5},{4,6},{5,7},{6,0},{7,1},{8,10},{9,11},{10,... | collective-permute-start | bytes 1179656 | tf_op jit(solution)/shard_map/ppermute | solution.py:280
  137.6 0.6 collective-permute-start.26
  138.1 2.1 %collective-permute-start.27 = (bf16[96,2048]{1,0:T(8,128)(2,1)S(1)}, bf16[96,2048]{1,0:T(8,128)(2,1)S(1)}, u32[]{:S(2)}, u32[]{:S(2)}) collective-permute-start(bf16[96,2048]{1,0:T(8,128)(2,1)S(1)} %get-tuple-element.84), channel_id=1, source_target_pairs={{0,6},{1,7},{2,0},{3,1},{4,2},{5,3},{6,4},{7,5},{8,14},{9,15},{10,... | collective-permute-start | bytes 1179656 | tf_op jit(solution)/shard_map/ppermute | solution.py:280
  142.0 0.0 copy-start.4
  142.0 0.0 copy-start.5
  142.0 1.4 unpack_input_grad.1
  143.4 0.9 multiply_subtract_fusion
  144.4 2.7 %collective-permute-done.25.refs_1_ = bf16[96,2048]{1,0:T(8,128)(2,1)S(1)} collective-permute-done((bf16[96,2048]{1,0:T(8,128)(2,1)S(1)}, bf16[96,2048]{1,0:T(8,128)(2,1)S(1)}, u32[]{:S(2)}, u32[]{:S(2)}) %collective-permute-start.25) | collective-permute-done | bytes 393248 | tf_op jit(solution)/shard_map/ppermute | solution.py:280
  147.1 3.0 %collective-permute-done.27.refs_3_ = bf16[96,2048]{1,0:T(8,128)(2,1)S(1)} collective-permute-done((bf16[96,2048]{1,0:T(8,128)(2,1)S(1)}, bf16[96,2048]{1,0:T(8,128)(2,1)S(1)}, u32[]{:S(2)}, u32[]{:S(2)}) %collective-permute-start.27) | collective-permute-done | bytes 393248 | tf_op jit(solution)/shard_map/ppermute | solution.py:280
  150.1 1.1 finish.1
  (26 shorter events, 0.1 us)
Async XLA Ops:
  0.6 20.0 %copy-start.1 = (bf16[128,8192]{1,0:T(8,128)(2,1)S(1)}, bf16[128,8192]{1,0:T(8,128)(2,1)}, u32[]{:S(2)}) copy-start(bf16[128,8192]{1,0:T(8,128)(2,1)} %x.1) | copy-start | bytes 6291460
  0.6 58.8 %collective-permute-start.1 = (bf16[256,8192]{1,0:T(8,128)(2,1)}, bf16[256,8192]{1,0:T(8,128)(2,1)S(1)}, u32[]{:S(2)}, u32[]{:S(2)}) collective-permute-start(bf16[256,8192]{1,0:T(8,128)(2,1)} %bitcast.4), channel_id=1, source_target_pairs={{0,8},{8,0},{16,24},{24,16},{32,40},{40,32},{48,56},{56,48},{64,72... | collective-permute-start | bytes 12582920 | tf_op jit(solution)/shard_map/ppermute | solution.py:218
  0.7 1.4 copy-start.2
  2.1 0.9 copy-start.3
  3.5 12.2 %collective-permute-start.5 = (bf16[96,2048]{1,0:T(8,128)(2,1)S(1)}, bf16[96,2048]{1,0:T(8,128)(2,1)S(1)}, u32[]{:S(2)}, u32[]{:S(2)}) collective-permute-start(bf16[96,2048]{1,0:T(8,128)(2,1)S(1)} %get-tuple-element.61), channel_id=1, source_target_pairs={{0,2},{1,3},{2,4},{3,5},{4,6},{5,7},{6,0},{7,1},{8,10},{9,11},{10,... | collective-permute-start | bytes 1179656 | tf_op jit(solution)/shard_map/ppermute | solution.py:229
  5.1 13.5 %collective-permute-start.6 = (bf16[96,2048]{1,0:T(8,128)(2,1)S(1)}, bf16[96,2048]{1,0:T(8,128)(2,1)S(1)}, u32[]{:S(2)}, u32[]{:S(2)}) collective-permute-start(bf16[96,2048]{1,0:T(8,128)(2,1)S(1)} %get-tuple-element.62), channel_id=1, source_target_pairs={{0,4},{1,5},{2,6},{3,7},{4,0},{5,1},{6,2},{7,3},{8,12},{9,13},{10,... | collective-permute-start | bytes 1179656 | tf_op jit(solution)/shard_map/ppermute | solution.py:229
  7.8 18.3 %collective-permute-start.7 = (bf16[96,2048]{1,0:T(8,128)(2,1)S(1)}, bf16[96,2048]{1,0:T(8,128)(2,1)S(1)}, u32[]{:S(2)}, u32[]{:S(2)}) collective-permute-start(bf16[96,2048]{1,0:T(8,128)(2,1)S(1)} %get-tuple-element.63), channel_id=1, source_target_pairs={{0,6},{1,7},{2,0},{3,1},{4,2},{5,3},{6,4},{7,5},{8,14},{9,15},{10,... | collective-permute-start | bytes 1179656 | tf_op jit(solution)/shard_map/ppermute | solution.py:229
  8.5 18.9 %collective-permute-start.11 = (bf16[64,2048]{1,0:T(8,128)(2,1)S(1)}, bf16[64,2048]{1,0:T(8,128)(2,1)S(1)}, u32[]{:S(2)}, u32[]{:S(2)}) collective-permute-start(bf16[64,2048]{1,0:T(8,128)(2,1)S(1)} %slice.12), channel_id=1, source_target_pairs={{0,1},{1,0},{2,3},{3,2},{4,5},{5,4},{6,7},{7,6},{8,9},{9,8},{10,11... | collective-permute-start | bytes 786440 | tf_op jit(solution)/shard_map/ppermute | solution.py:233
  15.7 15.6 %collective-permute-start.12 = (bf16[64,2048]{1,0:T(8,128)(2,1)S(1)}, bf16[64,2048]{1,0:T(8,128)(2,1)S(1)}, u32[]{:S(2)}, u32[]{:S(2)}) collective-permute-start(bf16[64,2048]{1,0:T(8,128)(2,1)S(1)} %slice.16), channel_id=1, source_target_pairs={{0,1},{1,0},{2,3},{3,2},{4,5},{5,4},{6,7},{7,6},{8,9},{9,8},{10,11... | collective-permute-start | bytes 786440 | tf_op jit(solution)/shard_map/ppermute | solution.py:233
  18.7 15.7 %collective-permute-start.13 = (bf16[64,2048]{1,0:T(8,128)(2,1)S(1)}, bf16[64,2048]{1,0:T(8,128)(2,1)S(1)}, u32[]{:S(2)}, u32[]{:S(2)}) collective-permute-start(bf16[64,2048]{1,0:T(8,128)(2,1)S(1)} %slice.17), channel_id=1, source_target_pairs={{0,1},{1,0},{2,3},{3,2},{4,5},{5,4},{6,7},{7,6},{8,9},{9,8},{10,11... | collective-permute-start | bytes 786440 | tf_op jit(solution)/shard_map/ppermute | solution.py:233
  26.2 16.1 %collective-permute-start.8 = (bf16[128,2048]{1,0:T(8,128)(2,1)S(1)}, bf16[128,2048]{1,0:T(8,128)(2,1)S(1)}, u32[]{:S(2)}, u32[]{:S(2)}) collective-permute-start(bf16[128,2048]{1,0:T(8,128)(2,1)S(1)} %get-tuple-element.65), channel_id=1, source_target_pairs={{0,2},{1,3},{2,4},{3,5},{4,6},{5,7},{6,0},{7,1},{8,10},{9,11},{10,... | collective-permute-start | bytes 1572872 | tf_op jit(solution)/shard_map/ppermute | solution.py:232
  27.4 16.8 %collective-permute-start.9 = (bf16[128,2048]{1,0:T(8,128)(2,1)S(1)}, bf16[128,2048]{1,0:T(8,128)(2,1)S(1)}, u32[]{:S(2)}, u32[]{:S(2)}) collective-permute-start(bf16[128,2048]{1,0:T(8,128)(2,1)S(1)} %get-tuple-element.66), channel_id=1, source_target_pairs={{0,4},{1,5},{2,6},{3,7},{4,0},{5,1},{6,2},{7,3},{8,12},{9,13},{10,... | collective-permute-start | bytes 1572872 | tf_op jit(solution)/shard_map/ppermute | solution.py:232
  31.4 21.6 %collective-permute-start.10 = (bf16[128,2048]{1,0:T(8,128)(2,1)S(1)}, bf16[128,2048]{1,0:T(8,128)(2,1)S(1)}, u32[]{:S(2)}, u32[]{:S(2)}) collective-permute-start(bf16[128,2048]{1,0:T(8,128)(2,1)S(1)} %get-tuple-element.67), channel_id=1, source_target_pairs={{0,6},{1,7},{2,0},{3,1},{4,2},{5,3},{6,4},{7,5},{8,14},{9,15},{10,... | collective-permute-start | bytes 1572872 | tf_op jit(solution)/shard_map/ppermute | solution.py:232
  34.3 6.5 %collective-permute-start.14 = (bf16[64,2048]{1,0:T(8,128)(2,1)S(1)}, bf16[64,2048]{1,0:T(8,128)(2,1)S(1)}, u32[]{:S(2)}, u32[]{:S(2)}) collective-permute-start(bf16[64,2048]{1,0:T(8,128)(2,1)S(1)} %slice.18), channel_id=1, source_target_pairs={{0,1},{1,0},{2,3},{3,2},{4,5},{5,4},{6,7},{7,6},{8,9},{9,8},{10,11... | collective-permute-start | bytes 786440 | tf_op jit(solution)/shard_map/ppermute | solution.py:233
  40.8 18.6 %copy-start = (bf16[1,256,8192]{2,1,0:T(8,128)(2,1)S(1)}, bf16[1,256,8192]{2,1,0:T(8,128)(2,1)}, u32[]{:S(2)}) copy-start(bf16[1,256,8192]{2,1,0:T(8,128)(2,1)} %param.7) | copy-start | bytes 12582916
  55.5 34.1 %collective-permute-start.15 = (bf16[256,2048]{1,0:T(8,128)(2,1)S(1)}, bf16[256,2048]{1,0:T(8,128)(2,1)S(1)}, u32[]{:S(2)}, u32[]{:S(2)}) collective-permute-start(bf16[256,2048]{1,0:T(8,128)(2,1)S(1)} %get-tuple-element.69), channel_id=1, source_target_pairs={{0,1},{1,0},{2,3},{3,2},{4,5},{5,4},{6,7},{7,6},{8,9},{9,8},{10,11... | collective-permute-start | bytes 3145736 | tf_op jit(solution)/shard_map/ppermute | solution.py:259
  57.4 1.3 collective-permute-start
  60.9 15.5 %collective-permute-start.2 = (bf16[256,1024]{1,0:T(8,128)(2,1)S(1)}, bf16[256,1024]{1,0:T(8,128)(2,1)S(1)}, u32[]{:S(2)}, u32[]{:S(2)}) collective-permute-start(bf16[256,1024]{1,0:T(8,128)(2,1)S(1)} %get-tuple-element.49), channel_id=1, source_target_pairs={{0,64},{8,72},{16,80},{24,88},{32,96},{40,104},{48,112},{56,120},{... | collective-permute-start | bytes 1572872 | tf_op jit(solution)/shard_map/ppermute | solution.py:238
  62.6 26.0 %collective-permute-start.3 = (bf16[256,1024]{1,0:T(8,128)(2,1)S(1)}, bf16[256,1024]{1,0:T(8,128)(2,1)S(1)}, u32[]{:S(2)}, u32[]{:S(2)}) collective-permute-start(bf16[256,1024]{1,0:T(8,128)(2,1)S(1)} %get-tuple-element.50), channel_id=1, source_target_pairs={{0,128},{8,136},{16,144},{24,152},{32,160},{40,168},{48,176},{56,1... | collective-permute-start | bytes 1572872 | tf_op jit(solution)/shard_map/ppermute | solution.py:238
  65.4 23.9 %collective-permute-start.4 = (bf16[256,1024]{1,0:T(8,128)(2,1)S(1)}, bf16[256,1024]{1,0:T(8,128)(2,1)S(1)}, u32[]{:S(2)}, u32[]{:S(2)}) collective-permute-start(bf16[256,1024]{1,0:T(8,128)(2,1)S(1)} %get-tuple-element.51), channel_id=1, source_target_pairs={{0,192},{8,200},{16,208},{24,216},{32,224},{40,232},{48,240},{56,2... | collective-permute-start | bytes 1572872 | tf_op jit(solution)/shard_map/ppermute | solution.py:238
  66.8 62.2 %collective-permute-start.28 = (bf16[128,2048]{1,0:T(8,128)(2,1)S(1)}, bf16[128,2048]{1,0:T(8,128)(2,1)S(1)}, u32[]{:S(2)}, u32[]{:S(2)}) collective-permute-start(bf16[128,2048]{1,0:T(8,128)(2,1)S(1)} %get-tuple-element.87), channel_id=1, source_target_pairs={{0,6},{1,7},{2,0},{3,1},{4,2},{5,3},{6,4},{7,5},{8,14},{9,15},{10,... | collective-permute-start | bytes 1572872 | tf_op jit(solution)/shard_map/ppermute | solution.py:249
  76.4 58.2 %collective-permute-start.29 = (bf16[128,2048]{1,0:T(8,128)(2,1)S(1)}, bf16[128,2048]{1,0:T(8,128)(2,1)S(1)}, u32[]{:S(2)}, u32[]{:S(2)}) collective-permute-start(bf16[128,2048]{1,0:T(8,128)(2,1)S(1)} %get-tuple-element.88), channel_id=1, source_target_pairs={{0,4},{1,5},{2,6},{3,7},{4,0},{5,1},{6,2},{7,3},{8,12},{9,13},{10,... | collective-permute-start | bytes 1572872 | tf_op jit(solution)/shard_map/ppermute | solution.py:249
  88.6 49.0 %collective-permute-start.30 = (bf16[128,2048]{1,0:T(8,128)(2,1)S(1)}, bf16[128,2048]{1,0:T(8,128)(2,1)S(1)}, u32[]{:S(2)}, u32[]{:S(2)}) collective-permute-start(bf16[128,2048]{1,0:T(8,128)(2,1)S(1)} %get-tuple-element.89), channel_id=1, source_target_pairs={{0,2},{1,3},{2,4},{3,5},{4,6},{5,7},{6,0},{7,1},{8,10},{9,11},{10,... | collective-permute-start | bytes 1572872 | tf_op jit(solution)/shard_map/ppermute | solution.py:249
  89.5 48.6 %collective-permute-start.18 = (bf16[256,256]{1,0:T(8,128)(2,1)S(1)}, bf16[256,256]{1,0:T(8,128)(2,1)S(1)}, u32[]{:S(2)}, u32[]{:S(2)}) collective-permute-start(bf16[256,256]{1,0:T(8,128)(2,1)S(1)} %get-tuple-element.73), channel_id=1, source_target_pairs={{0,48},{8,56},{16,0},{24,8},{32,16},{40,24},{48,32},{56,40},{64,11... | collective-permute-start | bytes 393224 | tf_op jit(solution)/shard_map/ppermute | solution.py:271
  95.5 4.9 %collective-permute-start.19 = (f32[1]{0:T(128)}, f32[1]{0:T(128)}, u32[]{:S(2)}, u32[]{:S(2)}) collective-permute-start(f32[1]{0:T(128)} %add.39), channel_id=1, source_target_pairs={{0,64},{8,72},{16,80},{24,88},{32,96},{40,104},{48,112},{56,120},{... | collective-permute-start | bytes 20 | tf_op jit(solution)/shard_map/ppermute | solution.py:239
  100.5 5.0 %collective-permute-start.20 = (f32[1]{0:T(128)}, f32[1]{0:T(128)}, u32[]{:S(2)}, u32[]{:S(2)}) collective-permute-start(f32[1]{0:T(128)} %add.39), channel_id=1, source_target_pairs={{0,128},{8,136},{16,144},{24,152},{32,160},{40,168},{48,176},{56,1... | collective-permute-start | bytes 20 | tf_op jit(solution)/shard_map/ppermute | solution.py:239
  105.5 3.6 %collective-permute-start.21 = (f32[1]{0:T(128)}, f32[1]{0:T(128)}, u32[]{:S(2)}, u32[]{:S(2)}) collective-permute-start(f32[1]{0:T(128)} %add.39), channel_id=1, source_target_pairs={{0,192},{8,200},{16,208},{24,216},{32,224},{40,232},{48,240},{56,2... | collective-permute-start | bytes 20 | tf_op jit(solution)/shard_map/ppermute | solution.py:239
  109.7 5.8 %collective-permute-start.22 = (f32[1]{0:T(128)}, f32[1]{0:T(128)}, u32[]{:S(2)}, u32[]{:S(2)}) collective-permute-start(f32[1]{0:T(128)} %add.42), channel_id=1, source_target_pairs={{0,16},{8,24},{16,32},{24,40},{32,48},{40,56},{48,0},{56,8},{64,80... | collective-permute-start | bytes 20 | tf_op jit(solution)/shard_map/ppermute | solution.py:272
  115.5 7.4 %collective-permute-start.23 = (f32[1]{0:T(128)}, f32[1]{0:T(128)}, u32[]{:S(2)}, u32[]{:S(2)}) collective-permute-start(f32[1]{0:T(128)} %add.42), channel_id=1, source_target_pairs={{0,32},{8,40},{16,48},{24,56},{32,0},{40,8},{48,16},{56,24},{64,96... | collective-permute-start | bytes 20 | tf_op jit(solution)/shard_map/ppermute | solution.py:272
  122.9 4.5 %collective-permute-start.24 = (f32[1]{0:T(128)}, f32[1]{0:T(128)}, u32[]{:S(2)}, u32[]{:S(2)}) collective-permute-start(f32[1]{0:T(128)} %add.42), channel_id=1, source_target_pairs={{0,48},{8,56},{16,0},{24,8},{32,16},{40,24},{48,32},{56,40},{64,11... | collective-permute-start | bytes 20 | tf_op jit(solution)/shard_map/ppermute | solution.py:272
  127.5 16.0 %collective-permute-start.17 = (bf16[256,256]{1,0:T(8,128)(2,1)S(1)}, bf16[256,256]{1,0:T(8,128)(2,1)S(1)}, u32[]{:S(2)}, u32[]{:S(2)}) collective-permute-start(bf16[256,256]{1,0:T(8,128)(2,1)S(1)} %get-tuple-element.72), channel_id=1, source_target_pairs={{0,32},{8,40},{16,48},{24,56},{32,0},{40,8},{48,16},{56,24},{64,96... | collective-permute-start | bytes 393224 | tf_op jit(solution)/shard_map/ppermute | solution.py:271
  129.0 14.5 %collective-permute-start.16 = (bf16[256,256]{1,0:T(8,128)(2,1)S(1)}, bf16[256,256]{1,0:T(8,128)(2,1)S(1)}, u32[]{:S(2)}, u32[]{:S(2)}) collective-permute-start(bf16[256,256]{1,0:T(8,128)(2,1)S(1)} %get-tuple-element.71), channel_id=1, source_target_pairs={{0,16},{8,24},{16,32},{24,40},{32,48},{40,56},{48,0},{56,8},{64,80... | collective-permute-start | bytes 393224 | tf_op jit(solution)/shard_map/ppermute | solution.py:271
  134.6 12.5 %collective-permute-start.25 = (bf16[96,2048]{1,0:T(8,128)(2,1)S(1)}, bf16[96,2048]{1,0:T(8,128)(2,1)S(1)}, u32[]{:S(2)}, u32[]{:S(2)}) collective-permute-start(bf16[96,2048]{1,0:T(8,128)(2,1)S(1)} %get-tuple-element.82), channel_id=1, source_target_pairs={{0,2},{1,3},{2,4},{3,5},{4,6},{5,7},{6,0},{7,1},{8,10},{9,11},{10,... | collective-permute-start | bytes 1179656 | tf_op jit(solution)/shard_map/ppermute | solution.py:280
  137.6 9.5 %collective-permute-start.26 = (bf16[96,2048]{1,0:T(8,128)(2,1)S(1)}, bf16[96,2048]{1,0:T(8,128)(2,1)S(1)}, u32[]{:S(2)}, u32[]{:S(2)}) collective-permute-start(bf16[96,2048]{1,0:T(8,128)(2,1)S(1)} %get-tuple-element.83), channel_id=1, source_target_pairs={{0,4},{1,5},{2,6},{3,7},{4,0},{5,1},{6,2},{7,3},{8,12},{9,13},{10,... | collective-permute-start | bytes 1179656 | tf_op jit(solution)/shard_map/ppermute | solution.py:280
  138.1 12.0 %collective-permute-start.27 = (bf16[96,2048]{1,0:T(8,128)(2,1)S(1)}, bf16[96,2048]{1,0:T(8,128)(2,1)S(1)}, u32[]{:S(2)}, u32[]{:S(2)}) collective-permute-start(bf16[96,2048]{1,0:T(8,128)(2,1)S(1)} %get-tuple-element.84), channel_id=1, source_target_pairs={{0,6},{1,7},{2,0},{3,1},{4,2},{5,3},{6,4},{7,5},{8,14},{9,15},{10,... | collective-permute-start | bytes 1179656 | tf_op jit(solution)/shard_map/ppermute | solution.py:280
  142.0 1.4 copy-start.4
  142.0 1.4 copy-start.5

commit v2 on v1

v2 whole, which is shorter than its diff:
```python
import functools

import jax
import jax.numpy as jnp
from jax import lax
from jax.experimental import pallas as pl
from jax.experimental.pallas import tpu as pltpu
from jax.sharding import PartitionSpec as P

momentum_decay = 0.9
outer_rate = 0.7

F32, BF16 = jnp.float32, jnp.bfloat16
ANY = pl.BlockSpec(memory_space=pl.ANY)
VMEM = pl.BlockSpec(memory_space=pltpu.VMEM)
SMEM = pl.BlockSpec(memory_space=pltpu.SMEM)
HBM = pl.BlockSpec(memory_space=pltpu.HBM)

SEG = 2048
ROWS = 64
TOK = 128
KVI = 512


def y_shift(k):
    return [(f, (f + 2 * k) % 8) for f in range(8)]


Z_SWAP = [(f, f ^ 1) for f in range(8)]
CORE_SWAP = [(r, r ^ 1) for r in range(32)]


def x_shift(k):
    return [(r, (r + 8 * k) % 32) for r in range(32)]


ZH_NEAR = [(r, r ^ 2) for r in range(32)]
ZH_FAR = [(r, r ^ 6) for r in range(32)]


def call(kernel, name, ins, outs, scratch=(), limit=24):
    arrays = [a for _, a in ins]
    return pl.pallas_call(
        kernel,
        name=name,
        in_specs=[s for s, _ in ins],
        out_specs=[s for s, _ in outs],
        out_shape=[o for _, o in outs],
        scratch_shapes=list(scratch),
        compiler_params=pltpu.CompilerParams(vmem_limit_bytes=limit << 20),
        cost_estimate=pl.CostEstimate(flops=0, bytes_accessed=0, transcendentals=0),
    )(*arrays)


def shape(*dims, dtype=BF16):
    return jax.ShapeDtypeStruct(dims, dtype)


def here():
    f = lax.axis_index("fsdp")
    return f // 2, f % 2


def run_all(copies):
    for c in copies:
        c.start()
    for c in copies:
        c.wait()


def pack_weight(w, *rest):
    outs, sems = rest[:4], rest[4]
    y, _ = here()
    copies = []
    for k in (1, 3, 2, 0):
        start = pl.multiple_of((y + k) % 4 * SEG, SEG)
        copies.append(pltpu.make_async_copy(w.at[:, pl.ds(start, SEG)], outs[k], sems.at[k]))
    run_all(copies)


def pack_inputs(x, cot, *rest):
    outs, sems = rest[:4], rest[4]
    y, _ = here()
    copies = []
    for k in range(4):
        start = pl.multiple_of((y + k) % 4 * SEG, SEG)
        copies.append((x.at[:, pl.ds(start, SEG)], outs[k].at[pl.ds(0, TOK)]))
        for j in range(4):
            copies.append((cot.at[pl.ds(32 * j, 32)], outs[k].at[pl.ds(TOK, 32), pl.ds(KVI * j, KVI)]))
    run_all([pltpu.make_async_copy(s, d, sems.at[i]) for i, (s, d) in enumerate(copies)])


def unpack_columns(*refs):
    parts, out, sems = refs[:4], refs[4], refs[5]
    y, _ = here()
    copies = []
    for k in range(4):
        start = pl.multiple_of((y + k) % 4 * SEG, SEG)
        copies.append(pltpu.make_async_copy(parts[k], out.at[:, pl.ds(start, SEG)], sems.at[k]))
    run_all(copies)


def stack(*refs):
    for k in range(4):
        refs[4][ROWS * k : ROWS * k + ROWS, :] = refs[k][...]


def grad_to_inputs(*refs):
    got, other, xs, outs, w, cots = refs[:4], refs[4], refs[5:9], refs[9:13], refs[13], refs[14]
    y, z = here()
    for k in range(4):
        owner = (y + 4 - k) % 4
        w[pl.ds(pl.multiple_of((owner * 2 + z) * ROWS, ROWS), ROWS), :] = got[k][...]
        w[pl.ds(pl.multiple_of((owner * 2 + 1 - z) * ROWS, ROWS), ROWS), :] = other[ROWS * k : ROWS * k + ROWS, :]
        for j in range(4):
            cots[TOK * k + 32 * j : TOK * k + 32 * j + 32, :] = xs[k][TOK : TOK + 32, KVI * j : KVI * j + KVI]
    for c in range(0, SEG, 512):
        part = jnp.dot(cots[...], w[:, c : c + 512], preferred_element_type=F32).astype(BF16)
        for k in range(4):
            outs[k][:, c : c + 512] = part[TOK * k : TOK * k + TOK]


def weight_grad(scale, *refs):
    xs, cots, mine, other, whole = refs[:4], refs[4], refs[5], refs[6], refs[7]
    y, z = here()
    for c in range(0, SEG, 256):
        total = None
        for k in range(4):
            term = lax.dot_general(
                cots[TOK * k : TOK * k + TOK, :],
                xs[k][0:TOK, c : c + 256],
                (((0,), (0,)), ((), ())),
                preferred_element_type=F32,
            )
            total = term if total is None else total + term
        whole[:, c : c + 256] = (total * scale).astype(BF16)
    for j in range(4):
        to = (y + j) % 4 * 2
        rows = slice(ROWS * j, ROWS * j + ROWS)
        mine[rows, :] = whole[pl.ds(pl.multiple_of((to + z) * ROWS, ROWS), ROWS), :]
        other[rows, :] = whole[pl.ds(pl.multiple_of((to + 1 - z) * ROWS, ROWS), ROWS), :]


def project(*refs):
    xs, w, outs = refs[:4], refs[4], refs[5:9]
    for k in range(4):
        outs[k][...] = lax.dot_general(
            xs[k][0:TOK, :], w[...], (((1,), (1,)), ((), ())), preferred_element_type=F32
        ).astype(BF16)


def sum_keys(*refs):
    total = refs[0][...].astype(F32)
    for r in refs[1:4]:
        total = total + r[...].astype(F32)
    refs[4][...] = total.astype(BF16)


def join_grads(mine, recv, *outs):
    for j in range(4):
        rows = slice(ROWS * j, ROWS * j + ROWS)
        outs[j][...] = (mine[rows, :].astype(F32) + recv[rows, :].astype(F32)).astype(BF16)


def finish(*refs):
    got, grads = refs[:4], refs[4]
    y, _ = here()
    for j in range(4):
        owner = (y + 4 - j) % 4
        grads[:, pl.ds(pl.multiple_of(owner * SEG, SEG), SEG)] = got[j][...]


def put_count(ref, row, value):
    half = ref.shape[1] // 2
    high = jnp.floor(value * (1.0 / 256.0))
    for i in range(0, half, 128):
        ref[row : row + 16, i : i + 128] = jnp.broadcast_to(high, (16, 128)).astype(BF16)
        ref[row : row + 16, half + i : half + i + 128] = jnp.broadcast_to(value - 256.0 * high, (16, 128)).astype(BF16)


def take_count(refs, row):
    half = refs[0].shape[1] // 2
    total = None
    for r in refs:
        high, low = r[row : row + 16, 0:128].astype(F32), r[row : row + 16, half : half + 128].astype(F32)
        term = high * 256.0 + low
        total = term if total is None else total + term
    return total[0:1, :]


def weigh(counts, counts_other, mine, other, *outs):
    r = lax.axis_index("replica")
    x, core = r // 8, r % 2
    own, theirs = counts[0], counts_other[0]
    for k in range(4):
        for h in range(4):
            start = pl.multiple_of((x + k) % 4 * 2048 + h * 512 + core * 256, 256)
            cols = pl.ds(start, 256)
            total = own * mine[:, cols].astype(F32) + theirs * other[:, cols].astype(F32)
            outs[k][0:256, 256 * h : 256 * h + 256] = total.astype(BF16)
        put_count(outs[k], 256, jnp.full((1, 128), own + theirs, F32))


def sum_blocks(*refs):
    parts, keep, send = refs[:4], refs[4], refs[5]
    zh = lax.axis_index("replica") // 2 % 4
    near = zh + 1 - 2 * (zh % 2)
    count = take_count(parts, 256)
    for out, first in ((keep, zh), (send, near)):
        for i, block in enumerate((first, 3 - first)):
            cols = pl.ds(pl.multiple_of(block * 256, 256), 256)
            total = parts[0][0:256, cols].astype(F32)
            for p in parts[1:]:
                total = total + p[0:256, cols].astype(F32)
            out[0:256, 256 * i : 256 * i + 256] = total.astype(BF16)
        put_count(out, 256, count)


def halve_blocks(kept, recv, keep, send):
    count = take_count((kept, recv), 256)
    for i, out in enumerate((keep, send)):
        cols = slice(256 * i, 256 * i + 256)
        out[0:256, :] = (kept[0:256, cols].astype(F32) + recv[0:256, cols].astype(F32)).astype(BF16)
        put_count(out, 256, count)


def outer_step(*refs):
    parts, master, momentum, new_master, new_momentum = refs[:2], *refs[2:6]
    count = take_count(parts, 256)
    for c in (0, 128):
        cols = slice(c, c + 128)
        total = parts[0][0:256, cols].astype(F32) + parts[1][0:256, cols].astype(F32)
        pseudo_grad = master[:, cols] - total / count
        moved = momentum_decay * momentum[:, cols] + pseudo_grad
        new_momentum[:, cols] = moved
        new_master[:, cols] = master[:, cols] - outer_rate * (pseudo_grad + momentum_decay * moved)


def together(*groups):
    flat = lax.optimization_barrier(tuple(v for g in groups for v in g))
    out, i = [], 0
    for g in groups:
        out.append(list(flat[i : i + len(g)]))
        i += len(g)
    return out


def local(local_frag, master, momentum, counts, inputs, inner_weight, cotangent):
    dma = pltpu.SemaphoreType.DMA
    fsdp = lambda a, perm: lax.ppermute(a, "fsdp", perm)
    replica = lambda a, perm: lax.ppermute(a, "replica", perm)

    frag = local_frag[0]
    count = counts.astype(F32)
    frag_other, count_other = replica(frag, CORE_SWAP), replica(count, CORE_SWAP)

    sent = call(pack_weight, "pack_weight", [(HBM, inner_weight[0])], [(ANY, shape(ROWS, SEG))] * 4, [dma((4,))])
    got = {k: fsdp(sent[k], y_shift(k)) for k in (1, 3, 2)}
    got = [sent[0], got[1], got[2], got[3]]

    parts = call(
        weigh,
        "weigh",
        [(SMEM, count), (SMEM, count_other), (VMEM, frag), (VMEM, frag_other)],
        [(VMEM, shape(272, 1024))] * 4,
    )
    x1, x3 = replica(parts[1], x_shift(1)), replica(parts[3], x_shift(3))

    packed = call(
        pack_inputs,
        "pack_inputs",
        [(HBM, inputs), (HBM, cotangent)],
        [(ANY, shape(TOK + 32, SEG))] * 4,
        [dma((20,))],
    )
    packed, got = together(packed, got)
    (stacked,) = call(stack, "stack_weight", [(VMEM, a) for a in got], [(VMEM, shape(4 * ROWS, SEG))])
    crossed = fsdp(stacked, Z_SWAP)
    xs = [packed[0]] + [fsdp(packed[k], y_shift(k)) for k in (1, 2, 3)]
    got, (x1, x3, t2) = together(got, (x1, x3, parts[2]))
    parts = [parts[0], x1, replica(t2, x_shift(2)), x3]

    *back, w_full, cots = call(
        grad_to_inputs,
        "input_grad",
        [(VMEM, a) for a in (*got, crossed, *xs)],
        [(VMEM, shape(TOK, SEG))] * 4 + [(VMEM, shape(KVI, SEG)), (VMEM, shape(4 * TOK, KVI))],
    )
    back = [back[0]] + [fsdp(back[k], y_shift(-k)) for k in (1, 2, 3)]

    mine, other = call(
        functools.partial(weight_grad, 1.0 / (TOK * lax.axis_size("fsdp"))),
        "weight_grad",
        [(VMEM, a) for a in (*xs, cots)],
        [(VMEM, shape(4 * ROWS, SEG))] * 2,
        [pltpu.VMEM((KVI, SEG), BF16)],
    )
    recv = fsdp(other, Z_SWAP)
    (other,), parts = together((other,), parts)
    kept, send = call(sum_blocks, "sum_blocks", [(VMEM, a) for a in parts], [(VMEM, shape(272, 512))] * 2)
    near = replica(send, ZH_NEAR)
    keys = call(project, "project", [(VMEM, a) for a in (*xs, w_full)], [(VMEM, shape(TOK, KVI))] * 4)
    kept, send = call(
        halve_blocks, "halve_blocks", [(VMEM, kept), (VMEM, near)], [(VMEM, shape(272, 256))] * 2
    )
    far = replica(send, ZH_FAR)
    back, keys = together(back, keys)
    keys = [keys[0]] + [fsdp(keys[k], y_shift(-k)) for k in (1, 2, 3)]
    (back_full,) = call(
        unpack_columns, "unpack_input_grad", [(ANY, a) for a in back], [(ANY, shape(TOK, 8192))], [dma((4,))]
    )

    joined = call(
        join_grads,
        "join_grads",
        [(VMEM, mine), (VMEM, recv)],
        [(VMEM, shape(ROWS, SEG))] * 4,
    )
    joined = [joined[0]] + [fsdp(joined[j], y_shift(j)) for j in (1, 2, 3)]
    (projected,) = call(sum_keys, "sum_keys", [(VMEM, a) for a in keys], [(VMEM, shape(TOK, KVI))])
    new_master, new_momentum = call(
        outer_step,
        "outer_step",
        [(VMEM, a) for a in (kept, far, master, momentum)],
        [(VMEM, shape(256, 256, dtype=F32))] * 2,
    )
    (grads,) = call(finish, "finish", [(VMEM, a) for a in joined], [(VMEM, shape(ROWS, 8192))])
    return new_master, new_momentum, projected, back_full, grads[None]


def solution(mesh):
    placed = (
        P("replica", "fsdp", None),
        P("fsdp", "replica"),
        P("fsdp", "replica"),
        P("replica"),
        P(("replica", "fsdp"), None),
        P("replica", "fsdp", None),
        P(("replica", "fsdp"), None),
    )
    return jax.shard_map(
        local,
        mesh=mesh,
        in_specs=placed,
        out_specs=(
            P("fsdp", "replica"),
            P("fsdp", "replica"),
            P(("replica", "fsdp"), None),
            P(("replica", "fsdp"), None),
            P("replica", "fsdp", None),
        ),
        check_vma=False,
    )
```

time: 151 us -> 114 us (0.75)
  the two profiles are of different devices: /device:TPU:8 before, /device:TPU:1 now
where the time goes in v2:
time: 114 us
  waiting for transfers between devices  57.1 us (50%)
  starting transfers between devices  37.9 us (33%)
  Pallas kernels  13.6 us (12%)
  local copies, waits for them, and re-layouts  3.43 us (3%)
  between operations  1.44 us (1%)
    ppermute x17, waiting for transfers between devices, local(): fsdp = lambda a, perm: lax.ppermute(a, 'fsdp', perm)  32.9 us
    ppermute x7, waiting for transfers between devices, local(): replica = lambda a, perm: lax.ppermute(a, 'replica', perm)  24.2 us
    ppermute x17, starting transfers between devices, local(): fsdp = lambda a, perm: lax.ppermute(a, 'fsdp', perm)  20.4 us
    ppermute x7, starting transfers between devices, local(): replica = lambda a, perm: lax.ppermute(a, 'replica', perm)  17.5 us
    pallas_call x14, Pallas kernels, call(): pl.pallas_call(kernel, name=name, in_specs=[s for s, _ in ins], out_specs...  13.6 us
    unnamed x12, local copies, waits for them, and re-layouts  3.43 us
  transfers between devices with their start and end apart: 24, of which 8 were waited for; matrix products, arithmetic and copies ran while one was open for 0% of the time, Pallas kernels for 8%

profile of v2, /device:TPU:1, one launch (start us, length us, event | category | flops | bytes accessed | tf_op | source)
XLA Modules:
  0.0 113.6 jit_solution(6446252500130651598)
XLA Ops:
  0.6 3.3 %collective-permute-start.7 = (bf16[256,8192]{1,0:T(8,128)(2,1)}, bf16[256,8192]{1,0:T(8,128)(2,1)S(1)}, u32[]{:S(2)}, u32[]{:S(2)}) collective-permute-start(bf16[256,8192]{1,0:T(8,128)(2,1)} %bitcast.3), channel_id=1, source_target_pairs={{0,8},{8,0},{16,24},{24,16},{32,40},{40,32},{48,56},{56,48},{64,72... | collective-permute-start | bytes 12582920 | tf_op jit(solution)/shard_map/ppermute | solution.py:251
  4.0 1.2 %copy-done.2 = bf16[1,64,8192]{2,1,0:T(8,128)(2,1)S(1)} copy-done((bf16[1,64,8192]{2,1,0:T(8,128)(2,1)S(1)}, bf16[1,64,8192]{2,1,0:T(8,128)(2,1)}, u32[]{:S(2)}) %copy-start.2) | copy-done | bytes 1048600
  5.2 0.1 pack_weight.1
  5.3 0.1 collective-permute-start
  5.4 2.2 %collective-permute-start.1 = (bf16[64,2048]{1,0:T(8,128)(2,1)S(1)}, bf16[64,2048]{1,0:T(8,128)(2,1)S(1)}, u32[]{:S(2)}, u32[]{:S(2)}) collective-permute-start(bf16[64,2048]{1,0:T(8,128)(2,1)S(1)} %get-tuple-element.72), channel_id=1, source_target_pairs={{0,4},{1,5},{2,6},{3,7},{4,0},{5,1},{6,2},{7,3},{8,12},{9,13},{10,... | collective-permute-start | bytes 786440 | tf_op jit(solution)/shard_map/ppermute | solution.py:250
  7.6 1.1 collective-permute-start.2
  9.3 1.9 %collective-permute-start.6 = (f32[1]{0:T(128)}, f32[1]{0:T(128)}, u32[]{:S(2)}, u32[]{:S(2)}) collective-permute-start(f32[1]{0:T(128)} %convert_element_type.3.counts), channel_id=1, source_target_pairs={{0,8},{8,0},{16,24},{24,16},{32,40},{40,32},{48,56},{56,48},{64,72... | collective-permute-start | bytes 20 | tf_op jit(solution)/shard_map/ppermute | solution.py:251
  11.2 0.0 collective-permute-done.7.other
  11.2 2.2 %copy-done = bf16[1,256,8192]{2,1,0:T(8,128)(2,1)S(1)} copy-done((bf16[1,256,8192]{2,1,0:T(8,128)(2,1)S(1)}, bf16[1,256,8192]{2,1,0:T(8,128)(2,1)}, u32[]{:S(2)}) %copy-start) | copy-done | bytes 4194328
  13.4 1.5 %weigh.1 = (bf16[272,1024]{1,0:T(8,128)(2,1)S(1)}, bf16[272,1024]{1,0:T(8,128)(2,1)S(1)}, bf16[272,1024]{1,0:T(8,128)(2,1)S(1)}, bf16[272,1024]{1,0:T(8,128)(2,1)S(1)}) custom-call(f32[1]{0:T(128)} %convert_element_type.3.counts, f32[1]{0:T(128)} %collective-permute-done.6.counts_other, bf16[256,8192]{1,0:T(8,128)(2,1)S(1)} %bitcast.4, ...), custom_call_target="tpu_custom_call" | custom-call | tf_op jit(solution)/shard_map/weigh/pallas_call | solution.py:43
  14.9 1.3 %collective-permute-start.8 = (bf16[272,1024]{1,0:T(8,128)(2,1)S(1)}, bf16[272,1024]{1,0:T(8,128)(2,1)S(1)}, u32[]{:S(2)}, u32[]{:S(2)}) collective-permute-start(bf16[272,1024]{1,0:T(8,128)(2,1)S(1)} %get-tuple-element.82), channel_id=1, source_target_pairs={{0,64},{8,72},{16,80},{24,88},{32,96},{40,104},{48,112},{56,120},{... | collective-permute-start | bytes 1671176 | tf_op jit(solution)/shard_map/ppermute | solution.py:251
  16.2 0.5 pack_inputs.1
  16.8 0.0 collective-permute-done.refs_1_
  16.8 2.9 %collective-permute-done.1.refs_2_ = bf16[64,2048]{1,0:T(8,128)(2,1)S(1)} collective-permute-done((bf16[64,2048]{1,0:T(8,128)(2,1)S(1)}, bf16[64,2048]{1,0:T(8,128)(2,1)S(1)}, u32[]{:S(2)}, u32[]{:S(2)}) %collective-permute-start.1) | collective-permute-done | bytes 262176 | tf_op jit(solution)/shard_map/ppermute | solution.py:250
  19.7 0.8 collective-permute-done.2.refs_3_
  20.4 0.1 stack_weight.1
  20.5 0.9 collective-permute-start.10
  21.4 0.6 collective-permute-start.3
  22.0 2.8 %collective-permute-start.4 = (bf16[160,2048]{1,0:T(8,128)(2,1)S(1)}, bf16[160,2048]{1,0:T(8,128)(2,1)S(1)}, u32[]{:S(2)}, u32[]{:S(2)}) collective-permute-start(bf16[160,2048]{1,0:T(8,128)(2,1)S(1)} %get-tuple-element.76), channel_id=1, source_target_pairs={{0,4},{1,5},{2,6},{3,7},{4,0},{5,1},{6,2},{7,3},{8,12},{9,13},{10,... | collective-permute-start | bytes 1966088 | tf_op jit(solution)/shard_map/ppermute | solution.py:250
  24.8 0.6 collective-permute-start.5
  25.5 4.6 %collective-permute-done.8.refs_1_ = bf16[272,1024]{1,0:T(8,128)(2,1)S(1)} collective-permute-done((bf16[272,1024]{1,0:T(8,128)(2,1)S(1)}, bf16[272,1024]{1,0:T(8,128)(2,1)S(1)}, u32[]{:S(2)}, u32[]{:S(2)}) %collective-permute-start.8) | collective-permute-done | bytes 557088 | tf_op jit(solution)/shard_map/ppermute | solution.py:251
  30.1 1.3 %collective-permute-start.9 = (bf16[272,1024]{1,0:T(8,128)(2,1)S(1)}, bf16[272,1024]{1,0:T(8,128)(2,1)S(1)}, u32[]{:S(2)}, u32[]{:S(2)}) collective-permute-start(bf16[272,1024]{1,0:T(8,128)(2,1)S(1)} %get-tuple-element.83), channel_id=1, source_target_pairs={{0,192},{8,200},{16,208},{24,216},{32,224},{40,232},{48,240},{56,2... | collective-permute-start | bytes 1671176 | tf_op jit(solution)/shard_map/ppermute | solution.py:251
  31.4 11.7 %collective-permute-done.9.refs_3_ = bf16[272,1024]{1,0:T(8,128)(2,1)S(1)} collective-permute-done((bf16[272,1024]{1,0:T(8,128)(2,1)S(1)}, bf16[272,1024]{1,0:T(8,128)(2,1)S(1)}, u32[]{:S(2)}, u32[]{:S(2)}) %collective-permute-start.9) | collective-permute-done | bytes 557088 | tf_op jit(solution)/shard_map/ppermute | solution.py:251
  43.1 0.0 collective-permute-done.3.refs_6_.refs_1_
  43.1 9.8 %collective-permute-done.4.refs_7_.refs_2_ = bf16[160,2048]{1,0:T(8,128)(2,1)S(1)} collective-permute-done((bf16[160,2048]{1,0:T(8,128)(2,1)S(1)}, bf16[160,2048]{1,0:T(8,128)(2,1)S(1)}, u32[]{:S(2)}, u32[]{:S(2)}) %collective-permute-start.4) | collective-permute-done | bytes 655392 | tf_op jit(solution)/shard_map/ppermute | solution.py:250
  52.9 0.0 collective-permute-done.5.refs_8_.refs_3_
  52.9 0.0 collective-permute-done.10.refs_4_
  52.9 1.4 %input_grad.1 = (bf16[128,2048]{1,0:T(8,128)(2,1)S(1)}, bf16[128,2048]{1,0:T(8,128)(2,1)S(1)}, bf16[128,2048]{1,0:T(8,128)(2,1)S(1)}, bf16[128,2048]{1,0:T(8,128...) custom-call(bf16[64,2048]{1,0:T(8,128)(2,1)S(1)} %get-tuple-element.85.refs_0_, ...), custom_call_target="tpu_custom_call" | custom-call | tf_op jit(solution)/shard_map/input_grad/pallas_call | solution.py:43
  54.4 2.5 %weight_grad.1 = (bf16[256,2048]{1,0:T(8,128)(2,1)S(1)}, bf16[256,2048]{1,0:T(8,128)(2,1)S(1)}) custom-call(bf16[160,2048]{1,0:T(8,128)(2,1)S(1)} %get-tuple-element.74.refs_5_.refs_0_, bf16[160,2048]{1,0:T(8,128)(2,1)S(1)} %collective-permute-done.3.refs_6_.refs_1_, bf16[160,2048]{1,0:T(8,128)(2,1)S(1)} %collective-permute-done.4.refs_7_.refs_2_, ...), custom_call_target="tpu_custom_call" | custom-call | tf_op jit(solution)/shard_map/weight_grad/pallas_call | solution.py:43
  56.9 1.4 %collective-permute-start.20 = (bf16[256,2048]{1,0:T(8,128)(2,1)S(1)}, bf16[256,2048]{1,0:T(8,128)(2,1)S(1)}, u32[]{:S(2)}, u32[]{:S(2)}) collective-permute-start(bf16[256,2048]{1,0:T(8,128)(2,1)S(1)} %get-tuple-element.90), channel_id=1, source_target_pairs={{0,1},{1,0},{2,3},{3,2},{4,5},{5,4},{6,7},{7,6},{8,9},{9,8},{10,11... | collective-permute-start | bytes 3145736 | tf_op jit(solution)/shard_map/ppermute | solution.py:250
  58.3 1.7 %collective-permute-start.11 = (bf16[272,1024]{1,0:T(8,128)(2,1)S(1)}, bf16[272,1024]{1,0:T(8,128)(2,1)S(1)}, u32[]{:S(2)}, u32[]{:S(2)}) collective-permute-start(bf16[272,1024]{1,0:T(8,128)(2,1)S(1)} %get-tuple-element.93), channel_id=1, source_target_pairs={{0,128},{8,136},{16,144},{24,152},{32,160},{40,168},{48,176},{56,1... | collective-permute-start | bytes 1671176 | tf_op jit(solution)/shard_map/ppermute | solution.py:251
  60.0 3.3 %collective-permute-start.14 = (bf16[128,2048]{1,0:T(8,128)(2,1)S(1)}, bf16[128,2048]{1,0:T(8,128)(2,1)S(1)}, u32[]{:S(2)}, u32[]{:S(2)}) collective-permute-start(bf16[128,2048]{1,0:T(8,128)(2,1)S(1)} %get-tuple-element.106), channel_id=1, source_target_pairs={{0,6},{1,7},{2,0},{3,1},{4,2},{5,3},{6,4},{7,5},{8,14},{9,15},{10,... | collective-permute-start | bytes 1572872 | tf_op jit(solution)/shard_map/ppermute | solution.py:250
  63.4 0.8 collective-permute-start.15
  64.1 0.0 collective-permute-start.16
  64.1 7.8 %collective-permute-done.11.refs_2_ = bf16[272,1024]{1,0:T(8,128)(2,1)S(1)} collective-permute-done((bf16[272,1024]{1,0:T(8,128)(2,1)S(1)}, bf16[272,1024]{1,0:T(8,128)(2,1)S(1)}, u32[]{:S(2)}, u32[]{:S(2)}) %collective-permute-start.11) | collective-permute-done | bytes 557088 | tf_op jit(solution)/shard_map/ppermute | solution.py:251
  72.0 0.3 sum_blocks.1
  72.3 2.4 %collective-permute-start.12 = (bf16[272,512]{1,0:T(8,128)(2,1)S(1)}, bf16[272,512]{1,0:T(8,128)(2,1)S(1)}, u32[]{:S(2)}, u32[]{:S(2)}) collective-permute-start(bf16[272,512]{1,0:T(8,128)(2,1)S(1)} %get-tuple-element.100), channel_id=1, source_target_pairs={{0,16},{8,24},{16,0},{24,8},{32,48},{40,56},{48,32},{56,40},{64,80... | collective-permute-start | bytes 835592 | tf_op jit(solution)/shard_map/ppermute | solution.py:251
  74.6 2.9 %project.1 = (bf16[128,512]{1,0:T(8,128)(2,1)S(1)}, bf16[128,512]{1,0:T(8,128)(2,1)S(1)}, bf16[128,512]{1,0:T(8,128)(2,1)S(1)}, bf16[128,512]{1,0:T(8,128)(2,1)S(1)}) custom-call(bf16[160,2048]{1,0:T(8,128)(2,1)S(1)} %get-tuple-element.74.refs_5_.refs_0_, bf16[160,2048]{1,0:T(8,128)(2,1)S(1)} %collective-permute-done.3.refs_6_.refs_1_, ...), custom_call_target="tpu_custom_call" | custom-call | tf_op jit(solution)/shard_map/project/pallas_call | solution.py:43
  77.5 0.0 collective-permute-done.14.refs_1_
  77.5 0.0 collective-permute-done.15.refs_2_
  77.5 12.4 %collective-permute-done.16.refs_3_ = bf16[128,2048]{1,0:T(8,128)(2,1)S(1)} collective-permute-done((bf16[128,2048]{1,0:T(8,128)(2,1)S(1)}, bf16[128,2048]{1,0:T(8,128)(2,1)S(1)}, u32[]{:S(2)}, u32[]{:S(2)}) %collective-permute-start.16) | collective-permute-done | bytes 524320 | tf_op jit(solution)/shard_map/ppermute | solution.py:250
  90.0 0.0 collective-permute-start.17
  90.0 0.8 collective-permute-start.18
  90.7 0.0 collective-permute-done.20.recv
  90.7 0.2 join_grads.1
  91.0 0.9 collective-permute-start.21
  91.9 3.4 %collective-permute-start.22 = (bf16[64,2048]{1,0:T(8,128)(2,1)S(1)}, bf16[64,2048]{1,0:T(8,128)(2,1)S(1)}, u32[]{:S(2)}, u32[]{:S(2)}) collective-permute-start(bf16[64,2048]{1,0:T(8,128)(2,1)S(1)} %get-tuple-element.125), channel_id=1, source_target_pairs={{0,4},{1,5},{2,6},{3,7},{4,0},{5,1},{6,2},{7,3},{8,12},{9,13},{10,... | collective-permute-start | bytes 786440 | tf_op jit(solution)/shard_map/ppermute | solution.py:250
  95.3 0.0 collective-permute-done.12.recv
  95.3 0.0 collective-permute-start.23
  95.3 0.1 halve_blocks.1
  95.4 0.0 collective-permute-done.17.refs_1_
  95.4 0.0 copy-start.3
  95.4 0.0 copy-start.4
  95.4 5.7 %collective-permute-start.13 = (bf16[272,256]{1,0:T(8,128)(2,1)S(1)}, bf16[272,256]{1,0:T(8,128)(2,1)S(1)}, u32[]{:S(2)}, u32[]{:S(2)}) collective-permute-start(bf16[272,256]{1,0:T(8,128)(2,1)S(1)} %get-tuple-element.102), channel_id=1, source_target_pairs={{0,48},{8,56},{16,32},{24,40},{32,16},{40,24},{48,0},{56,8},{64,11... | collective-permute-start | bytes 417800 | tf_op jit(solution)/shard_map/ppermute | solution.py:251
  101.1 0.0 collective-permute-done.18.refs_2_
  101.1 1.5 %collective-permute-start.19 = (bf16[128,512]{1,0:T(8,128)(2,1)S(1)}, bf16[128,512]{1,0:T(8,128)(2,1)S(1)}, u32[]{:S(2)}, u32[]{:S(2)}) collective-permute-start(bf16[128,512]{1,0:T(8,128)(2,1)S(1)} %get-tuple-element.117), channel_id=1, source_target_pairs={{0,2},{1,3},{2,4},{3,5},{4,6},{5,7},{6,0},{7,1},{8,10},{9,11},{10,... | collective-permute-start | bytes 393224 | tf_op jit(solution)/shard_map/ppermute | solution.py:250
  102.6 1.3 %unpack_input_grad.1 = bf16[128,8192]{1,0:T(8,128)(2,1)} custom-call(bf16[128,2048]{1,0:T(8,128)(2,1)S(1)} %get-tuple-element.118.refs_0_, bf16[128,2048]{1,0:T(8,128)(2,1)S(1)} %collective-permute-done.14.refs_1_, bf16[128,2048]{1,0:T(8,128)(2,1)S(1)} %collective-permute-done.15.refs_2_, bf16[128,2048]{1,0:T(8,128)(2,1)S(1)} %collective-permute-done.16.refs_3_), custom_call_target="tpu_custom_call" | custom-call | tf_op jit(solution)/shard_map/unpack_input_grad/pallas_call | solution.py:43
  103.9 6.9 %collective-permute-done.19.refs_3_ = bf16[128,512]{1,0:T(8,128)(2,1)S(1)} collective-permute-done((bf16[128,512]{1,0:T(8,128)(2,1)S(1)}, bf16[128,512]{1,0:T(8,128)(2,1)S(1)}, u32[]{:S(2)}, u32[]{:S(2)}) %collective-permute-start.19) | collective-permute-done | bytes 131104 | tf_op jit(solution)/shard_map/ppermute | solution.py:250
  110.9 0.7 sum_keys.1
  111.6 0.0 collective-permute-done.13.refs_1_
  111.6 0.9 outer_step.1
  112.5 0.0 collective-permute-done.21.refs_1_
  112.5 0.0 collective-permute-done.22.refs_2_
  112.5 1.1 finish.1
  (10 shorter events, 0.0 us)
Async XLA Ops:
  0.6 10.6 %collective-permute-start.7 = (bf16[256,8192]{1,0:T(8,128)(2,1)}, bf16[256,8192]{1,0:T(8,128)(2,1)S(1)}, u32[]{:S(2)}, u32[]{:S(2)}) collective-permute-start(bf16[256,8192]{1,0:T(8,128)(2,1)} %bitcast.3), channel_id=1, source_target_pairs={{0,8},{8,0},{16,24},{24,16},{32,40},{40,32},{48,56},{56,48},{64,72... | collective-permute-start | bytes 12582920 | tf_op jit(solution)/shard_map/ppermute | solution.py:251
  4.0 1.2 %copy-start.2 = (bf16[1,64,8192]{2,1,0:T(8,128)(2,1)S(1)}, bf16[1,64,8192]{2,1,0:T(8,128)(2,1)}, u32[]{:S(2)}) copy-start(bf16[1,64,8192]{2,1,0:T(8,128)(2,1)} %param.12) | copy-start | bytes 3145732
  5.3 11.4 %collective-permute-start = (bf16[64,2048]{1,0:T(8,128)(2,1)S(1)}, bf16[64,2048]{1,0:T(8,128)(2,1)S(1)}, u32[]{:S(2)}, u32[]{:S(2)}) collective-permute-start(bf16[64,2048]{1,0:T(8,128)(2,1)S(1)} %get-tuple-element.71), channel_id=1, source_target_pairs={{0,2},{1,3},{2,4},{3,5},{4,6},{5,7},{6,0},{7,1},{8,10},{9,11},{10,... | collective-permute-start | bytes 786440 | tf_op jit(solution)/shard_map/ppermute | solution.py:250
  5.4 14.3 %collective-permute-start.1 = (bf16[64,2048]{1,0:T(8,128)(2,1)S(1)}, bf16[64,2048]{1,0:T(8,128)(2,1)S(1)}, u32[]{:S(2)}, u32[]{:S(2)}) collective-permute-start(bf16[64,2048]{1,0:T(8,128)(2,1)S(1)} %get-tuple-element.72), channel_id=1, source_target_pairs={{0,4},{1,5},{2,6},{3,7},{4,0},{5,1},{6,2},{7,3},{8,12},{9,13},{10,... | collective-permute-start | bytes 786440 | tf_op jit(solution)/shard_map/ppermute | solution.py:250
  7.6 12.9 %collective-permute-start.2 = (bf16[64,2048]{1,0:T(8,128)(2,1)S(1)}, bf16[64,2048]{1,0:T(8,128)(2,1)S(1)}, u32[]{:S(2)}, u32[]{:S(2)}) collective-permute-start(bf16[64,2048]{1,0:T(8,128)(2,1)S(1)} %get-tuple-element.73), channel_id=1, source_target_pairs={{0,6},{1,7},{2,0},{3,1},{4,2},{5,3},{6,4},{7,5},{8,14},{9,15},{10,... | collective-permute-start | bytes 786440 | tf_op jit(solution)/shard_map/ppermute | solution.py:250
  9.3 1.9 %collective-permute-start.6 = (f32[1]{0:T(128)}, f32[1]{0:T(128)}, u32[]{:S(2)}, u32[]{:S(2)}) collective-permute-start(f32[1]{0:T(128)} %convert_element_type.3.counts), channel_id=1, source_target_pairs={{0,8},{8,0},{16,24},{24,16},{32,40},{40,32},{48,56},{56,48},{64,72... | collective-permute-start | bytes 20 | tf_op jit(solution)/shard_map/ppermute | solution.py:251
  11.2 2.2 %copy-start = (bf16[1,256,8192]{2,1,0:T(8,128)(2,1)S(1)}, bf16[1,256,8192]{2,1,0:T(8,128)(2,1)}, u32[]{:S(2)}) copy-start(bf16[1,256,8192]{2,1,0:T(8,128)(2,1)} %param.7) | copy-start | bytes 12582916
  13.4 2.8 %copy-start.1 = (bf16[128,8192]{1,0:T(8,128)(2,1)S(1)}, bf16[128,8192]{1,0:T(8,128)(2,1)}, u32[]{:S(2)}) copy-start(bf16[128,8192]{1,0:T(8,128)(2,1)} %x.1) | copy-start | bytes 6291460
  13.4 2.8 %copy-start.5 = (bf16[128,512]{1,0:T(8,128)(2,1)S(1)}, bf16[128,512]{1,0:T(8,128)(2,1)}, u32[]{:S(2)}) copy-start(bf16[128,512]{1,0:T(8,128)(2,1)} %cot.1) | copy-start | bytes 393220
  14.9 15.2 %collective-permute-start.8 = (bf16[272,1024]{1,0:T(8,128)(2,1)S(1)}, bf16[272,1024]{1,0:T(8,128)(2,1)S(1)}, u32[]{:S(2)}, u32[]{:S(2)}) collective-permute-start(bf16[272,1024]{1,0:T(8,128)(2,1)S(1)} %get-tuple-element.82), channel_id=1, source_target_pairs={{0,64},{8,72},{16,80},{24,88},{32,96},{40,104},{48,112},{56,120},{... | collective-permute-start | bytes 1671176 | tf_op jit(solution)/shard_map/ppermute | solution.py:251
  20.5 32.4 %collective-permute-start.10 = (bf16[256,2048]{1,0:T(8,128)(2,1)S(1)}, bf16[256,2048]{1,0:T(8,128)(2,1)S(1)}, u32[]{:S(2)}, u32[]{:S(2)}) collective-permute-start(bf16[256,2048]{1,0:T(8,128)(2,1)S(1)} %stack_weight.1), channel_id=1, source_target_pairs={{0,1},{1,0},{2,3},{3,2},{4,5},{5,4},{6,7},{7,6},{8,9},{9,8},{10,11... | collective-permute-start | bytes 3145736 | tf_op jit(solution)/shard_map/ppermute | solution.py:250
  21.4 21.7 %collective-permute-start.3 = (bf16[160,2048]{1,0:T(8,128)(2,1)S(1)}, bf16[160,2048]{1,0:T(8,128)(2,1)S(1)}, u32[]{:S(2)}, u32[]{:S(2)}) collective-permute-start(bf16[160,2048]{1,0:T(8,128)(2,1)S(1)} %get-tuple-element.75), channel_id=1, source_target_pairs={{0,2},{1,3},{2,4},{3,5},{4,6},{5,7},{6,0},{7,1},{8,10},{9,11},{10,... | collective-permute-start | bytes 1966088 | tf_op jit(solution)/shard_map/ppermute | solution.py:250
  22.0 30.9 %collective-permute-start.4 = (bf16[160,2048]{1,0:T(8,128)(2,1)S(1)}, bf16[160,2048]{1,0:T(8,128)(2,1)S(1)}, u32[]{:S(2)}, u32[]{:S(2)}) collective-permute-start(bf16[160,2048]{1,0:T(8,128)(2,1)S(1)} %get-tuple-element.76), channel_id=1, source_target_pairs={{0,4},{1,5},{2,6},{3,7},{4,0},{5,1},{6,2},{7,3},{8,12},{9,13},{10,... | collective-permute-start | bytes 1966088 | tf_op jit(solution)/shard_map/ppermute | solution.py:250
  24.8 28.1 %collective-permute-start.5 = (bf16[160,2048]{1,0:T(8,128)(2,1)S(1)}, bf16[160,2048]{1,0:T(8,128)(2,1)S(1)}, u32[]{:S(2)}, u32[]{:S(2)}) collective-permute-start(bf16[160,2048]{1,0:T(8,128)(2,1)S(1)} %get-tuple-element.77), channel_id=1, source_target_pairs={{0,6},{1,7},{2,0},{3,1},{4,2},{5,3},{6,4},{7,5},{8,14},{9,15},{10,... | collective-permute-start | bytes 1966088 | tf_op jit(solution)/shard_map/ppermute | solution.py:250
  30.1 13.0 %collective-permute-start.9 = (bf16[272,1024]{1,0:T(8,128)(2,1)S(1)}, bf16[272,1024]{1,0:T(8,128)(2,1)S(1)}, u32[]{:S(2)}, u32[]{:S(2)}) collective-permute-start(bf16[272,1024]{1,0:T(8,128)(2,1)S(1)} %get-tuple-element.83), channel_id=1, source_target_pairs={{0,192},{8,200},{16,208},{24,216},{32,224},{40,232},{48,240},{56,2... | collective-permute-start | bytes 1671176 | tf_op jit(solution)/shard_map/ppermute | solution.py:251
  56.9 33.8 %collective-permute-start.20 = (bf16[256,2048]{1,0:T(8,128)(2,1)S(1)}, bf16[256,2048]{1,0:T(8,128)(2,1)S(1)}, u32[]{:S(2)}, u32[]{:S(2)}) collective-permute-start(bf16[256,2048]{1,0:T(8,128)(2,1)S(1)} %get-tuple-element.90), channel_id=1, source_target_pairs={{0,1},{1,0},{2,3},{3,2},{4,5},{5,4},{6,7},{7,6},{8,9},{9,8},{10,11... | collective-permute-start | bytes 3145736 | tf_op jit(solution)/shard_map/ppermute | solution.py:250
  58.3 13.7 %collective-permute-start.11 = (bf16[272,1024]{1,0:T(8,128)(2,1)S(1)}, bf16[272,1024]{1,0:T(8,128)(2,1)S(1)}, u32[]{:S(2)}, u32[]{:S(2)}) collective-permute-start(bf16[272,1024]{1,0:T(8,128)(2,1)S(1)} %get-tuple-element.93), channel_id=1, source_target_pairs={{0,128},{8,136},{16,144},{24,152},{32,160},{40,168},{48,176},{56,1... | collective-permute-start | bytes 1671176 | tf_op jit(solution)/shard_map/ppermute | solution.py:251
  60.0 17.5 %collective-permute-start.14 = (bf16[128,2048]{1,0:T(8,128)(2,1)S(1)}, bf16[128,2048]{1,0:T(8,128)(2,1)S(1)}, u32[]{:S(2)}, u32[]{:S(2)}) collective-permute-start(bf16[128,2048]{1,0:T(8,128)(2,1)S(1)} %get-tuple-element.106), channel_id=1, source_target_pairs={{0,6},{1,7},{2,0},{3,1},{4,2},{5,3},{6,4},{7,5},{8,14},{9,15},{10,... | collective-permute-start | bytes 1572872 | tf_op jit(solution)/shard_map/ppermute | solution.py:250
  63.4 14.1 %collective-permute-start.15 = (bf16[128,2048]{1,0:T(8,128)(2,1)S(1)}, bf16[128,2048]{1,0:T(8,128)(2,1)S(1)}, u32[]{:S(2)}, u32[]{:S(2)}) collective-permute-start(bf16[128,2048]{1,0:T(8,128)(2,1)S(1)} %get-tuple-element.107), channel_id=1, source_target_pairs={{0,4},{1,5},{2,6},{3,7},{4,0},{5,1},{6,2},{7,3},{8,12},{9,13},{10,... | collective-permute-start | bytes 1572872 | tf_op jit(solution)/shard_map/ppermute | solution.py:250
  64.1 25.8 %collective-permute-start.16 = (bf16[128,2048]{1,0:T(8,128)(2,1)S(1)}, bf16[128,2048]{1,0:T(8,128)(2,1)S(1)}, u32[]{:S(2)}, u32[]{:S(2)}) collective-permute-start(bf16[128,2048]{1,0:T(8,128)(2,1)S(1)} %get-tuple-element.108), channel_id=1, source_target_pairs={{0,2},{1,3},{2,4},{3,5},{4,6},{5,7},{6,0},{7,1},{8,10},{9,11},{10,... | collective-permute-start | bytes 1572872 | tf_op jit(solution)/shard_map/ppermute | solution.py:250
  72.3 23.1 %collective-permute-start.12 = (bf16[272,512]{1,0:T(8,128)(2,1)S(1)}, bf16[272,512]{1,0:T(8,128)(2,1)S(1)}, u32[]{:S(2)}, u32[]{:S(2)}) collective-permute-start(bf16[272,512]{1,0:T(8,128)(2,1)S(1)} %get-tuple-element.100), channel_id=1, source_target_pairs={{0,16},{8,24},{16,0},{24,8},{32,48},{40,56},{48,32},{56,40},{64,80... | collective-permute-start | bytes 835592 | tf_op jit(solution)/shard_map/ppermute | solution.py:251
  90.0 5.4 %collective-permute-start.17 = (bf16[128,512]{1,0:T(8,128)(2,1)S(1)}, bf16[128,512]{1,0:T(8,128)(2,1)S(1)}, u32[]{:S(2)}, u32[]{:S(2)}) collective-permute-start(bf16[128,512]{1,0:T(8,128)(2,1)S(1)} %get-tuple-element.115), channel_id=1, source_target_pairs={{0,6},{1,7},{2,0},{3,1},{4,2},{5,3},{6,4},{7,5},{8,14},{9,15},{10,... | collective-permute-start | bytes 393224 | tf_op jit(solution)/shard_map/ppermute | solution.py:250
  90.0 11.1 %collective-permute-start.18 = (bf16[128,512]{1,0:T(8,128)(2,1)S(1)}, bf16[128,512]{1,0:T(8,128)(2,1)S(1)}, u32[]{:S(2)}, u32[]{:S(2)}) collective-permute-start(bf16[128,512]{1,0:T(8,128)(2,1)S(1)} %get-tuple-element.116), channel_id=1, source_target_pairs={{0,4},{1,5},{2,6},{3,7},{4,0},{5,1},{6,2},{7,3},{8,12},{9,13},{10,... | collective-permute-start | bytes 393224 | tf_op jit(solution)/shard_map/ppermute | solution.py:250
  91.0 21.5 %collective-permute-start.21 = (bf16[64,2048]{1,0:T(8,128)(2,1)S(1)}, bf16[64,2048]{1,0:T(8,128)(2,1)S(1)}, u32[]{:S(2)}, u32[]{:S(2)}) collective-permute-start(bf16[64,2048]{1,0:T(8,128)(2,1)S(1)} %get-tuple-element.124), channel_id=1, source_target_pairs={{0,2},{1,3},{2,4},{3,5},{4,6},{5,7},{6,0},{7,1},{8,10},{9,11},{10,... | collective-permute-start | bytes 786440 | tf_op jit(solution)/shard_map/ppermute | solution.py:250
  91.9 20.6 %collective-permute-start.22 = (bf16[64,2048]{1,0:T(8,128)(2,1)S(1)}, bf16[64,2048]{1,0:T(8,128)(2,1)S(1)}, u32[]{:S(2)}, u32[]{:S(2)}) collective-permute-start(bf16[64,2048]{1,0:T(8,128)(2,1)S(1)} %get-tuple-element.125), channel_id=1, source_target_pairs={{0,4},{1,5},{2,6},{3,7},{4,0},{5,1},{6,2},{7,3},{8,12},{9,13},{10,... | collective-permute-start | bytes 786440 | tf_op jit(solution)/shard_map/ppermute | solution.py:250
  95.3 17.2 %collective-permute-start.23 = (bf16[64,2048]{1,0:T(8,128)(2,1)S(1)}, bf16[64,2048]{1,0:T(8,128)(2,1)S(1)}, u32[]{:S(2)}, u32[]{:S(2)}) collective-permute-start(bf16[64,2048]{1,0:T(8,128)(2,1)S(1)} %get-tuple-element.126), channel_id=1, source_target_pairs={{0,6},{1,7},{2,0},{3,1},{4,2},{5,3},{6,4},{7,5},{8,14},{9,15},{10,... | collective-permute-start | bytes 786440 | tf_op jit(solution)/shard_map/ppermute | solution.py:250
  95.4 16.2 %copy-start.3 = (f32[256,256]{1,0:T(8,128)S(1)}, f32[256,256]{1,0:T(8,128)}, u32[]{:S(2)}) copy-start(f32[256,256]{1,0:T(8,128)} %refs_2_.1) | copy-start | bytes 786436
  95.4 16.2 %copy-start.4 = (f32[256,256]{1,0:T(8,128)S(1)}, f32[256,256]{1,0:T(8,128)}, u32[]{:S(2)}) copy-start(f32[256,256]{1,0:T(8,128)} %refs_3_.1) | copy-start | bytes 786436
  95.4 16.1 %collective-permute-start.13 = (bf16[272,256]{1,0:T(8,128)(2,1)S(1)}, bf16[272,256]{1,0:T(8,128)(2,1)S(1)}, u32[]{:S(2)}, u32[]{:S(2)}) collective-permute-start(bf16[272,256]{1,0:T(8,128)(2,1)S(1)} %get-tuple-element.102), channel_id=1, source_target_pairs={{0,48},{8,56},{16,32},{24,40},{32,16},{40,24},{48,0},{56,8},{64,11... | collective-permute-start | bytes 417800 | tf_op jit(solution)/shard_map/ppermute | solution.py:251
  101.1 9.8 %collective-permute-start.19 = (bf16[128,512]{1,0:T(8,128)(2,1)S(1)}, bf16[128,512]{1,0:T(8,128)(2,1)S(1)}, u32[]{:S(2)}, u32[]{:S(2)}) collective-permute-start(bf16[128,512]{1,0:T(8,128)(2,1)S(1)} %get-tuple-element.117), channel_id=1, source_target_pairs={{0,2},{1,3},{2,4},{3,5},{4,6},{5,7},{6,0},{7,1},{8,10},{9,11},{10,... | collective-permute-start | bytes 393224 | tf_op jit(solution)/shard_map/ppermute | solution.py:250

commit v3 on v2

--- a/solution.py
+++ b/solution.py
@@ -30,10 +30,8 @@
 CORE_SWAP = [(r, r ^ 1) for r in range(32)]
 
 
-def x_shift(k):
-    return [(r, (r + 8 * k) % 32) for r in range(32)]
-
-
+X_NEAR = [(r, r ^ 8) for r in range(32)]
+X_FAR = [(r, r ^ 24) for r in range(32)]
 ZH_NEAR = [(r, r ^ 2) for r in range(32)]
 ZH_FAR = [(r, r ^ 6) for r in range(32)]
 
@@ -102,11 +100,11 @@
 
 def stack(*refs):
     for k in range(4):
-        refs[4][ROWS * k : ROWS * k + ROWS, :] = refs[k][...]
+        refs[4][ROWS * k : ROWS * k + ROWS, :] = refs[k][0:ROWS, :]
 
 
 def grad_to_inputs(*refs):
-    got, other, xs, outs, w, cots = refs[:4], refs[4], refs[5:9], refs[9:13], refs[13], refs[14]
+    got, other, xs, outs, w, turned, cots = refs[:4], refs[4], refs[5:9], refs[9:13], refs[13], refs[14], refs[15]
     y, z = here()
     for k in range(4):
         owner = (y + 4 - k) % 4
@@ -118,21 +116,15 @@
         part = jnp.dot(cots[...], w[:, c : c + 512], preferred_element_type=F32).astype(BF16)
         for k in range(4):
             outs[k][:, c : c + 512] = part[TOK * k : TOK * k + TOK]
+    turned[...] = cots[...].T
 
 
 def weight_grad(scale, *refs):
-    xs, cots, mine, other, whole = refs[:4], refs[4], refs[5], refs[6], refs[7]
+    xs, turned, mine, other, whole = refs[:4], refs[4], refs[5], refs[6], refs[7]
     y, z = here()
     for c in range(0, SEG, 256):
-        total = None
-        for k in range(4):
-            term = lax.dot_general(
-                cots[TOK * k : TOK * k + TOK, :],
-                xs[k][0:TOK, c : c + 256],
-                (((0,), (0,)), ((), ())),
-                preferred_element_type=F32,
-            )
-            total = term if total is None else total + term
+        columns = jnp.concatenate([x[0:TOK, c : c + 256] for x in xs], axis=0)
+        total = jnp.dot(turned[...], columns, preferred_element_type=F32)
         whole[:, c : c + 256] = (total * scale).astype(BF16)
     for j in range(4):
         to = (y + j) % 4 * 2
@@ -143,31 +135,36 @@
 
 def project(*refs):
     xs, w, outs = refs[:4], refs[4], refs[5:9]
-    for k in range(4):
-        outs[k][...] = lax.dot_general(
-            xs[k][0:TOK, :], w[...], (((1,), (1,)), ((), ())), preferred_element_type=F32
-        ).astype(BF16)
-
-
-def sum_keys(*refs):
-    total = refs[0][...].astype(F32)
-    for r in refs[1:4]:
-        total = total + r[...].astype(F32)
-    refs[4][...] = total.astype(BF16)
-
-
-def join_grads(mine, recv, *outs):
+    total = None
+    for c in range(0, SEG, 512):
+        columns = jnp.concatenate([x[0:TOK, c : c + 512] for x in xs], axis=0)
+        term = lax.dot_general(columns, w[:, c : c + 512], (((1,), (1,)), ((), ())), preferred_element_type=F32)
+        total = term if total is None else total + term
+    for k in range(4):
+        outs[k][...] = total[TOK * k : TOK * k + TOK, :].astype(BF16)
+
+
+def join_grads(mine, recv, *refs):
+    parts, outs = refs[:4], refs[4:8]
     for j in range(4):
         rows = slice(ROWS * j, ROWS * j + ROWS)
-        outs[j][...] = (mine[rows, :].astype(F32) + recv[rows, :].astype(F32)).astype(BF16)
+        outs[j][0:ROWS, :] = (mine[rows, :].astype(F32) + recv[rows, :].astype(F32)).astype(BF16)
+        for i in range(4):
+            outs[j][ROWS : ROWS + 32, KVI * i : KVI * i + KVI] = parts[(4 - j) % 4][32 * i : 32 * i + 32, :]
 
 
 def finish(*refs):
-    got, grads = refs[:4], refs[4]
+    got, grads, keys = refs[:4], refs[4], refs[5]
     y, _ = here()
     for j in range(4):
         owner = (y + 4 - j) % 4
-        grads[:, pl.ds(pl.multiple_of(owner * SEG, SEG), SEG)] = got[j][...]
+        grads[:, pl.ds(pl.multiple_of(owner * SEG, SEG), SEG)] = got[j][0:ROWS, :]
+    for i in range(4):
+        total = None
+        for j in range(4):
+            term = got[j][ROWS : ROWS + 32, KVI * i : KVI * i + KVI].astype(F32)
+            total = term if total is None else total + term
+        keys[32 * i : 32 * i + 32, :] = total.astype(BF16)
 
 
 def put_count(ref, row, value):
@@ -188,39 +185,36 @@
     return total[0:1, :]
 
 
-def weigh(counts, counts_other, mine, other, *outs):
+def weigh(counts, counts_other, mine, other, keep, send):
     r = lax.axis_index("replica")
     x, core = r // 8, r % 2
     own, theirs = counts[0], counts_other[0]
-    for k in range(4):
-        for h in range(4):
-            start = pl.multiple_of((x + k) % 4 * 2048 + h * 512 + core * 256, 256)
-            cols = pl.ds(start, 256)
-            total = own * mine[:, cols].astype(F32) + theirs * other[:, cols].astype(F32)
-            outs[k][0:256, 256 * h : 256 * h + 256] = total.astype(BF16)
-        put_count(outs[k], 256, jnp.full((1, 128), own + theirs, F32))
-
-
-def sum_blocks(*refs):
-    parts, keep, send = refs[:4], refs[4], refs[5]
+    for out, first in ((keep, x), (send, x + 1 - 2 * (x % 2))):
+        for i, block in enumerate((first, 3 - first)):
+            for h in range(4):
+                cols = pl.ds(pl.multiple_of(block * 2048 + h * 512 + core * 256, 256), 256)
+                total = own * mine[:, cols].astype(F32) + theirs * other[:, cols].astype(F32)
+                out[0:256, 1024 * i + 256 * h : 1024 * i + 256 * h + 256] = total.astype(BF16)
+        put_count(out, 256, jnp.full((1, 128), own + theirs, F32))
+
+
+def halve(kept, recv, keep, send):
+    count = take_count((kept, recv), 256)
+    width = kept.shape[1] // 2
+    for i, out in enumerate((keep, send)):
+        cols = slice(width * i, width * i + width)
+        out[0:256, :] = (kept[0:256, cols].astype(F32) + recv[0:256, cols].astype(F32)).astype(BF16)
+        put_count(out, 256, count)
+
+
+def sum_blocks(kept, recv, keep, send):
     zh = lax.axis_index("replica") // 2 % 4
-    near = zh + 1 - 2 * (zh % 2)
-    count = take_count(parts, 256)
-    for out, first in ((keep, zh), (send, near)):
+    count = take_count((kept, recv), 256)
+    for out, first in ((keep, zh), (send, zh + 1 - 2 * (zh % 2))):
         for i, block in enumerate((first, 3 - first)):
             cols = pl.ds(pl.multiple_of(block * 256, 256), 256)
-            total = parts[0][0:256, cols].astype(F32)
-            for p in parts[1:]:
-                total = total + p[0:256, cols].astype(F32)
+            total = kept[0:256, cols].astype(F32) + recv[0:256, cols].astype(F32)
             out[0:256, 256 * i : 256 * i + 256] = total.astype(BF16)
-        put_count(out, 256, count)
-
-
-def halve_blocks(kept, recv, keep, send):
-    count = take_count((kept, recv), 256)
-    for i, out in enumerate((keep, send)):
-        cols = slice(256 * i, 256 * i + 256)
-        out[0:256, :] = (kept[0:256, cols].astype(F32) + recv[0:256, cols].astype(F32)).astype(BF16)
         put_count(out, 256, count)
 
 
@@ -258,13 +252,13 @@
     got = {k: fsdp(sent[k], y_shift(k)) for k in (1, 3, 2)}
     got = [sent[0], got[1], got[2], got[3]]
 
-    parts = call(
+    kept, send = call(
         weigh,
         "weigh",
         [(SMEM, count), (SMEM, count_other), (VMEM, frag), (VMEM, frag_other)],
-        [(VMEM, shape(272, 1024))] * 4,
-    )
-    x1, x3 = replica(parts[1], x_shift(1)), replica(parts[3], x_shift(3))
+        [(VMEM, shape(272, 2048))] * 2,
+    )
+    x_near = replica(send, X_NEAR)
 
     packed = call(
         pack_inputs,
@@ -277,54 +271,52 @@
     (stacked,) = call(stack, "stack_weight", [(VMEM, a) for a in got], [(VMEM, shape(4 * ROWS, SEG))])
     crossed = fsdp(stacked, Z_SWAP)
     xs = [packed[0]] + [fsdp(packed[k], y_shift(k)) for k in (1, 2, 3)]
-    got, (x1, x3, t2) = together(got, (x1, x3, parts[2]))
-    parts = [parts[0], x1, replica(t2, x_shift(2)), x3]
-
-    *back, w_full, cots = call(
+    kept, send = call(halve, "halve_x", [(VMEM, kept), (VMEM, x_near)], [(VMEM, shape(272, 1024))] * 2)
+    got, (kept, send) = together(got, (kept, send))
+    x_far = replica(send, X_FAR)
+
+    *back, w_full, turned = call(
         grad_to_inputs,
         "input_grad",
         [(VMEM, a) for a in (*got, crossed, *xs)],
-        [(VMEM, shape(TOK, SEG))] * 4 + [(VMEM, shape(KVI, SEG)), (VMEM, shape(4 * TOK, KVI))],
-    )
-    back = [back[0]] + [fsdp(back[k], y_shift(-k)) for k in (1, 2, 3)]
-
+        [(VMEM, shape(TOK, SEG))] * 4 + [(VMEM, shape(KVI, SEG)), (VMEM, shape(KVI, 4 * TOK))],
+        [pltpu.VMEM((4 * TOK, KVI), BF16)],
+    )
     mine, other = call(
         functools.partial(weight_grad, 1.0 / (TOK * lax.axis_size("fsdp"))),
         "weight_grad",
-        [(VMEM, a) for a in (*xs, cots)],
+        [(VMEM, a) for a in (*xs, turned)],
         [(VMEM, shape(4 * ROWS, SEG))] * 2,
         [pltpu.VMEM((KVI, SEG), BF16)],
     )
+    back = [back[0]] + [fsdp(back[k], y_shift(-k)) for k in (1, 2, 3)]
     recv = fsdp(other, Z_SWAP)
-    (other,), parts = together((other,), parts)
-    kept, send = call(sum_blocks, "sum_blocks", [(VMEM, a) for a in parts], [(VMEM, shape(272, 512))] * 2)
+    kept, send = call(sum_blocks, "sum_blocks", [(VMEM, kept), (VMEM, x_far)], [(VMEM, shape(272, 512))] * 2)
+    (send,), (w_full,) = together((send,), (w_full,))
     near = replica(send, ZH_NEAR)
     keys = call(project, "project", [(VMEM, a) for a in (*xs, w_full)], [(VMEM, shape(TOK, KVI))] * 4)
-    kept, send = call(
-        halve_blocks, "halve_blocks", [(VMEM, kept), (VMEM, near)], [(VMEM, shape(272, 256))] * 2
-    )
-    far = replica(send, ZH_FAR)
-    back, keys = together(back, keys)
-    keys = [keys[0]] + [fsdp(keys[k], y_shift(-k)) for k in (1, 2, 3)]
-    (back_full,) = call(
-        unpack_columns, "unpack_input_grad", [(ANY, a) for a in back], [(ANY, shape(TOK, 8192))], [dma((4,))]
-    )
-
+    (recv,), back = together((recv,), back)
     joined = call(
         join_grads,
         "join_grads",
-        [(VMEM, mine), (VMEM, recv)],
-        [(VMEM, shape(ROWS, SEG))] * 4,
+        [(VMEM, a) for a in (mine, recv, *keys)],
+        [(VMEM, shape(ROWS + 32, SEG))] * 4,
     )
     joined = [joined[0]] + [fsdp(joined[j], y_shift(j)) for j in (1, 2, 3)]
-    (projected,) = call(sum_keys, "sum_keys", [(VMEM, a) for a in keys], [(VMEM, shape(TOK, KVI))])
+    (back_full,) = call(
+        unpack_columns, "unpack_input_grad", [(ANY, a) for a in back], [(ANY, shape(TOK, 8192))], [dma((4,))]
+    )
+    kept, send = call(halve, "halve_z", [(VMEM, kept), (VMEM, near)], [(VMEM, shape(272, 256))] * 2)
+    far = replica(send, ZH_FAR)
     new_master, new_momentum = call(
         outer_step,
         "outer_step",
         [(VMEM, a) for a in (kept, far, master, momentum)],
         [(VMEM, shape(256, 256, dtype=F32))] * 2,
     )
-    (grads,) = call(finish, "finish", [(VMEM, a) for a in joined], [(VMEM, shape(ROWS, 8192))])
+    grads, projected = call(
+        finish, "finish", [(VMEM, a) for a in joined], [(VMEM, shape(ROWS, 8192)), (VMEM, shape(TOK, KVI))]
+    )
     return new_master, new_momentum, projected, back_full, grads[None]
 
 

time: 114 us -> 110 us (0.965)
  the two profiles are of different devices: /device:TPU:1 before, /device:TPU:8 now
where the time goes in v3:
time: 110 us; the launch traced here: 109 us
  waiting for transfers between devices  60.1 us (55%)
  starting transfers between devices  33.5 us (30%)
  Pallas kernels  10.4 us (9%)
  local copies, waits for them, and re-layouts  3.43 us (3%)
  between operations  1.46 us (1%)
    ppermute x14, waiting for transfers between devices, local(): fsdp = lambda a, perm: lax.ppermute(a, 'fsdp', perm)  31.6 us
    ppermute x6, waiting for transfers between devices, local(): replica = lambda a, perm: lax.ppermute(a, 'replica', perm)  28.5 us
    ppermute x14, starting transfers between devices, local(): fsdp = lambda a, perm: lax.ppermute(a, 'fsdp', perm)  20.3 us
    ppermute x6, starting transfers between devices, local(): replica = lambda a, perm: lax.ppermute(a, 'replica', perm)  13.2 us
    pallas_call x14, Pallas kernels, call(): pl.pallas_call(kernel, name=name, in_specs=[s for s, _ in ins], out_specs...  10.4 us
    unnamed x12, local copies, waits for them, and re-layouts  3.43 us
  transfers between devices with their start and end apart: 20, of which 11 were waited for; matrix products, arithmetic and copies ran while one was open for 0% of the time, Pallas kernels for 6%

profile of v3, /device:TPU:8, one launch (start us, length us, event | category | flops | bytes accessed | tf_op | source)
XLA Modules:
  0.0 108.9 jit_solution(15242863519893318046)
XLA Ops:
  0.6 0.1 collective-permute-start.4
  0.7 0.0 copy-start.2
  0.7 1.2 %copy-done.2 = bf16[1,64,8192]{2,1,0:T(8,128)(2,1)S(1)} copy-done((bf16[1,64,8192]{2,1,0:T(8,128)(2,1)S(1)}, bf16[1,64,8192]{2,1,0:T(8,128)(2,1)}, u32[]{:S(2)}) %copy-start.2) | copy-done | bytes 1048600
  2.0 0.1 pack_weight.1
  2.1 1.7 %collective-permute-start = (bf16[64,2048]{1,0:T(8,128)(2,1)S(1)}, bf16[64,2048]{1,0:T(8,128)(2,1)S(1)}, u32[]{:S(2)}, u32[]{:S(2)}) collective-permute-start(bf16[64,2048]{1,0:T(8,128)(2,1)S(1)} %get-tuple-element.67), channel_id=1, source_target_pairs={{0,2},{1,3},{2,4},{3,5},{4,6},{5,7},{6,0},{7,1},{8,10},{9,11},{10,... | collective-permute-start | bytes 786440 | tf_op jit(solution)/shard_map/ppermute | solution.py:244
  3.7 2.7 %collective-permute-start.1 = (bf16[64,2048]{1,0:T(8,128)(2,1)S(1)}, bf16[64,2048]{1,0:T(8,128)(2,1)S(1)}, u32[]{:S(2)}, u32[]{:S(2)}) collective-permute-start(bf16[64,2048]{1,0:T(8,128)(2,1)S(1)} %get-tuple-element.68), channel_id=1, source_target_pairs={{0,4},{1,5},{2,6},{3,7},{4,0},{5,1},{6,2},{7,3},{8,12},{9,13},{10,... | collective-permute-start | bytes 786440 | tf_op jit(solution)/shard_map/ppermute | solution.py:244
  6.4 0.7 collective-permute-start.2
  7.7 0.9 collective-permute-start.3
  8.7 0.3 collective-permute-done.3.counts_other
  8.9 0.0 collective-permute-done.4.other
  8.9 0.0 copy-start
  8.9 2.2 %copy-done = bf16[1,256,8192]{2,1,0:T(8,128)(2,1)S(1)} copy-done((bf16[1,256,8192]{2,1,0:T(8,128)(2,1)S(1)}, bf16[1,256,8192]{2,1,0:T(8,128)(2,1)}, u32[]{:S(2)}) %copy-start) | copy-done | bytes 4194328
  11.1 1.6 %weigh.1 = (bf16[272,2048]{1,0:T(8,128)(2,1)S(1)}, bf16[272,2048]{1,0:T(8,128)(2,1)S(1)}) custom-call(f32[1]{0:T(128)} %convert_element_type.3.counts, f32[1]{0:T(128)} %collective-permute-done.3.counts_other, bf16[256,8192]{1,0:T(8,128)(2,1)S(1)} %bitcast.4, bf16[256,8192]{1,0:T(8,128)(2,1)S(1)} %collective-permute-done.4.other), custom_call_target="tpu_custom_call" | custom-call | tf_op jit(solution)/shard_map/weigh/pallas_call | solution.py:41
  12.7 1.6 %collective-permute-start.5 = (bf16[272,2048]{1,0:T(8,128)(2,1)S(1)}, bf16[272,2048]{1,0:T(8,128)(2,1)S(1)}, u32[]{:S(2)}, u32[]{:S(2)}) collective-permute-start(bf16[272,2048]{1,0:T(8,128)(2,1)S(1)} %get-tuple-element.75), channel_id=1, source_target_pairs={{0,64},{8,72},{16,80},{24,88},{32,96},{40,104},{48,112},{56,120},{... | collective-permute-start | bytes 3342344 | tf_op jit(solution)/shard_map/ppermute | solution.py:245
  14.3 0.0 copy-done.1
  14.3 0.0 copy-done.5
  14.3 0.5 pack_inputs.1
  14.8 0.0 collective-permute-done.refs_1_
  14.8 0.0 collective-permute-done.1.refs_2_
  14.9 4.4 %collective-permute-done.2.refs_3_ = bf16[64,2048]{1,0:T(8,128)(2,1)S(1)} collective-permute-done((bf16[64,2048]{1,0:T(8,128)(2,1)S(1)}, bf16[64,2048]{1,0:T(8,128)(2,1)S(1)}, u32[]{:S(2)}, u32[]{:S(2)}) %collective-permute-start.2) | collective-permute-done | bytes 262176 | tf_op jit(solution)/shard_map/ppermute | solution.py:244
  19.3 0.1 stack_weight.1
  19.4 1.3 %collective-permute-start.7 = (bf16[256,2048]{1,0:T(8,128)(2,1)S(1)}, bf16[256,2048]{1,0:T(8,128)(2,1)S(1)}, u32[]{:S(2)}, u32[]{:S(2)}) collective-permute-start(bf16[256,2048]{1,0:T(8,128)(2,1)S(1)} %stack_weight.1), channel_id=1, source_target_pairs={{0,1},{1,0},{2,3},{3,2},{4,5},{5,4},{6,7},{7,6},{8,9},{9,8},{10,11... | collective-permute-start | bytes 3145736 | tf_op jit(solution)/shard_map/ppermute | solution.py:244
  20.7 1.3 %collective-permute-start.8 = (bf16[160,2048]{1,0:T(8,128)(2,1)S(1)}, bf16[160,2048]{1,0:T(8,128)(2,1)S(1)}, u32[]{:S(2)}, u32[]{:S(2)}) collective-permute-start(bf16[160,2048]{1,0:T(8,128)(2,1)S(1)} %get-tuple-element.87), channel_id=1, source_target_pairs={{0,2},{1,3},{2,4},{3,5},{4,6},{5,7},{6,0},{7,1},{8,10},{9,11},{10,... | collective-permute-start | bytes 1966088 | tf_op jit(solution)/shard_map/ppermute | solution.py:244
  22.0 1.6 %collective-permute-start.9 = (bf16[160,2048]{1,0:T(8,128)(2,1)S(1)}, bf16[160,2048]{1,0:T(8,128)(2,1)S(1)}, u32[]{:S(2)}, u32[]{:S(2)}) collective-permute-start(bf16[160,2048]{1,0:T(8,128)(2,1)S(1)} %get-tuple-element.88), channel_id=1, source_target_pairs={{0,4},{1,5},{2,6},{3,7},{4,0},{5,1},{6,2},{7,3},{8,12},{9,13},{10,... | collective-permute-start | bytes 1966088 | tf_op jit(solution)/shard_map/ppermute | solution.py:244
  23.5 1.6 %collective-permute-start.10 = (bf16[160,2048]{1,0:T(8,128)(2,1)S(1)}, bf16[160,2048]{1,0:T(8,128)(2,1)S(1)}, u32[]{:S(2)}, u32[]{:S(2)}) collective-permute-start(bf16[160,2048]{1,0:T(8,128)(2,1)S(1)} %get-tuple-element.89), channel_id=1, source_target_pairs={{0,6},{1,7},{2,0},{3,1},{4,2},{5,3},{6,4},{7,5},{8,14},{9,15},{10,... | collective-permute-start | bytes 1966088 | tf_op jit(solution)/shard_map/ppermute | solution.py:244
  25.1 14.4 %collective-permute-done.5.recv = bf16[272,2048]{1,0:T(8,128)(2,1)S(1)} collective-permute-done((bf16[272,2048]{1,0:T(8,128)(2,1)S(1)}, bf16[272,2048]{1,0:T(8,128)(2,1)S(1)}, u32[]{:S(2)}, u32[]{:S(2)}) %collective-permute-start.5) | collective-permute-done | bytes 1114144 | tf_op jit(solution)/shard_map/ppermute | solution.py:245
  39.5 0.2 halve_x.1
  39.8 0.0 collective-permute-done.8.refs_6_.refs_1_
  39.8 1.4 %collective-permute-done.9.refs_7_.refs_2_ = bf16[160,2048]{1,0:T(8,128)(2,1)S(1)} collective-permute-done((bf16[160,2048]{1,0:T(8,128)(2,1)S(1)}, bf16[160,2048]{1,0:T(8,128)(2,1)S(1)}, u32[]{:S(2)}, u32[]{:S(2)}) %collective-permute-start.9) | collective-permute-done | bytes 655392 | tf_op jit(solution)/shard_map/ppermute | solution.py:244
  41.1 11.8 %collective-permute-done.10.refs_8_.refs_3_ = bf16[160,2048]{1,0:T(8,128)(2,1)S(1)} collective-permute-done((bf16[160,2048]{1,0:T(8,128)(2,1)S(1)}, bf16[160,2048]{1,0:T(8,128)(2,1)S(1)}, u32[]{:S(2)}, u32[]{:S(2)}) %collective-permute-start.10) | collective-permute-done | bytes 655392 | tf_op jit(solution)/shard_map/ppermute | solution.py:244
  53.0 0.0 collective-permute-done.7.refs_4_
  53.0 1.4 %input_grad.1 = (bf16[128,2048]{1,0:T(8,128)(2,1)S(1)}, bf16[128,2048]{1,0:T(8,128)(2,1)S(1)}, bf16[128,2048]{1,0:T(8,128)(2,1)S(1)}, bf16[128,2048]{1,0:T(8,128...) custom-call(bf16[64,2048]{1,0:T(8,128)(2,1)S(1)} %get-tuple-element.82.refs_0_, ...), custom_call_target="tpu_custom_call" | custom-call | tf_op jit(solution)/shard_map/input_grad/pallas_call | solution.py:41
  54.4 1.4 %weight_grad.1 = (bf16[256,2048]{1,0:T(8,128)(2,1)S(1)}, bf16[256,2048]{1,0:T(8,128)(2,1)S(1)}) custom-call(bf16[160,2048]{1,0:T(8,128)(2,1)S(1)} %get-tuple-element.86.refs_5_.refs_0_, bf16[160,2048]{1,0:T(8,128)(2,1)S(1)} %collective-permute-done.8.refs_6_.refs_1_, bf16[160,2048]{1,0:T(8,128)(2,1)S(1)} %collective-permute-done.9.refs_7_.refs_2_, ...), custom_call_target="tpu_custom_call" | custom-call | tf_op jit(solution)/shard_map/weight_grad/pallas_call | solution.py:41
  55.8 0.5 collective-permute-start.13
  56.3 2.7 %collective-permute-start.6 = (bf16[272,1024]{1,0:T(8,128)(2,1)S(1)}, bf16[272,1024]{1,0:T(8,128)(2,1)S(1)}, u32[]{:S(2)}, u32[]{:S(2)}) collective-permute-start(bf16[272,1024]{1,0:T(8,128)(2,1)S(1)} %get-tuple-element.79), channel_id=1, source_target_pairs={{0,192},{8,200},{16,208},{24,216},{32,224},{40,232},{48,240},{56,2... | collective-permute-start | bytes 1671176 | tf_op jit(solution)/shard_map/ppermute | solution.py:245
  59.0 0.5 collective-permute-start.14
  59.5 1.6 %collective-permute-start.15 = (bf16[128,2048]{1,0:T(8,128)(2,1)S(1)}, bf16[128,2048]{1,0:T(8,128)(2,1)S(1)}, u32[]{:S(2)}, u32[]{:S(2)}) collective-permute-start(bf16[128,2048]{1,0:T(8,128)(2,1)S(1)} %get-tuple-element.101), channel_id=1, source_target_pairs={{0,4},{1,5},{2,6},{3,7},{4,0},{5,1},{6,2},{7,3},{8,12},{9,13},{10,... | collective-permute-start | bytes 1572872 | tf_op jit(solution)/shard_map/ppermute | solution.py:244
  61.1 2.4 %collective-permute-start.16 = (bf16[128,2048]{1,0:T(8,128)(2,1)S(1)}, bf16[128,2048]{1,0:T(8,128)(2,1)S(1)}, u32[]{:S(2)}, u32[]{:S(2)}) collective-permute-start(bf16[128,2048]{1,0:T(8,128)(2,1)S(1)} %get-tuple-element.102), channel_id=1, source_target_pairs={{0,2},{1,3},{2,4},{3,5},{4,6},{5,7},{6,0},{7,1},{8,10},{9,11},{10,... | collective-permute-start | bytes 1572872 | tf_op jit(solution)/shard_map/ppermute | solution.py:244
  63.6 8.2 %collective-permute-done.6.recv = bf16[272,1024]{1,0:T(8,128)(2,1)S(1)} collective-permute-done((bf16[272,1024]{1,0:T(8,128)(2,1)S(1)}, bf16[272,1024]{1,0:T(8,128)(2,1)S(1)}, u32[]{:S(2)}, u32[]{:S(2)}) %collective-permute-start.6) | collective-permute-done | bytes 557088 | tf_op jit(solution)/shard_map/ppermute | solution.py:245
  71.8 0.2 sum_blocks.1
  72.0 3.3 %collective-permute-start.11 = (bf16[272,512]{1,0:T(8,128)(2,1)S(1)}, bf16[272,512]{1,0:T(8,128)(2,1)S(1)}, u32[]{:S(2)}, u32[]{:S(2)}) collective-permute-start(bf16[272,512]{1,0:T(8,128)(2,1)S(1)} %get-tuple-element.91), channel_id=1, source_target_pairs={{0,16},{8,24},{16,0},{24,8},{32,48},{40,56},{48,32},{56,40},{64,80... | collective-permute-start | bytes 835592 | tf_op jit(solution)/shard_map/ppermute | solution.py:245
  75.3 1.3 %project.1 = (bf16[128,512]{1,0:T(8,128)(2,1)S(1)}, bf16[128,512]{1,0:T(8,128)(2,1)S(1)}, bf16[128,512]{1,0:T(8,128)(2,1)S(1)}, bf16[128,512]{1,0:T(8,128)(2,1)S(1)}) custom-call(bf16[160,2048]{1,0:T(8,128)(2,1)S(1)} %get-tuple-element.86.refs_5_.refs_0_, bf16[160,2048]{1,0:T(8,128)(2,1)S(1)} %collective-permute-done.8.refs_6_.refs_1_, ...), custom_call_target="tpu_custom_call" | custom-call | tf_op jit(solution)/shard_map/project/pallas_call | solution.py:41
  76.6 0.0 copy-start.3
  76.6 0.0 copy-start.4
  76.6 0.0 collective-permute-done.14.refs_1_
  76.6 7.1 %collective-permute-done.15.refs_2_ = bf16[128,2048]{1,0:T(8,128)(2,1)S(1)} collective-permute-done((bf16[128,2048]{1,0:T(8,128)(2,1)S(1)}, bf16[128,2048]{1,0:T(8,128)(2,1)S(1)}, u32[]{:S(2)}, u32[]{:S(2)}) %collective-permute-start.15) | collective-permute-done | bytes 524320 | tf_op jit(solution)/shard_map/ppermute | solution.py:244
  83.7 1.7 %collective-permute-done.16.refs_3_ = bf16[128,2048]{1,0:T(8,128)(2,1)S(1)} collective-permute-done((bf16[128,2048]{1,0:T(8,128)(2,1)S(1)}, bf16[128,2048]{1,0:T(8,128)(2,1)S(1)}, u32[]{:S(2)}, u32[]{:S(2)}) %collective-permute-start.16) | collective-permute-done | bytes 524320 | tf_op jit(solution)/shard_map/ppermute | solution.py:244
  85.4 1.6 %collective-permute-done.13.recv = bf16[256,2048]{1,0:T(8,128)(2,1)S(1)} collective-permute-done((bf16[256,2048]{1,0:T(8,128)(2,1)S(1)}, bf16[256,2048]{1,0:T(8,128)(2,1)S(1)}, u32[]{:S(2)}, u32[]{:S(2)}) %collective-permute-start.13) | collective-permute-done | bytes 1048608 | tf_op jit(solution)/shard_map/ppermute | solution.py:244
  87.0 0.2 join_grads.1
  87.2 0.1 collective-permute-start.17
  87.3 2.9 %collective-permute-start.18 = (bf16[96,2048]{1,0:T(8,128)(2,1)S(1)}, bf16[96,2048]{1,0:T(8,128)(2,1)S(1)}, u32[]{:S(2)}, u32[]{:S(2)}) collective-permute-start(bf16[96,2048]{1,0:T(8,128)(2,1)S(1)} %get-tuple-element.111), channel_id=1, source_target_pairs={{0,4},{1,5},{2,6},{3,7},{4,0},{5,1},{6,2},{7,3},{8,12},{9,13},{10,... | collective-permute-start | bytes 1179656 | tf_op jit(solution)/shard_map/ppermute | solution.py:244
  90.2 1.6 %collective-permute-start.19 = (bf16[96,2048]{1,0:T(8,128)(2,1)S(1)}, bf16[96,2048]{1,0:T(8,128)(2,1)S(1)}, u32[]{:S(2)}, u32[]{:S(2)}) collective-permute-start(bf16[96,2048]{1,0:T(8,128)(2,1)S(1)} %get-tuple-element.112), channel_id=1, source_target_pairs={{0,6},{1,7},{2,0},{3,1},{4,2},{5,3},{6,4},{7,5},{8,14},{9,15},{10,... | collective-permute-start | bytes 1179656 | tf_op jit(solution)/shard_map/ppermute | solution.py:244
  91.8 0.0 collective-permute-done.11.recv
  91.8 0.1 halve_z.1
  91.9 4.6 %collective-permute-start.12 = (bf16[272,256]{1,0:T(8,128)(2,1)S(1)}, bf16[272,256]{1,0:T(8,128)(2,1)S(1)}, u32[]{:S(2)}, u32[]{:S(2)}) collective-permute-start(bf16[272,256]{1,0:T(8,128)(2,1)S(1)} %get-tuple-element.93), channel_id=1, source_target_pairs={{0,48},{8,56},{16,32},{24,40},{32,16},{40,24},{48,0},{56,8},{64,11... | collective-permute-start | bytes 417800 | tf_op jit(solution)/shard_map/ppermute | solution.py:245
  96.4 5.5 %collective-permute-done.12.refs_1_ = bf16[272,256]{1,0:T(8,128)(2,1)S(1)} collective-permute-done((bf16[272,256]{1,0:T(8,128)(2,1)S(1)}, bf16[272,256]{1,0:T(8,128)(2,1)S(1)}, u32[]{:S(2)}, u32[]{:S(2)}) %collective-permute-start.12) | collective-permute-done | bytes 139296 | tf_op jit(solution)/shard_map/ppermute | solution.py:245
  102.0 0.0 copy-done.3
  102.0 0.0 copy-done.4
  102.0 0.9 outer_step.1
  102.9 1.3 %unpack_input_grad.1 = bf16[128,8192]{1,0:T(8,128)(2,1)} custom-call(bf16[128,2048]{1,0:T(8,128)(2,1)S(1)} %get-tuple-element.114.refs_0_, bf16[128,2048]{1,0:T(8,128)(2,1)S(1)} %collective-permute-done.14.refs_1_, bf16[128,2048]{1,0:T(8,128)(2,1)S(1)} %collective-permute-done.15.refs_2_, bf16[128,2048]{1,0:T(8,128)(2,1)S(1)} %collective-permute-done.16.refs_3_), custom_call_target="tpu_custom_call" | custom-call | tf_op jit(solution)/shard_map/unpack_input_grad/pallas_call | solution.py:41
  104.2 0.0 collective-permute-done.17.refs_1_
  104.2 0.0 collective-permute-done.18.refs_2_
  104.2 3.6 %collective-permute-done.19.refs_3_ = bf16[96,2048]{1,0:T(8,128)(2,1)S(1)} collective-permute-done((bf16[96,2048]{1,0:T(8,128)(2,1)S(1)}, bf16[96,2048]{1,0:T(8,128)(2,1)S(1)}, u32[]{:S(2)}, u32[]{:S(2)}) %collective-permute-start.19) | collective-permute-done | bytes 393248 | tf_op jit(solution)/shard_map/ppermute | solution.py:244
  107.8 1.1 %finish.1 = (bf16[64,8192]{1,0:T(8,128)(2,1)}, bf16[128,512]{1,0:T(8,128)(2,1)}) custom-call(bf16[96,2048]{1,0:T(8,128)(2,1)S(1)} %get-tuple-element.109.refs_0_, bf16[96,2048]{1,0:T(8,128)(2,1)S(1)} %collective-permute-done.17.refs_1_, bf16[96,2048]{1,0:T(8,128)(2,1)S(1)} %collective-permute-done.18.refs_2_, ...), custom_call_target="tpu_custom_call" | custom-call | tf_op jit(solution)/shard_map/finish/pallas_call | solution.py:41
  (2 shorter events, 0.0 us)
Async XLA Ops:
  0.6 8.3 %collective-permute-start.4 = (bf16[256,8192]{1,0:T(8,128)(2,1)}, bf16[256,8192]{1,0:T(8,128)(2,1)S(1)}, u32[]{:S(2)}, u32[]{:S(2)}) collective-permute-start(bf16[256,8192]{1,0:T(8,128)(2,1)} %bitcast.3), channel_id=1, source_target_pairs={{0,8},{8,0},{16,24},{24,16},{32,40},{40,32},{48,56},{56,48},{64,72... | collective-permute-start | bytes 12582920 | tf_op jit(solution)/shard_map/ppermute | solution.py:245
  0.7 1.2 %copy-start.2 = (bf16[1,64,8192]{2,1,0:T(8,128)(2,1)S(1)}, bf16[1,64,8192]{2,1,0:T(8,128)(2,1)}, u32[]{:S(2)}) copy-start(bf16[1,64,8192]{2,1,0:T(8,128)(2,1)} %param.12) | copy-start | bytes 3145732
  2.1 12.8 %collective-permute-start = (bf16[64,2048]{1,0:T(8,128)(2,1)S(1)}, bf16[64,2048]{1,0:T(8,128)(2,1)S(1)}, u32[]{:S(2)}, u32[]{:S(2)}) collective-permute-start(bf16[64,2048]{1,0:T(8,128)(2,1)S(1)} %get-tuple-element.67), channel_id=1, source_target_pairs={{0,2},{1,3},{2,4},{3,5},{4,6},{5,7},{6,0},{7,1},{8,10},{9,11},{10,... | collective-permute-start | bytes 786440 | tf_op jit(solution)/shard_map/ppermute | solution.py:244
  3.7 11.1 %collective-permute-start.1 = (bf16[64,2048]{1,0:T(8,128)(2,1)S(1)}, bf16[64,2048]{1,0:T(8,128)(2,1)S(1)}, u32[]{:S(2)}, u32[]{:S(2)}) collective-permute-start(bf16[64,2048]{1,0:T(8,128)(2,1)S(1)} %get-tuple-element.68), channel_id=1, source_target_pairs={{0,4},{1,5},{2,6},{3,7},{4,0},{5,1},{6,2},{7,3},{8,12},{9,13},{10,... | collective-permute-start | bytes 786440 | tf_op jit(solution)/shard_map/ppermute | solution.py:244
  6.4 12.9 %collective-permute-start.2 = (bf16[64,2048]{1,0:T(8,128)(2,1)S(1)}, bf16[64,2048]{1,0:T(8,128)(2,1)S(1)}, u32[]{:S(2)}, u32[]{:S(2)}) collective-permute-start(bf16[64,2048]{1,0:T(8,128)(2,1)S(1)} %get-tuple-element.69), channel_id=1, source_target_pairs={{0,6},{1,7},{2,0},{3,1},{4,2},{5,3},{6,4},{7,5},{8,14},{9,15},{10,... | collective-permute-start | bytes 786440 | tf_op jit(solution)/shard_map/ppermute | solution.py:244
  7.7 1.2 %collective-permute-start.3 = (f32[1]{0:T(128)}, f32[1]{0:T(128)}, u32[]{:S(2)}, u32[]{:S(2)}) collective-permute-start(f32[1]{0:T(128)} %convert_element_type.3.counts), channel_id=1, source_target_pairs={{0,8},{8,0},{16,24},{24,16},{32,40},{40,32},{48,56},{56,48},{64,72... | collective-permute-start | bytes 20 | tf_op jit(solution)/shard_map/ppermute | solution.py:245
  8.9 2.2 %copy-start = (bf16[1,256,8192]{2,1,0:T(8,128)(2,1)S(1)}, bf16[1,256,8192]{2,1,0:T(8,128)(2,1)}, u32[]{:S(2)}) copy-start(bf16[1,256,8192]{2,1,0:T(8,128)(2,1)} %param.7) | copy-start | bytes 12582916
  11.1 3.2 %copy-start.1 = (bf16[128,8192]{1,0:T(8,128)(2,1)S(1)}, bf16[128,8192]{1,0:T(8,128)(2,1)}, u32[]{:S(2)}) copy-start(bf16[128,8192]{1,0:T(8,128)(2,1)} %x.1) | copy-start | bytes 6291460
  11.1 3.2 %copy-start.5 = (bf16[128,512]{1,0:T(8,128)(2,1)S(1)}, bf16[128,512]{1,0:T(8,128)(2,1)}, u32[]{:S(2)}) copy-start(bf16[128,512]{1,0:T(8,128)(2,1)} %cot.1) | copy-start | bytes 393220
  12.7 26.8 %collective-permute-start.5 = (bf16[272,2048]{1,0:T(8,128)(2,1)S(1)}, bf16[272,2048]{1,0:T(8,128)(2,1)S(1)}, u32[]{:S(2)}, u32[]{:S(2)}) collective-permute-start(bf16[272,2048]{1,0:T(8,128)(2,1)S(1)} %get-tuple-element.75), channel_id=1, source_target_pairs={{0,64},{8,72},{16,80},{24,88},{32,96},{40,104},{48,112},{56,120},{... | collective-permute-start | bytes 3342344 | tf_op jit(solution)/shard_map/ppermute | solution.py:245
  19.4 33.6 %collective-permute-start.7 = (bf16[256,2048]{1,0:T(8,128)(2,1)S(1)}, bf16[256,2048]{1,0:T(8,128)(2,1)S(1)}, u32[]{:S(2)}, u32[]{:S(2)}) collective-permute-start(bf16[256,2048]{1,0:T(8,128)(2,1)S(1)} %stack_weight.1), channel_id=1, source_target_pairs={{0,1},{1,0},{2,3},{3,2},{4,5},{5,4},{6,7},{7,6},{8,9},{9,8},{10,11... | collective-permute-start | bytes 3145736 | tf_op jit(solution)/shard_map/ppermute | solution.py:244
  20.7 19.1 %collective-permute-start.8 = (bf16[160,2048]{1,0:T(8,128)(2,1)S(1)}, bf16[160,2048]{1,0:T(8,128)(2,1)S(1)}, u32[]{:S(2)}, u32[]{:S(2)}) collective-permute-start(bf16[160,2048]{1,0:T(8,128)(2,1)S(1)} %get-tuple-element.87), channel_id=1, source_target_pairs={{0,2},{1,3},{2,4},{3,5},{4,6},{5,7},{6,0},{7,1},{8,10},{9,11},{10,... | collective-permute-start | bytes 1966088 | tf_op jit(solution)/shard_map/ppermute | solution.py:244
  22.0 19.2 %collective-permute-start.9 = (bf16[160,2048]{1,0:T(8,128)(2,1)S(1)}, bf16[160,2048]{1,0:T(8,128)(2,1)S(1)}, u32[]{:S(2)}, u32[]{:S(2)}) collective-permute-start(bf16[160,2048]{1,0:T(8,128)(2,1)S(1)} %get-tuple-element.88), channel_id=1, source_target_pairs={{0,4},{1,5},{2,6},{3,7},{4,0},{5,1},{6,2},{7,3},{8,12},{9,13},{10,... | collective-permute-start | bytes 1966088 | tf_op jit(solution)/shard_map/ppermute | solution.py:244
  23.5 29.5 %collective-permute-start.10 = (bf16[160,2048]{1,0:T(8,128)(2,1)S(1)}, bf16[160,2048]{1,0:T(8,128)(2,1)S(1)}, u32[]{:S(2)}, u32[]{:S(2)}) collective-permute-start(bf16[160,2048]{1,0:T(8,128)(2,1)S(1)} %get-tuple-element.89), channel_id=1, source_target_pairs={{0,6},{1,7},{2,0},{3,1},{4,2},{5,3},{6,4},{7,5},{8,14},{9,15},{10,... | collective-permute-start | bytes 1966088 | tf_op jit(solution)/shard_map/ppermute | solution.py:244
  55.8 31.1 %collective-permute-start.13 = (bf16[256,2048]{1,0:T(8,128)(2,1)S(1)}, bf16[256,2048]{1,0:T(8,128)(2,1)S(1)}, u32[]{:S(2)}, u32[]{:S(2)}) collective-permute-start(bf16[256,2048]{1,0:T(8,128)(2,1)S(1)} %get-tuple-element.98), channel_id=1, source_target_pairs={{0,1},{1,0},{2,3},{3,2},{4,5},{5,4},{6,7},{7,6},{8,9},{9,8},{10,11... | collective-permute-start | bytes 3145736 | tf_op jit(solution)/shard_map/ppermute | solution.py:244
  56.3 15.5 %collective-permute-start.6 = (bf16[272,1024]{1,0:T(8,128)(2,1)S(1)}, bf16[272,1024]{1,0:T(8,128)(2,1)S(1)}, u32[]{:S(2)}, u32[]{:S(2)}) collective-permute-start(bf16[272,1024]{1,0:T(8,128)(2,1)S(1)} %get-tuple-element.79), channel_id=1, source_target_pairs={{0,192},{8,200},{16,208},{24,216},{32,224},{40,232},{48,240},{56,2... | collective-permute-start | bytes 1671176 | tf_op jit(solution)/shard_map/ppermute | solution.py:245
  59.0 17.6 %collective-permute-start.14 = (bf16[128,2048]{1,0:T(8,128)(2,1)S(1)}, bf16[128,2048]{1,0:T(8,128)(2,1)S(1)}, u32[]{:S(2)}, u32[]{:S(2)}) collective-permute-start(bf16[128,2048]{1,0:T(8,128)(2,1)S(1)} %get-tuple-element.100), channel_id=1, source_target_pairs={{0,6},{1,7},{2,0},{3,1},{4,2},{5,3},{6,4},{7,5},{8,14},{9,15},{10,... | collective-permute-start | bytes 1572872 | tf_op jit(solution)/shard_map/ppermute | solution.py:244
  59.5 24.2 %collective-permute-start.15 = (bf16[128,2048]{1,0:T(8,128)(2,1)S(1)}, bf16[128,2048]{1,0:T(8,128)(2,1)S(1)}, u32[]{:S(2)}, u32[]{:S(2)}) collective-permute-start(bf16[128,2048]{1,0:T(8,128)(2,1)S(1)} %get-tuple-element.101), channel_id=1, source_target_pairs={{0,4},{1,5},{2,6},{3,7},{4,0},{5,1},{6,2},{7,3},{8,12},{9,13},{10,... | collective-permute-start | bytes 1572872 | tf_op jit(solution)/shard_map/ppermute | solution.py:244
  61.1 24.3 %collective-permute-start.16 = (bf16[128,2048]{1,0:T(8,128)(2,1)S(1)}, bf16[128,2048]{1,0:T(8,128)(2,1)S(1)}, u32[]{:S(2)}, u32[]{:S(2)}) collective-permute-start(bf16[128,2048]{1,0:T(8,128)(2,1)S(1)} %get-tuple-element.102), channel_id=1, source_target_pairs={{0,2},{1,3},{2,4},{3,5},{4,6},{5,7},{6,0},{7,1},{8,10},{9,11},{10,... | collective-permute-start | bytes 1572872 | tf_op jit(solution)/shard_map/ppermute | solution.py:244
  72.0 19.8 %collective-permute-start.11 = (bf16[272,512]{1,0:T(8,128)(2,1)S(1)}, bf16[272,512]{1,0:T(8,128)(2,1)S(1)}, u32[]{:S(2)}, u32[]{:S(2)}) collective-permute-start(bf16[272,512]{1,0:T(8,128)(2,1)S(1)} %get-tuple-element.91), channel_id=1, source_target_pairs={{0,16},{8,24},{16,0},{24,8},{32,48},{40,56},{48,32},{56,40},{64,80... | collective-permute-start | bytes 835592 | tf_op jit(solution)/shard_map/ppermute | solution.py:245
  76.6 25.4 %copy-start.3 = (f32[256,256]{1,0:T(8,128)S(1)}, f32[256,256]{1,0:T(8,128)}, u32[]{:S(2)}) copy-start(f32[256,256]{1,0:T(8,128)} %refs_2_.1) | copy-start | bytes 786436
  76.6 25.4 %copy-start.4 = (f32[256,256]{1,0:T(8,128)S(1)}, f32[256,256]{1,0:T(8,128)}, u32[]{:S(2)}) copy-start(f32[256,256]{1,0:T(8,128)} %refs_3_.1) | copy-start | bytes 786436
  87.2 17.0 %collective-permute-start.17 = (bf16[96,2048]{1,0:T(8,128)(2,1)S(1)}, bf16[96,2048]{1,0:T(8,128)(2,1)S(1)}, u32[]{:S(2)}, u32[]{:S(2)}) collective-permute-start(bf16[96,2048]{1,0:T(8,128)(2,1)S(1)} %get-tuple-element.110), channel_id=1, source_target_pairs={{0,2},{1,3},{2,4},{3,5},{4,6},{5,7},{6,0},{7,1},{8,10},{9,11},{10,... | collective-permute-start | bytes 1179656 | tf_op jit(solution)/shard_map/ppermute | solution.py:244
  87.3 16.9 %collective-permute-start.18 = (bf16[96,2048]{1,0:T(8,128)(2,1)S(1)}, bf16[96,2048]{1,0:T(8,128)(2,1)S(1)}, u32[]{:S(2)}, u32[]{:S(2)}) collective-permute-start(bf16[96,2048]{1,0:T(8,128)(2,1)S(1)} %get-tuple-element.111), channel_id=1, source_target_pairs={{0,4},{1,5},{2,6},{3,7},{4,0},{5,1},{6,2},{7,3},{8,12},{9,13},{10,... | collective-permute-start | bytes 1179656 | tf_op jit(solution)/shard_map/ppermute | solution.py:244
  90.2 17.6 %collective-permute-start.19 = (bf16[96,2048]{1,0:T(8,128)(2,1)S(1)}, bf16[96,2048]{1,0:T(8,128)(2,1)S(1)}, u32[]{:S(2)}, u32[]{:S(2)}) collective-permute-start(bf16[96,2048]{1,0:T(8,128)(2,1)S(1)} %get-tuple-element.112), channel_id=1, source_target_pairs={{0,6},{1,7},{2,0},{3,1},{4,2},{5,3},{6,4},{7,5},{8,14},{9,15},{10,... | collective-permute-start | bytes 1179656 | tf_op jit(solution)/shard_map/ppermute | solution.py:244
  91.9 10.1 %collective-permute-start.12 = (bf16[272,256]{1,0:T(8,128)(2,1)S(1)}, bf16[272,256]{1,0:T(8,128)(2,1)S(1)}, u32[]{:S(2)}, u32[]{:S(2)}) collective-permute-start(bf16[272,256]{1,0:T(8,128)(2,1)S(1)} %get-tuple-element.93), channel_id=1, source_target_pairs={{0,48},{8,56},{16,32},{24,40},{32,16},{40,24},{48,0},{56,8},{64,11... | collective-permute-start | bytes 417800 | tf_op jit(solution)/shard_map/ppermute | solution.py:245

commit v4 on v3

--- a/solution.py
+++ b/solution.py
@@ -66,26 +66,26 @@
         c.wait()
 
 
-def pack_weight(w, *rest):
+def pack_weight(w, cot, *rest):
     outs, sems = rest[:4], rest[4]
     y, _ = here()
     copies = []
-    for k in (1, 3, 2, 0):
+    for k in (2, 1, 3, 0):
         start = pl.multiple_of((y + k) % 4 * SEG, SEG)
-        copies.append(pltpu.make_async_copy(w.at[:, pl.ds(start, SEG)], outs[k], sems.at[k]))
-    run_all(copies)
-
-
-def pack_inputs(x, cot, *rest):
+        copies.append((w.at[:, pl.ds(start, SEG)], outs[k].at[pl.ds(0, ROWS)]))
+        for j in range(4):
+            copies.append((cot.at[pl.ds(32 * j, 32)], outs[k].at[pl.ds(ROWS, 32), pl.ds(KVI * j, KVI)]))
+    run_all([pltpu.make_async_copy(s, d, sems.at[i]) for i, (s, d) in enumerate(copies)])
+
+
+def pack_inputs(x, *rest):
     outs, sems = rest[:4], rest[4]
     y, _ = here()
     copies = []
     for k in range(4):
         start = pl.multiple_of((y + k) % 4 * SEG, SEG)
-        copies.append((x.at[:, pl.ds(start, SEG)], outs[k].at[pl.ds(0, TOK)]))
-        for j in range(4):
-            copies.append((cot.at[pl.ds(32 * j, 32)], outs[k].at[pl.ds(TOK, 32), pl.ds(KVI * j, KVI)]))
-    run_all([pltpu.make_async_copy(s, d, sems.at[i]) for i, (s, d) in enumerate(copies)])
+        copies.append(pltpu.make_async_copy(x.at[:, pl.ds(start, SEG)], outs[k], sems.at[k]))
+    run_all(copies)
 
 
 def unpack_columns(*refs):
@@ -104,14 +104,14 @@
 
 
 def grad_to_inputs(*refs):
-    got, other, xs, outs, w, turned, cots = refs[:4], refs[4], refs[5:9], refs[9:13], refs[13], refs[14], refs[15]
+    got, other, outs, w, turned, cots = refs[:4], refs[4], refs[5:9], refs[9], refs[10], refs[11]
     y, z = here()
     for k in range(4):
         owner = (y + 4 - k) % 4
-        w[pl.ds(pl.multiple_of((owner * 2 + z) * ROWS, ROWS), ROWS), :] = got[k][...]
+        w[pl.ds(pl.multiple_of((owner * 2 + z) * ROWS, ROWS), ROWS), :] = got[k][0:ROWS, :]
         w[pl.ds(pl.multiple_of((owner * 2 + 1 - z) * ROWS, ROWS), ROWS), :] = other[ROWS * k : ROWS * k + ROWS, :]
         for j in range(4):
-            cots[TOK * k + 32 * j : TOK * k + 32 * j + 32, :] = xs[k][TOK : TOK + 32, KVI * j : KVI * j + KVI]
+            cots[TOK * k + 32 * j : TOK * k + 32 * j + 32, :] = got[k][ROWS : ROWS + 32, KVI * j : KVI * j + KVI]
     for c in range(0, SEG, 512):
         part = jnp.dot(cots[...], w[:, c : c + 512], preferred_element_type=F32).astype(BF16)
         for k in range(4):
@@ -123,7 +123,7 @@
     xs, turned, mine, other, whole = refs[:4], refs[4], refs[5], refs[6], refs[7]
     y, z = here()
     for c in range(0, SEG, 256):
-        columns = jnp.concatenate([x[0:TOK, c : c + 256] for x in xs], axis=0)
+        columns = jnp.concatenate([x[:, c : c + 256] for x in xs], axis=0)
         total = jnp.dot(turned[...], columns, preferred_element_type=F32)
         whole[:, c : c + 256] = (total * scale).astype(BF16)
     for j in range(4):
@@ -137,7 +137,7 @@
     xs, w, outs = refs[:4], refs[4], refs[5:9]
     total = None
     for c in range(0, SEG, 512):
-        columns = jnp.concatenate([x[0:TOK, c : c + 512] for x in xs], axis=0)
+        columns = jnp.concatenate([x[:, c : c + 512] for x in xs], axis=0)
         term = lax.dot_general(columns, w[:, c : c + 512], (((1,), (1,)), ((), ())), preferred_element_type=F32)
         total = term if total is None else total + term
     for k in range(4):
@@ -248,7 +248,13 @@
     count = counts.astype(F32)
     frag_other, count_other = replica(frag, CORE_SWAP), replica(count, CORE_SWAP)
 
-    sent = call(pack_weight, "pack_weight", [(HBM, inner_weight[0])], [(ANY, shape(ROWS, SEG))] * 4, [dma((4,))])
+    sent = call(
+        pack_weight,
+        "pack_weight",
+        [(HBM, inner_weight[0]), (HBM, cotangent)],
+        [(ANY, shape(ROWS + 32, SEG))] * 4,
+        [dma((20,))],
+    )
     got = {k: fsdp(sent[k], y_shift(k)) for k in (1, 3, 2)}
     got = [sent[0], got[1], got[2], got[3]]
 
@@ -260,13 +266,7 @@
     )
     x_near = replica(send, X_NEAR)
 
-    packed = call(
-        pack_inputs,
-        "pack_inputs",
-        [(HBM, inputs), (HBM, cotangent)],
-        [(ANY, shape(TOK + 32, SEG))] * 4,
-        [dma((20,))],
-    )
+    packed = call(pack_inputs, "pack_inputs", [(HBM, inputs)], [(ANY, shape(TOK, SEG))] * 4, [dma((4,))])
     packed, got = together(packed, got)
     (stacked,) = call(stack, "stack_weight", [(VMEM, a) for a in got], [(VMEM, shape(4 * ROWS, SEG))])
     crossed = fsdp(stacked, Z_SWAP)
@@ -278,7 +278,7 @@
     *back, w_full, turned = call(
         grad_to_inputs,
         "input_grad",
-        [(VMEM, a) for a in (*got, crossed, *xs)],
+        [(VMEM, a) for a in (*got, crossed)],
         [(VMEM, shape(TOK, SEG))] * 4 + [(VMEM, shape(KVI, SEG)), (VMEM, shape(KVI, 4 * TOK))],
         [pltpu.VMEM((4 * TOK, KVI), BF16)],
     )
@@ -289,6 +289,7 @@
         [(VMEM, shape(4 * ROWS, SEG))] * 2,
         [pltpu.VMEM((KVI, SEG), BF16)],
     )
+    back, (x_far,) = together(back, (x_far,))
     back = [back[0]] + [fsdp(back[k], y_shift(-k)) for k in (1, 2, 3)]
     recv = fsdp(other, Z_SWAP)
     kept, send = call(sum_blocks, "sum_blocks", [(VMEM, kept), (VMEM, x_far)], [(VMEM, shape(272, 512))] * 2)

time: 110 us -> 109 us (level)
    ppermute x6, waiting for transfers between devices: 28.5 us -> 14.1 us  [local(): replica = lambda a, perm: lax.ppermute(a, 'replica', perm)]
    ppermute x14, waiting for transfers between devices: 31.6 us -> 45.2 us  [local(): fsdp = lambda a, perm: lax.ppermute(a, 'fsdp', perm)]
    ppermute x6, starting transfers between devices: 13.2 us -> 12 us  [local(): replica = lambda a, perm: lax.ppermute(a, 'replica', perm)]
  transfers between devices with their start and end apart: 20 -> 20, of which waited for: 11 -> 10; matrix products, arithmetic and copies ran while one was open for 0% -> 0% of each run, Pallas kernels for 6% -> 9%
where the time goes in v4:
time: 109 us; the launch traced here: 108 us
  waiting for transfers between devices  59.2 us (54%)
  starting transfers between devices  33 us (30%)
  Pallas kernels  10.4 us (10%)
  local copies, waits for them, and re-layouts  4.33 us (4%)
  between operations  1.47 us (1%)
    ppermute x14, waiting for transfers between devices, local(): fsdp = lambda a, perm: lax.ppermute(a, 'fsdp', perm)  45.2 us
    ppermute x14, starting transfers between devices, local(): fsdp = lambda a, perm: lax.ppermute(a, 'fsdp', perm)  21 us
    ppermute x6, waiting for transfers between devices, local(): replica = lambda a, perm: lax.ppermute(a, 'replica', perm)  14.1 us
    ppermute x6, starting transfers between devices, local(): replica = lambda a, perm: lax.ppermute(a, 'replica', perm)  12 us
    pallas_call x14, Pallas kernels, call(): pl.pallas_call(kernel, name=name, in_specs=[s for s, _ in ins], out_specs...  10.4 us
    unnamed x12, local copies, waits for them, and re-layouts  4.33 us
  transfers between devices with their start and end apart: 20, of which 10 were waited for; matrix products, arithmetic and copies ran while one was open for 0% of the time, Pallas kernels for 9%

profile of v4, /device:TPU:8, one launch (start us, length us, event | category | flops | bytes accessed | tf_op | source)
XLA Modules:
  0.0 108.4 jit_solution(14820283192924769302)
XLA Ops:
  0.6 0.1 collective-permute-start.4
  0.7 0.0 copy-start.2
  0.7 1.2 %copy-done.2 = bf16[1,64,8192]{2,1,0:T(8,128)(2,1)S(1)} copy-done((bf16[1,64,8192]{2,1,0:T(8,128)(2,1)S(1)}, bf16[1,64,8192]{2,1,0:T(8,128)(2,1)}, u32[]{:S(2)}) %copy-start.2) | copy-done | bytes 1048600
  2.0 0.0 copy-start.5
  2.0 0.9 copy-done.5
  2.9 0.5 pack_weight.1
  3.3 1.7 %collective-permute-start = (bf16[96,2048]{1,0:T(8,128)(2,1)S(1)}, bf16[96,2048]{1,0:T(8,128)(2,1)S(1)}, u32[]{:S(2)}, u32[]{:S(2)}) collective-permute-start(bf16[96,2048]{1,0:T(8,128)(2,1)S(1)} %get-tuple-element.72), channel_id=1, source_target_pairs={{0,2},{1,3},{2,4},{3,5},{4,6},{5,7},{6,0},{7,1},{8,10},{9,11},{10,... | collective-permute-start | bytes 1179656 | tf_op jit(solution)/shard_map/ppermute | solution.py:244
  5.0 2.7 %collective-permute-start.1 = (bf16[96,2048]{1,0:T(8,128)(2,1)S(1)}, bf16[96,2048]{1,0:T(8,128)(2,1)S(1)}, u32[]{:S(2)}, u32[]{:S(2)}) collective-permute-start(bf16[96,2048]{1,0:T(8,128)(2,1)S(1)} %get-tuple-element.73), channel_id=1, source_target_pairs={{0,4},{1,5},{2,6},{3,7},{4,0},{5,1},{6,2},{7,3},{8,12},{9,13},{10,... | collective-permute-start | bytes 1179656 | tf_op jit(solution)/shard_map/ppermute | solution.py:244
  7.7 0.7 collective-permute-start.2
  9.0 0.9 collective-permute-start.3
  9.9 0.3 collective-permute-done.3.counts_other
  10.2 0.0 collective-permute-done.4.other
  10.2 2.2 %copy-done = bf16[1,256,8192]{2,1,0:T(8,128)(2,1)S(1)} copy-done((bf16[1,256,8192]{2,1,0:T(8,128)(2,1)S(1)}, bf16[1,256,8192]{2,1,0:T(8,128)(2,1)}, u32[]{:S(2)}) %copy-start) | copy-done | bytes 4194328
  12.4 1.6 %weigh.1 = (bf16[272,2048]{1,0:T(8,128)(2,1)S(1)}, bf16[272,2048]{1,0:T(8,128)(2,1)S(1)}) custom-call(f32[1]{0:T(128)} %convert_element_type.3.counts, f32[1]{0:T(128)} %collective-permute-done.3.counts_other, bf16[256,8192]{1,0:T(8,128)(2,1)S(1)} %bitcast.4, bf16[256,8192]{1,0:T(8,128)(2,1)S(1)} %collective-permute-done.4.other), custom_call_target="tpu_custom_call" | custom-call | tf_op jit(solution)/shard_map/weigh/pallas_call | solution.py:41
  14.0 1.6 %collective-permute-start.5 = (bf16[272,2048]{1,0:T(8,128)(2,1)S(1)}, bf16[272,2048]{1,0:T(8,128)(2,1)S(1)}, u32[]{:S(2)}, u32[]{:S(2)}) collective-permute-start(bf16[272,2048]{1,0:T(8,128)(2,1)S(1)} %get-tuple-element.80), channel_id=1, source_target_pairs={{0,64},{8,72},{16,80},{24,88},{32,96},{40,104},{48,112},{56,120},{... | collective-permute-start | bytes 3342344 | tf_op jit(solution)/shard_map/ppermute | solution.py:245
  15.5 0.0 copy-done.1
  15.5 0.2 pack_inputs.1
  15.7 0.0 collective-permute-done.refs_1_
  15.7 2.7 %collective-permute-done.1.refs_2_ = bf16[96,2048]{1,0:T(8,128)(2,1)S(1)} collective-permute-done((bf16[96,2048]{1,0:T(8,128)(2,1)S(1)}, bf16[96,2048]{1,0:T(8,128)(2,1)S(1)}, u32[]{:S(2)}, u32[]{:S(2)}) %collective-permute-start.1) | collective-permute-done | bytes 393248 | tf_op jit(solution)/shard_map/ppermute | solution.py:244
  18.5 7.7 %collective-permute-done.2.refs_3_ = bf16[96,2048]{1,0:T(8,128)(2,1)S(1)} collective-permute-done((bf16[96,2048]{1,0:T(8,128)(2,1)S(1)}, bf16[96,2048]{1,0:T(8,128)(2,1)S(1)}, u32[]{:S(2)}, u32[]{:S(2)}) %collective-permute-start.2) | collective-permute-done | bytes 393248 | tf_op jit(solution)/shard_map/ppermute | solution.py:244
  26.1 0.1 stack_weight.1
  26.2 1.3 %collective-permute-start.6 = (bf16[256,2048]{1,0:T(8,128)(2,1)S(1)}, bf16[256,2048]{1,0:T(8,128)(2,1)S(1)}, u32[]{:S(2)}, u32[]{:S(2)}) collective-permute-start(bf16[256,2048]{1,0:T(8,128)(2,1)S(1)} %stack_weight.1), channel_id=1, source_target_pairs={{0,1},{1,0},{2,3},{3,2},{4,5},{5,4},{6,7},{7,6},{8,9},{9,8},{10,11... | collective-permute-start | bytes 3145736 | tf_op jit(solution)/shard_map/ppermute | solution.py:244
  27.5 1.3 %collective-permute-start.10 = (bf16[128,2048]{1,0:T(8,128)(2,1)S(1)}, bf16[128,2048]{1,0:T(8,128)(2,1)S(1)}, u32[]{:S(2)}, u32[]{:S(2)}) collective-permute-start(bf16[128,2048]{1,0:T(8,128)(2,1)S(1)} %get-tuple-element.103), channel_id=1, source_target_pairs={{0,2},{1,3},{2,4},{3,5},{4,6},{5,7},{6,0},{7,1},{8,10},{9,11},{10,... | collective-permute-start | bytes 1572872 | tf_op jit(solution)/shard_map/ppermute | solution.py:244
  28.8 1.6 %collective-permute-start.11 = (bf16[128,2048]{1,0:T(8,128)(2,1)S(1)}, bf16[128,2048]{1,0:T(8,128)(2,1)S(1)}, u32[]{:S(2)}, u32[]{:S(2)}) collective-permute-start(bf16[128,2048]{1,0:T(8,128)(2,1)S(1)} %get-tuple-element.104), channel_id=1, source_target_pairs={{0,4},{1,5},{2,6},{3,7},{4,0},{5,1},{6,2},{7,3},{8,12},{9,13},{10,... | collective-permute-start | bytes 1572872 | tf_op jit(solution)/shard_map/ppermute | solution.py:244
  30.4 1.6 %collective-permute-start.12 = (bf16[128,2048]{1,0:T(8,128)(2,1)S(1)}, bf16[128,2048]{1,0:T(8,128)(2,1)S(1)}, u32[]{:S(2)}, u32[]{:S(2)}) collective-permute-start(bf16[128,2048]{1,0:T(8,128)(2,1)S(1)} %get-tuple-element.105), channel_id=1, source_target_pairs={{0,6},{1,7},{2,0},{3,1},{4,2},{5,3},{6,4},{7,5},{8,14},{9,15},{10,... | collective-permute-start | bytes 1572872 | tf_op jit(solution)/shard_map/ppermute | solution.py:244
  32.0 8.8 %collective-permute-done.5.recv = bf16[272,2048]{1,0:T(8,128)(2,1)S(1)} collective-permute-done((bf16[272,2048]{1,0:T(8,128)(2,1)S(1)}, bf16[272,2048]{1,0:T(8,128)(2,1)S(1)}, u32[]{:S(2)}, u32[]{:S(2)}) %collective-permute-start.5) | collective-permute-done | bytes 1114144 | tf_op jit(solution)/shard_map/ppermute | solution.py:245
  40.8 0.2 halve_x.1
  41.0 2.8 %collective-permute-start.7 = (bf16[272,1024]{1,0:T(8,128)(2,1)S(1)}, bf16[272,1024]{1,0:T(8,128)(2,1)S(1)}, u32[]{:S(2)}, u32[]{:S(2)}) collective-permute-start(bf16[272,1024]{1,0:T(8,128)(2,1)S(1)} %get-tuple-element.92), channel_id=1, source_target_pairs={{0,192},{8,200},{16,208},{24,216},{32,224},{40,232},{48,240},{56,2... | collective-permute-start | bytes 1671176 | tf_op jit(solution)/shard_map/ppermute | solution.py:245
  43.8 7.5 %collective-permute-done.6.refs_4_ = bf16[256,2048]{1,0:T(8,128)(2,1)S(1)} collective-permute-done((bf16[256,2048]{1,0:T(8,128)(2,1)S(1)}, bf16[256,2048]{1,0:T(8,128)(2,1)S(1)}, u32[]{:S(2)}, u32[]{:S(2)}) %collective-permute-start.6) | collective-permute-done | bytes 1048608 | tf_op jit(solution)/shard_map/ppermute | solution.py:244
  51.4 1.4 %input_grad.1 = (bf16[128,2048]{1,0:T(8,128)(2,1)S(1)}, bf16[128,2048]{1,0:T(8,128)(2,1)S(1)}, bf16[128,2048]{1,0:T(8,128)(2,1)S(1)}, bf16[128,2048]{1,0:T(8,128...) custom-call(bf16[96,2048]{1,0:T(8,128)(2,1)S(1)} %get-tuple-element.84.refs_0_, ...), custom_call_target="tpu_custom_call" | custom-call | tf_op jit(solution)/shard_map/input_grad/pallas_call | solution.py:41
  52.8 0.0 collective-permute-done.10.refs_1_
  52.8 0.0 collective-permute-done.11.refs_2_
  52.8 1.4 %collective-permute-done.12.refs_3_ = bf16[128,2048]{1,0:T(8,128)(2,1)S(1)} collective-permute-done((bf16[128,2048]{1,0:T(8,128)(2,1)S(1)}, bf16[128,2048]{1,0:T(8,128)(2,1)S(1)}, u32[]{:S(2)}, u32[]{:S(2)}) %collective-permute-start.12) | collective-permute-done | bytes 524320 | tf_op jit(solution)/shard_map/ppermute | solution.py:244
  54.2 1.4 %weight_grad.1 = (bf16[256,2048]{1,0:T(8,128)(2,1)S(1)}, bf16[256,2048]{1,0:T(8,128)(2,1)S(1)}) custom-call(bf16[128,2048]{1,0:T(8,128)(2,1)S(1)} %get-tuple-element.102.refs_0_, bf16[128,2048]{1,0:T(8,128)(2,1)S(1)} %collective-permute-done.10.refs_1_, bf16[128,2048]{1,0:T(8,128)(2,1)S(1)} %collective-permute-done.11.refs_2_, ...), custom_call_target="tpu_custom_call" | custom-call | tf_op jit(solution)/shard_map/weight_grad/pallas_call | solution.py:41
  55.6 0.5 collective-permute-start.13
  56.1 0.1 collective-permute-done.7.recv
  56.2 1.7 %collective-permute-start.14 = (bf16[128,2048]{1,0:T(8,128)(2,1)S(1)}, bf16[128,2048]{1,0:T(8,128)(2,1)S(1)}, u32[]{:S(2)}, u32[]{:S(2)}) collective-permute-start(bf16[128,2048]{1,0:T(8,128)(2,1)S(1)} %get-tuple-element.110), channel_id=1, source_target_pairs={{0,6},{1,7},{2,0},{3,1},{4,2},{5,3},{6,4},{7,5},{8,14},{9,15},{10,... | collective-permute-start | bytes 1572872 | tf_op jit(solution)/shard_map/ppermute | solution.py:244
  57.9 1.1 %collective-permute-start.15 = (bf16[128,2048]{1,0:T(8,128)(2,1)S(1)}, bf16[128,2048]{1,0:T(8,128)(2,1)S(1)}, u32[]{:S(2)}, u32[]{:S(2)}) collective-permute-start(bf16[128,2048]{1,0:T(8,128)(2,1)S(1)} %get-tuple-element.111), channel_id=1, source_target_pairs={{0,4},{1,5},{2,6},{3,7},{4,0},{5,1},{6,2},{7,3},{8,12},{9,13},{10,... | collective-permute-start | bytes 1572872 | tf_op jit(solution)/shard_map/ppermute | solution.py:244
  59.1 2.4 %collective-permute-start.16 = (bf16[128,2048]{1,0:T(8,128)(2,1)S(1)}, bf16[128,2048]{1,0:T(8,128)(2,1)S(1)}, u32[]{:S(2)}, u32[]{:S(2)}) collective-permute-start(bf16[128,2048]{1,0:T(8,128)(2,1)S(1)} %get-tuple-element.112), channel_id=1, source_target_pairs={{0,2},{1,3},{2,4},{3,5},{4,6},{5,7},{6,0},{7,1},{8,10},{9,11},{10,... | collective-permute-start | bytes 1572872 | tf_op jit(solution)/shard_map/ppermute | solution.py:244
  61.4 0.2 sum_blocks.1
  61.6 2.5 %collective-permute-start.8 = (bf16[272,512]{1,0:T(8,128)(2,1)S(1)}, bf16[272,512]{1,0:T(8,128)(2,1)S(1)}, u32[]{:S(2)}, u32[]{:S(2)}) collective-permute-start(bf16[272,512]{1,0:T(8,128)(2,1)S(1)} %get-tuple-element.97), channel_id=1, source_target_pairs={{0,16},{8,24},{16,0},{24,8},{32,48},{40,56},{48,32},{56,40},{64,80... | collective-permute-start | bytes 835592 | tf_op jit(solution)/shard_map/ppermute | solution.py:245
  64.1 1.3 %project.1 = (bf16[128,512]{1,0:T(8,128)(2,1)S(1)}, bf16[128,512]{1,0:T(8,128)(2,1)S(1)}, bf16[128,512]{1,0:T(8,128)(2,1)S(1)}, bf16[128,512]{1,0:T(8,128)(2,1)S(1)}) custom-call(bf16[128,2048]{1,0:T(8,128)(2,1)S(1)} %get-tuple-element.102.refs_0_, bf16[128,2048]{1,0:T(8,128)(2,1)S(1)} %collective-permute-done.10.refs_1_, ...), custom_call_target="tpu_custom_call" | custom-call | tf_op jit(solution)/shard_map/project/pallas_call | solution.py:41
  65.4 0.0 copy-start.3
  65.4 0.0 copy-start.4
  65.4 21.3 %collective-permute-done.13.recv = bf16[256,2048]{1,0:T(8,128)(2,1)S(1)} collective-permute-done((bf16[256,2048]{1,0:T(8,128)(2,1)S(1)}, bf16[256,2048]{1,0:T(8,128)(2,1)S(1)}, u32[]{:S(2)}, u32[]{:S(2)}) %collective-permute-start.13) | collective-permute-done | bytes 1048608 | tf_op jit(solution)/shard_map/ppermute | solution.py:244
  86.8 0.0 collective-permute-done.14.refs_1_
  86.8 0.0 collective-permute-done.15.refs_2_
  86.8 0.0 collective-permute-done.16.refs_3_
  86.8 0.2 join_grads.1
  87.0 0.1 collective-permute-start.17
  87.1 2.0 %collective-permute-start.18 = (bf16[96,2048]{1,0:T(8,128)(2,1)S(1)}, bf16[96,2048]{1,0:T(8,128)(2,1)S(1)}, u32[]{:S(2)}, u32[]{:S(2)}) collective-permute-start(bf16[96,2048]{1,0:T(8,128)(2,1)S(1)} %get-tuple-element.121), channel_id=1, source_target_pairs={{0,4},{1,5},{2,6},{3,7},{4,0},{5,1},{6,2},{7,3},{8,12},{9,13},{10,... | collective-permute-start | bytes 1179656 | tf_op jit(solution)/shard_map/ppermute | solution.py:244
  89.1 2.5 %collective-permute-start.19 = (bf16[96,2048]{1,0:T(8,128)(2,1)S(1)}, bf16[96,2048]{1,0:T(8,128)(2,1)S(1)}, u32[]{:S(2)}, u32[]{:S(2)}) collective-permute-start(bf16[96,2048]{1,0:T(8,128)(2,1)S(1)} %get-tuple-element.122), channel_id=1, source_target_pairs={{0,6},{1,7},{2,0},{3,1},{4,2},{5,3},{6,4},{7,5},{8,14},{9,15},{10,... | collective-permute-start | bytes 1179656 | tf_op jit(solution)/shard_map/ppermute | solution.py:244
  91.6 0.0 collective-permute-done.8.recv
  91.6 0.1 halve_z.1
  91.7 4.0 %collective-permute-start.9 = (bf16[272,256]{1,0:T(8,128)(2,1)S(1)}, bf16[272,256]{1,0:T(8,128)(2,1)S(1)}, u32[]{:S(2)}, u32[]{:S(2)}) collective-permute-start(bf16[272,256]{1,0:T(8,128)(2,1)S(1)} %get-tuple-element.99), channel_id=1, source_target_pairs={{0,48},{8,56},{16,32},{24,40},{32,16},{40,24},{48,0},{56,8},{64,11... | collective-permute-start | bytes 417800 | tf_op jit(solution)/shard_map/ppermute | solution.py:245
  95.7 4.9 %collective-permute-done.9.refs_1_ = bf16[272,256]{1,0:T(8,128)(2,1)S(1)} collective-permute-done((bf16[272,256]{1,0:T(8,128)(2,1)S(1)}, bf16[272,256]{1,0:T(8,128)(2,1)S(1)}, u32[]{:S(2)}, u32[]{:S(2)}) %collective-permute-start.9) | collective-permute-done | bytes 139296 | tf_op jit(solution)/shard_map/ppermute | solution.py:245
  100.6 0.0 copy-done.3
  100.6 0.0 copy-done.4
  100.6 0.9 outer_step.1
  101.5 1.3 %unpack_input_grad.1 = bf16[128,8192]{1,0:T(8,128)(2,1)} custom-call(bf16[128,2048]{1,0:T(8,128)(2,1)S(1)} %get-tuple-element.124.refs_0_, bf16[128,2048]{1,0:T(8,128)(2,1)S(1)} %collective-permute-done.14.refs_1_, bf16[128,2048]{1,0:T(8,128)(2,1)S(1)} %collective-permute-done.15.refs_2_, bf16[128,2048]{1,0:T(8,128)(2,1)S(1)} %collective-permute-done.16.refs_3_), custom_call_target="tpu_custom_call" | custom-call | tf_op jit(solution)/shard_map/unpack_input_grad/pallas_call | solution.py:41
  102.8 0.0 collective-permute-done.17.refs_1_
  102.8 0.0 collective-permute-done.18.refs_2_
  102.8 4.5 %collective-permute-done.19.refs_3_ = bf16[96,2048]{1,0:T(8,128)(2,1)S(1)} collective-permute-done((bf16[96,2048]{1,0:T(8,128)(2,1)S(1)}, bf16[96,2048]{1,0:T(8,128)(2,1)S(1)}, u32[]{:S(2)}, u32[]{:S(2)}) %collective-permute-start.19) | collective-permute-done | bytes 393248 | tf_op jit(solution)/shard_map/ppermute | solution.py:244
  107.3 1.1 %finish.1 = (bf16[64,8192]{1,0:T(8,128)(2,1)}, bf16[128,512]{1,0:T(8,128)(2,1)}) custom-call(bf16[96,2048]{1,0:T(8,128)(2,1)S(1)} %get-tuple-element.119.refs_0_, bf16[96,2048]{1,0:T(8,128)(2,1)S(1)} %collective-permute-done.17.refs_1_, bf16[96,2048]{1,0:T(8,128)(2,1)S(1)} %collective-permute-done.18.refs_2_, ...), custom_call_target="tpu_custom_call" | custom-call | tf_op jit(solution)/shard_map/finish/pallas_call | solution.py:41
  (2 shorter events, 0.0 us)
Async XLA Ops:
  0.6 9.5 %collective-permute-start.4 = (bf16[256,8192]{1,0:T(8,128)(2,1)}, bf16[256,8192]{1,0:T(8,128)(2,1)S(1)}, u32[]{:S(2)}, u32[]{:S(2)}) collective-permute-start(bf16[256,8192]{1,0:T(8,128)(2,1)} %bitcast.3), channel_id=1, source_target_pairs={{0,8},{8,0},{16,24},{24,16},{32,40},{40,32},{48,56},{56,48},{64,72... | collective-permute-start | bytes 12582920 | tf_op jit(solution)/shard_map/ppermute | solution.py:245
  0.7 1.2 %copy-start.2 = (bf16[1,64,8192]{2,1,0:T(8,128)(2,1)S(1)}, bf16[1,64,8192]{2,1,0:T(8,128)(2,1)}, u32[]{:S(2)}) copy-start(bf16[1,64,8192]{2,1,0:T(8,128)(2,1)} %param.12) | copy-start | bytes 3145732
  2.0 0.9 copy-start.5
  3.3 12.4 %collective-permute-start = (bf16[96,2048]{1,0:T(8,128)(2,1)S(1)}, bf16[96,2048]{1,0:T(8,128)(2,1)S(1)}, u32[]{:S(2)}, u32[]{:S(2)}) collective-permute-start(bf16[96,2048]{1,0:T(8,128)(2,1)S(1)} %get-tuple-element.72), channel_id=1, source_target_pairs={{0,2},{1,3},{2,4},{3,5},{4,6},{5,7},{6,0},{7,1},{8,10},{9,11},{10,... | collective-permute-start | bytes 1179656 | tf_op jit(solution)/shard_map/ppermute | solution.py:244
  5.0 13.5 %collective-permute-start.1 = (bf16[96,2048]{1,0:T(8,128)(2,1)S(1)}, bf16[96,2048]{1,0:T(8,128)(2,1)S(1)}, u32[]{:S(2)}, u32[]{:S(2)}) collective-permute-start(bf16[96,2048]{1,0:T(8,128)(2,1)S(1)} %get-tuple-element.73), channel_id=1, source_target_pairs={{0,4},{1,5},{2,6},{3,7},{4,0},{5,1},{6,2},{7,3},{8,12},{9,13},{10,... | collective-permute-start | bytes 1179656 | tf_op jit(solution)/shard_map/ppermute | solution.py:244
  7.7 18.5 %collective-permute-start.2 = (bf16[96,2048]{1,0:T(8,128)(2,1)S(1)}, bf16[96,2048]{1,0:T(8,128)(2,1)S(1)}, u32[]{:S(2)}, u32[]{:S(2)}) collective-permute-start(bf16[96,2048]{1,0:T(8,128)(2,1)S(1)} %get-tuple-element.74), channel_id=1, source_target_pairs={{0,6},{1,7},{2,0},{3,1},{4,2},{5,3},{6,4},{7,5},{8,14},{9,15},{10,... | collective-permute-start | bytes 1179656 | tf_op jit(solution)/shard_map/ppermute | solution.py:244
  9.0 1.2 %collective-permute-start.3 = (f32[1]{0:T(128)}, f32[1]{0:T(128)}, u32[]{:S(2)}, u32[]{:S(2)}) collective-permute-start(f32[1]{0:T(128)} %convert_element_type.3.counts), channel_id=1, source_target_pairs={{0,8},{8,0},{16,24},{24,16},{32,40},{40,32},{48,56},{56,48},{64,72... | collective-permute-start | bytes 20 | tf_op jit(solution)/shard_map/ppermute | solution.py:245
  10.2 2.2 %copy-start = (bf16[1,256,8192]{2,1,0:T(8,128)(2,1)S(1)}, bf16[1,256,8192]{2,1,0:T(8,128)(2,1)}, u32[]{:S(2)}) copy-start(bf16[1,256,8192]{2,1,0:T(8,128)(2,1)} %param.7) | copy-start | bytes 12582916
  12.4 3.2 %copy-start.1 = (bf16[128,8192]{1,0:T(8,128)(2,1)S(1)}, bf16[128,8192]{1,0:T(8,128)(2,1)}, u32[]{:S(2)}) copy-start(bf16[128,8192]{1,0:T(8,128)(2,1)} %x.1) | copy-start | bytes 6291460
  14.0 26.8 %collective-permute-start.5 = (bf16[272,2048]{1,0:T(8,128)(2,1)S(1)}, bf16[272,2048]{1,0:T(8,128)(2,1)S(1)}, u32[]{:S(2)}, u32[]{:S(2)}) collective-permute-start(bf16[272,2048]{1,0:T(8,128)(2,1)S(1)} %get-tuple-element.80), channel_id=1, source_target_pairs={{0,64},{8,72},{16,80},{24,88},{32,96},{40,104},{48,112},{56,120},{... | collective-permute-start | bytes 3342344 | tf_op jit(solution)/shard_map/ppermute | solution.py:245
  26.2 25.2 %collective-permute-start.6 = (bf16[256,2048]{1,0:T(8,128)(2,1)S(1)}, bf16[256,2048]{1,0:T(8,128)(2,1)S(1)}, u32[]{:S(2)}, u32[]{:S(2)}) collective-permute-start(bf16[256,2048]{1,0:T(8,128)(2,1)S(1)} %stack_weight.1), channel_id=1, source_target_pairs={{0,1},{1,0},{2,3},{3,2},{4,5},{5,4},{6,7},{7,6},{8,9},{9,8},{10,11... | collective-permute-start | bytes 3145736 | tf_op jit(solution)/shard_map/ppermute | solution.py:244
  27.5 25.3 %collective-permute-start.10 = (bf16[128,2048]{1,0:T(8,128)(2,1)S(1)}, bf16[128,2048]{1,0:T(8,128)(2,1)S(1)}, u32[]{:S(2)}, u32[]{:S(2)}) collective-permute-start(bf16[128,2048]{1,0:T(8,128)(2,1)S(1)} %get-tuple-element.103), channel_id=1, source_target_pairs={{0,2},{1,3},{2,4},{3,5},{4,6},{5,7},{6,0},{7,1},{8,10},{9,11},{10,... | collective-permute-start | bytes 1572872 | tf_op jit(solution)/shard_map/ppermute | solution.py:244
  28.8 24.0 %collective-permute-start.11 = (bf16[128,2048]{1,0:T(8,128)(2,1)S(1)}, bf16[128,2048]{1,0:T(8,128)(2,1)S(1)}, u32[]{:S(2)}, u32[]{:S(2)}) collective-permute-start(bf16[128,2048]{1,0:T(8,128)(2,1)S(1)} %get-tuple-element.104), channel_id=1, source_target_pairs={{0,4},{1,5},{2,6},{3,7},{4,0},{5,1},{6,2},{7,3},{8,12},{9,13},{10,... | collective-permute-start | bytes 1572872 | tf_op jit(solution)/shard_map/ppermute | solution.py:244
  30.4 23.8 %collective-permute-start.12 = (bf16[128,2048]{1,0:T(8,128)(2,1)S(1)}, bf16[128,2048]{1,0:T(8,128)(2,1)S(1)}, u32[]{:S(2)}, u32[]{:S(2)}) collective-permute-start(bf16[128,2048]{1,0:T(8,128)(2,1)S(1)} %get-tuple-element.105), channel_id=1, source_target_pairs={{0,6},{1,7},{2,0},{3,1},{4,2},{5,3},{6,4},{7,5},{8,14},{9,15},{10,... | collective-permute-start | bytes 1572872 | tf_op jit(solution)/shard_map/ppermute | solution.py:244
  41.0 15.2 %collective-permute-start.7 = (bf16[272,1024]{1,0:T(8,128)(2,1)S(1)}, bf16[272,1024]{1,0:T(8,128)(2,1)S(1)}, u32[]{:S(2)}, u32[]{:S(2)}) collective-permute-start(bf16[272,1024]{1,0:T(8,128)(2,1)S(1)} %get-tuple-element.92), channel_id=1, source_target_pairs={{0,192},{8,200},{16,208},{24,216},{32,224},{40,232},{48,240},{56,2... | collective-permute-start | bytes 1671176 | tf_op jit(solution)/shard_map/ppermute | solution.py:245
  55.6 31.1 %collective-permute-start.13 = (bf16[256,2048]{1,0:T(8,128)(2,1)S(1)}, bf16[256,2048]{1,0:T(8,128)(2,1)S(1)}, u32[]{:S(2)}, u32[]{:S(2)}) collective-permute-start(bf16[256,2048]{1,0:T(8,128)(2,1)S(1)} %get-tuple-element.108), channel_id=1, source_target_pairs={{0,1},{1,0},{2,3},{3,2},{4,5},{5,4},{6,7},{7,6},{8,9},{9,8},{10,11... | collective-permute-start | bytes 3145736 | tf_op jit(solution)/shard_map/ppermute | solution.py:244
  56.2 30.5 %collective-permute-start.14 = (bf16[128,2048]{1,0:T(8,128)(2,1)S(1)}, bf16[128,2048]{1,0:T(8,128)(2,1)S(1)}, u32[]{:S(2)}, u32[]{:S(2)}) collective-permute-start(bf16[128,2048]{1,0:T(8,128)(2,1)S(1)} %get-tuple-element.110), channel_id=1, source_target_pairs={{0,6},{1,7},{2,0},{3,1},{4,2},{5,3},{6,4},{7,5},{8,14},{9,15},{10,... | collective-permute-start | bytes 1572872 | tf_op jit(solution)/shard_map/ppermute | solution.py:244
  57.9 28.9 %collective-permute-start.15 = (bf16[128,2048]{1,0:T(8,128)(2,1)S(1)}, bf16[128,2048]{1,0:T(8,128)(2,1)S(1)}, u32[]{:S(2)}, u32[]{:S(2)}) collective-permute-start(bf16[128,2048]{1,0:T(8,128)(2,1)S(1)} %get-tuple-element.111), channel_id=1, source_target_pairs={{0,4},{1,5},{2,6},{3,7},{4,0},{5,1},{6,2},{7,3},{8,12},{9,13},{10,... | collective-permute-start | bytes 1572872 | tf_op jit(solution)/shard_map/ppermute | solution.py:244
  59.1 27.7 %collective-permute-start.16 = (bf16[128,2048]{1,0:T(8,128)(2,1)S(1)}, bf16[128,2048]{1,0:T(8,128)(2,1)S(1)}, u32[]{:S(2)}, u32[]{:S(2)}) collective-permute-start(bf16[128,2048]{1,0:T(8,128)(2,1)S(1)} %get-tuple-element.112), channel_id=1, source_target_pairs={{0,2},{1,3},{2,4},{3,5},{4,6},{5,7},{6,0},{7,1},{8,10},{9,11},{10,... | collective-permute-start | bytes 1572872 | tf_op jit(solution)/shard_map/ppermute | solution.py:244
  61.6 30.0 %collective-permute-start.8 = (bf16[272,512]{1,0:T(8,128)(2,1)S(1)}, bf16[272,512]{1,0:T(8,128)(2,1)S(1)}, u32[]{:S(2)}, u32[]{:S(2)}) collective-permute-start(bf16[272,512]{1,0:T(8,128)(2,1)S(1)} %get-tuple-element.97), channel_id=1, source_target_pairs={{0,16},{8,24},{16,0},{24,8},{32,48},{40,56},{48,32},{56,40},{64,80... | collective-permute-start | bytes 835592 | tf_op jit(solution)/shard_map/ppermute | solution.py:245
  65.4 35.2 %copy-start.3 = (f32[256,256]{1,0:T(8,128)S(1)}, f32[256,256]{1,0:T(8,128)}, u32[]{:S(2)}) copy-start(f32[256,256]{1,0:T(8,128)} %refs_2_.1) | copy-start | bytes 786436
  65.4 35.2 %copy-start.4 = (f32[256,256]{1,0:T(8,128)S(1)}, f32[256,256]{1,0:T(8,128)}, u32[]{:S(2)}) copy-start(f32[256,256]{1,0:T(8,128)} %refs_3_.1) | copy-start | bytes 786436
  87.0 15.8 %collective-permute-start.17 = (bf16[96,2048]{1,0:T(8,128)(2,1)S(1)}, bf16[96,2048]{1,0:T(8,128)(2,1)S(1)}, u32[]{:S(2)}, u32[]{:S(2)}) collective-permute-start(bf16[96,2048]{1,0:T(8,128)(2,1)S(1)} %get-tuple-element.120), channel_id=1, source_target_pairs={{0,2},{1,3},{2,4},{3,5},{4,6},{5,7},{6,0},{7,1},{8,10},{9,11},{10,... | collective-permute-start | bytes 1179656 | tf_op jit(solution)/shard_map/ppermute | solution.py:244
  87.1 15.7 %collective-permute-start.18 = (bf16[96,2048]{1,0:T(8,128)(2,1)S(1)}, bf16[96,2048]{1,0:T(8,128)(2,1)S(1)}, u32[]{:S(2)}, u32[]{:S(2)}) collective-permute-start(bf16[96,2048]{1,0:T(8,128)(2,1)S(1)} %get-tuple-element.121), channel_id=1, source_target_pairs={{0,4},{1,5},{2,6},{3,7},{4,0},{5,1},{6,2},{7,3},{8,12},{9,13},{10,... | collective-permute-start | bytes 1179656 | tf_op jit(solution)/shard_map/ppermute | solution.py:244
  89.1 18.2 %collective-permute-start.19 = (bf16[96,2048]{1,0:T(8,128)(2,1)S(1)}, bf16[96,2048]{1,0:T(8,128)(2,1)S(1)}, u32[]{:S(2)}, u32[]{:S(2)}) collective-permute-start(bf16[96,2048]{1,0:T(8,128)(2,1)S(1)} %get-tuple-element.122), channel_id=1, source_target_pairs={{0,6},{1,7},{2,0},{3,1},{4,2},{5,3},{6,4},{7,5},{8,14},{9,15},{10,... | collective-permute-start | bytes 1179656 | tf_op jit(solution)/shard_map/ppermute | solution.py:244
  91.7 8.9 %collective-permute-start.9 = (bf16[272,256]{1,0:T(8,128)(2,1)S(1)}, bf16[272,256]{1,0:T(8,128)(2,1)S(1)}, u32[]{:S(2)}, u32[]{:S(2)}) collective-permute-start(bf16[272,256]{1,0:T(8,128)(2,1)S(1)} %get-tuple-element.99), channel_id=1, source_target_pairs={{0,48},{8,56},{16,32},{24,40},{32,16},{40,24},{48,0},{56,8},{64,11... | collective-permute-start | bytes 417800 | tf_op jit(solution)/shard_map/ppermute | solution.py:245

commit v5 on v4

--- a/solution.py
+++ b/solution.py
@@ -294,15 +294,16 @@
     recv = fsdp(other, Z_SWAP)
     kept, send = call(sum_blocks, "sum_blocks", [(VMEM, kept), (VMEM, x_far)], [(VMEM, shape(272, 512))] * 2)
     (send,), (w_full,) = together((send,), (w_full,))
-    near = replica(send, ZH_NEAR)
     keys = call(project, "project", [(VMEM, a) for a in (*xs, w_full)], [(VMEM, shape(TOK, KVI))] * 4)
-    (recv,), back = together((recv,), back)
+    (recv,), (back[1], back[2]) = together((recv,), (back[1], back[2]))
     joined = call(
         join_grads,
         "join_grads",
         [(VMEM, a) for a in (mine, recv, *keys)],
         [(VMEM, shape(ROWS + 32, SEG))] * 4,
     )
+    joined, (send,) = together(joined, (send,))
+    near = replica(send, ZH_NEAR)
     joined = [joined[0]] + [fsdp(joined[j], y_shift(j)) for j in (1, 2, 3)]
     (back_full,) = call(
         unpack_columns, "unpack_input_grad", [(ANY, a) for a in back], [(ANY, shape(TOK, 8192))], [dma((4,))]
@@ -315,6 +316,7 @@
         [(VMEM, a) for a in (kept, far, master, momentum)],
         [(VMEM, shape(256, 256, dtype=F32))] * 2,
     )
+    joined, (new_master, new_momentum) = together(joined, (new_master, new_momentum))
     grads, projected = call(
         finish, "finish", [(VMEM, a) for a in joined], [(VMEM, shape(ROWS, 8192)), (VMEM, shape(TOK, KVI))]
     )

time: 109 us -> 109 us (level)
  waiting for transfers between devices: 59.2 us -> 58 us
    ppermute x14, waiting for transfers between devices: 45.2 us -> 38.3 us  [local(): fsdp = lambda a, perm: lax.ppermute(a, 'fsdp', perm)]
    ppermute x6, waiting for transfers between devices: 14.1 us -> 19.7 us  [local(): replica = lambda a, perm: lax.ppermute(a, 'replica', perm)]
  transfers between devices with their start and end apart: 20 -> 20, of which waited for: 10 -> 11; matrix products, arithmetic and copies ran while one was open for 0% -> 0% of each run, Pallas kernels for 9% -> 9%
where the time goes in v5:
time: 109 us; the launch traced here: 108 us
  waiting for transfers between devices  58 us (53%)
  starting transfers between devices  33.4 us (31%)
  Pallas kernels  10.4 us (10%)
  local copies, waits for them, and re-layouts  4.33 us (4%)
  between operations  1.44 us (1%)
    ppermute x14, waiting for transfers between devices, local(): fsdp = lambda a, perm: lax.ppermute(a, 'fsdp', perm)  38.3 us
    ppermute x14, starting transfers between devices, local(): fsdp = lambda a, perm: lax.ppermute(a, 'fsdp', perm)  22 us
    ppermute x6, waiting for transfers between devices, local(): replica = lambda a, perm: lax.ppermute(a, 'replica', perm)  19.7 us
    ppermute x6, starting transfers between devices, local(): replica = lambda a, perm: lax.ppermute(a, 'replica', perm)  11.4 us
    pallas_call x14, Pallas kernels, call(): pl.pallas_call(kernel, name=name, in_specs=[s for s, _ in ins], out_specs...  10.4 us
    unnamed x12, local copies, waits for them, and re-layouts  4.33 us
  transfers between devices with their start and end apart: 20, of which 11 were waited for; matrix products, arithmetic and copies ran while one was open for 0% of the time, Pallas kernels for 9%

profile of v5, /device:TPU:8, one launch (start us, length us, event | category | flops | bytes accessed | tf_op | source)
XLA Modules:
  0.0 107.7 jit_solution(160540690998795820)
XLA Ops:
  0.6 0.1 collective-permute-start.7
  0.7 0.0 copy-start.2
  0.7 1.2 %copy-done.2 = bf16[1,64,8192]{2,1,0:T(8,128)(2,1)S(1)} copy-done((bf16[1,64,8192]{2,1,0:T(8,128)(2,1)S(1)}, bf16[1,64,8192]{2,1,0:T(8,128)(2,1)}, u32[]{:S(2)}) %copy-start.2) | copy-done | bytes 1048600
  2.0 0.0 copy-start.5
  2.0 0.9 copy-done.5
  2.9 0.5 pack_weight.1
  3.3 1.7 %collective-permute-start = (bf16[96,2048]{1,0:T(8,128)(2,1)S(1)}, bf16[96,2048]{1,0:T(8,128)(2,1)S(1)}, u32[]{:S(2)}, u32[]{:S(2)}) collective-permute-start(bf16[96,2048]{1,0:T(8,128)(2,1)S(1)} %get-tuple-element.81), channel_id=1, source_target_pairs={{0,2},{1,3},{2,4},{3,5},{4,6},{5,7},{6,0},{7,1},{8,10},{9,11},{10,... | collective-permute-start | bytes 1179656 | tf_op jit(solution)/shard_map/ppermute | solution.py:244
  5.0 2.7 %collective-permute-start.1 = (bf16[96,2048]{1,0:T(8,128)(2,1)S(1)}, bf16[96,2048]{1,0:T(8,128)(2,1)S(1)}, u32[]{:S(2)}, u32[]{:S(2)}) collective-permute-start(bf16[96,2048]{1,0:T(8,128)(2,1)S(1)} %get-tuple-element.82), channel_id=1, source_target_pairs={{0,4},{1,5},{2,6},{3,7},{4,0},{5,1},{6,2},{7,3},{8,12},{9,13},{10,... | collective-permute-start | bytes 1179656 | tf_op jit(solution)/shard_map/ppermute | solution.py:244
  7.7 0.7 collective-permute-start.2
  9.0 0.9 collective-permute-start.6
  9.9 0.3 collective-permute-done.6.counts_other
  10.2 0.0 collective-permute-done.7.other
  10.2 2.2 %copy-done = bf16[1,256,8192]{2,1,0:T(8,128)(2,1)S(1)} copy-done((bf16[1,256,8192]{2,1,0:T(8,128)(2,1)S(1)}, bf16[1,256,8192]{2,1,0:T(8,128)(2,1)}, u32[]{:S(2)}) %copy-start) | copy-done | bytes 4194328
  12.4 1.6 %weigh.1 = (bf16[272,2048]{1,0:T(8,128)(2,1)S(1)}, bf16[272,2048]{1,0:T(8,128)(2,1)S(1)}) custom-call(f32[1]{0:T(128)} %convert_element_type.3.counts, f32[1]{0:T(128)} %collective-permute-done.6.counts_other, bf16[256,8192]{1,0:T(8,128)(2,1)S(1)} %bitcast.4, bf16[256,8192]{1,0:T(8,128)(2,1)S(1)} %collective-permute-done.7.other), custom_call_target="tpu_custom_call" | custom-call | tf_op jit(solution)/shard_map/weigh/pallas_call | solution.py:41
  14.0 1.6 %collective-permute-start.8 = (bf16[272,2048]{1,0:T(8,128)(2,1)S(1)}, bf16[272,2048]{1,0:T(8,128)(2,1)S(1)}, u32[]{:S(2)}, u32[]{:S(2)}) collective-permute-start(bf16[272,2048]{1,0:T(8,128)(2,1)S(1)} %get-tuple-element.93), channel_id=1, source_target_pairs={{0,64},{8,72},{16,80},{24,88},{32,96},{40,104},{48,112},{56,120},{... | collective-permute-start | bytes 3342344 | tf_op jit(solution)/shard_map/ppermute | solution.py:245
  15.5 0.0 copy-done.1
  15.5 0.2 pack_inputs.1
  15.7 0.0 collective-permute-done.refs_1_
  15.7 2.7 %collective-permute-done.1.refs_2_ = bf16[96,2048]{1,0:T(8,128)(2,1)S(1)} collective-permute-done((bf16[96,2048]{1,0:T(8,128)(2,1)S(1)}, bf16[96,2048]{1,0:T(8,128)(2,1)S(1)}, u32[]{:S(2)}, u32[]{:S(2)}) %collective-permute-start.1) | collective-permute-done | bytes 393248 | tf_op jit(solution)/shard_map/ppermute | solution.py:244
  18.5 7.7 %collective-permute-done.2.refs_3_ = bf16[96,2048]{1,0:T(8,128)(2,1)S(1)} collective-permute-done((bf16[96,2048]{1,0:T(8,128)(2,1)S(1)}, bf16[96,2048]{1,0:T(8,128)(2,1)S(1)}, u32[]{:S(2)}, u32[]{:S(2)}) %collective-permute-start.2) | collective-permute-done | bytes 393248 | tf_op jit(solution)/shard_map/ppermute | solution.py:244
  26.1 0.1 stack_weight.1
  26.2 1.3 %collective-permute-start.9 = (bf16[256,2048]{1,0:T(8,128)(2,1)S(1)}, bf16[256,2048]{1,0:T(8,128)(2,1)S(1)}, u32[]{:S(2)}, u32[]{:S(2)}) collective-permute-start(bf16[256,2048]{1,0:T(8,128)(2,1)S(1)} %stack_weight.1), channel_id=1, source_target_pairs={{0,1},{1,0},{2,3},{3,2},{4,5},{5,4},{6,7},{7,6},{8,9},{9,8},{10,11... | collective-permute-start | bytes 3145736 | tf_op jit(solution)/shard_map/ppermute | solution.py:244
  27.5 1.3 %collective-permute-start.3 = (bf16[128,2048]{1,0:T(8,128)(2,1)S(1)}, bf16[128,2048]{1,0:T(8,128)(2,1)S(1)}, u32[]{:S(2)}, u32[]{:S(2)}) collective-permute-start(bf16[128,2048]{1,0:T(8,128)(2,1)S(1)} %get-tuple-element.85), channel_id=1, source_target_pairs={{0,2},{1,3},{2,4},{3,5},{4,6},{5,7},{6,0},{7,1},{8,10},{9,11},{10,... | collective-permute-start | bytes 1572872 | tf_op jit(solution)/shard_map/ppermute | solution.py:244
  28.8 1.6 %collective-permute-start.4 = (bf16[128,2048]{1,0:T(8,128)(2,1)S(1)}, bf16[128,2048]{1,0:T(8,128)(2,1)S(1)}, u32[]{:S(2)}, u32[]{:S(2)}) collective-permute-start(bf16[128,2048]{1,0:T(8,128)(2,1)S(1)} %get-tuple-element.86), channel_id=1, source_target_pairs={{0,4},{1,5},{2,6},{3,7},{4,0},{5,1},{6,2},{7,3},{8,12},{9,13},{10,... | collective-permute-start | bytes 1572872 | tf_op jit(solution)/shard_map/ppermute | solution.py:244
  30.4 1.6 %collective-permute-start.5 = (bf16[128,2048]{1,0:T(8,128)(2,1)S(1)}, bf16[128,2048]{1,0:T(8,128)(2,1)S(1)}, u32[]{:S(2)}, u32[]{:S(2)}) collective-permute-start(bf16[128,2048]{1,0:T(8,128)(2,1)S(1)} %get-tuple-element.87), channel_id=1, source_target_pairs={{0,6},{1,7},{2,0},{3,1},{4,2},{5,3},{6,4},{7,5},{8,14},{9,15},{10,... | collective-permute-start | bytes 1572872 | tf_op jit(solution)/shard_map/ppermute | solution.py:244
  32.0 8.8 %collective-permute-done.8.recv = bf16[272,2048]{1,0:T(8,128)(2,1)S(1)} collective-permute-done((bf16[272,2048]{1,0:T(8,128)(2,1)S(1)}, bf16[272,2048]{1,0:T(8,128)(2,1)S(1)}, u32[]{:S(2)}, u32[]{:S(2)}) %collective-permute-start.8) | collective-permute-done | bytes 1114144 | tf_op jit(solution)/shard_map/ppermute | solution.py:245
  40.8 0.2 halve_x.1
  41.0 2.8 %collective-permute-start.11 = (bf16[272,1024]{1,0:T(8,128)(2,1)S(1)}, bf16[272,1024]{1,0:T(8,128)(2,1)S(1)}, u32[]{:S(2)}, u32[]{:S(2)}) collective-permute-start(bf16[272,1024]{1,0:T(8,128)(2,1)S(1)} %get-tuple-element.107), channel_id=1, source_target_pairs={{0,192},{8,200},{16,208},{24,216},{32,224},{40,232},{48,240},{56,2... | collective-permute-start | bytes 1671176 | tf_op jit(solution)/shard_map/ppermute | solution.py:245
  43.8 7.5 %collective-permute-done.9.refs_4_ = bf16[256,2048]{1,0:T(8,128)(2,1)S(1)} collective-permute-done((bf16[256,2048]{1,0:T(8,128)(2,1)S(1)}, bf16[256,2048]{1,0:T(8,128)(2,1)S(1)}, u32[]{:S(2)}, u32[]{:S(2)}) %collective-permute-start.9) | collective-permute-done | bytes 1048608 | tf_op jit(solution)/shard_map/ppermute | solution.py:244
  51.4 1.4 %input_grad.1 = (bf16[128,2048]{1,0:T(8,128)(2,1)S(1)}, bf16[128,2048]{1,0:T(8,128)(2,1)S(1)}, bf16[128,2048]{1,0:T(8,128)(2,1)S(1)}, bf16[128,2048]{1,0:T(8,128...) custom-call(bf16[96,2048]{1,0:T(8,128)(2,1)S(1)} %get-tuple-element.96.refs_0_, ...), custom_call_target="tpu_custom_call" | custom-call | tf_op jit(solution)/shard_map/input_grad/pallas_call | solution.py:41
  52.8 0.0 collective-permute-done.3.refs_1_
  52.8 0.0 collective-permute-done.4.refs_2_
  52.8 1.4 %collective-permute-done.5.refs_3_ = bf16[128,2048]{1,0:T(8,128)(2,1)S(1)} collective-permute-done((bf16[128,2048]{1,0:T(8,128)(2,1)S(1)}, bf16[128,2048]{1,0:T(8,128)(2,1)S(1)}, u32[]{:S(2)}, u32[]{:S(2)}) %collective-permute-start.5) | collective-permute-done | bytes 524320 | tf_op jit(solution)/shard_map/ppermute | solution.py:244
  54.2 1.4 %weight_grad.1 = (bf16[256,2048]{1,0:T(8,128)(2,1)S(1)}, bf16[256,2048]{1,0:T(8,128)(2,1)S(1)}) custom-call(bf16[128,2048]{1,0:T(8,128)(2,1)S(1)} %get-tuple-element.84.refs_0_, bf16[128,2048]{1,0:T(8,128)(2,1)S(1)} %collective-permute-done.3.refs_1_, bf16[128,2048]{1,0:T(8,128)(2,1)S(1)} %collective-permute-done.4.refs_2_, ...), custom_call_target="tpu_custom_call" | custom-call | tf_op jit(solution)/shard_map/weight_grad/pallas_call | solution.py:41
  55.6 0.5 collective-permute-start.10
  56.1 0.1 collective-permute-done.11.recv
  56.2 1.7 %collective-permute-start.12 = (bf16[128,2048]{1,0:T(8,128)(2,1)S(1)}, bf16[128,2048]{1,0:T(8,128)(2,1)S(1)}, u32[]{:S(2)}, u32[]{:S(2)}) collective-permute-start(bf16[128,2048]{1,0:T(8,128)(2,1)S(1)} %get-tuple-element.108), channel_id=1, source_target_pairs={{0,6},{1,7},{2,0},{3,1},{4,2},{5,3},{6,4},{7,5},{8,14},{9,15},{10,... | collective-permute-start | bytes 1572872 | tf_op jit(solution)/shard_map/ppermute | solution.py:244
  57.9 1.1 %collective-permute-start.13 = (bf16[128,2048]{1,0:T(8,128)(2,1)S(1)}, bf16[128,2048]{1,0:T(8,128)(2,1)S(1)}, u32[]{:S(2)}, u32[]{:S(2)}) collective-permute-start(bf16[128,2048]{1,0:T(8,128)(2,1)S(1)} %get-tuple-element.109), channel_id=1, source_target_pairs={{0,4},{1,5},{2,6},{3,7},{4,0},{5,1},{6,2},{7,3},{8,12},{9,13},{10,... | collective-permute-start | bytes 1572872 | tf_op jit(solution)/shard_map/ppermute | solution.py:244
  59.1 2.4 %collective-permute-start.19 = (bf16[128,2048]{1,0:T(8,128)(2,1)S(1)}, bf16[128,2048]{1,0:T(8,128)(2,1)S(1)}, u32[]{:S(2)}, u32[]{:S(2)}) collective-permute-start(bf16[128,2048]{1,0:T(8,128)(2,1)S(1)} %get-tuple-element.145), channel_id=1, source_target_pairs={{0,2},{1,3},{2,4},{3,5},{4,6},{5,7},{6,0},{7,1},{8,10},{9,11},{10,... | collective-permute-start | bytes 1572872 | tf_op jit(solution)/shard_map/ppermute | solution.py:244
  61.4 0.2 sum_blocks.1
  61.6 1.3 %project.1 = (bf16[128,512]{1,0:T(8,128)(2,1)S(1)}, bf16[128,512]{1,0:T(8,128)(2,1)S(1)}, bf16[128,512]{1,0:T(8,128)(2,1)S(1)}, bf16[128,512]{1,0:T(8,128)(2,1)S(1)}) custom-call(bf16[128,2048]{1,0:T(8,128)(2,1)S(1)} %get-tuple-element.84.refs_0_, bf16[128,2048]{1,0:T(8,128)(2,1)S(1)} %collective-permute-done.3.refs_1_, ...), custom_call_target="tpu_custom_call" | custom-call | tf_op jit(solution)/shard_map/project/pallas_call | solution.py:41
  62.9 17.9 %collective-permute-done.10.recv = bf16[256,2048]{1,0:T(8,128)(2,1)S(1)} collective-permute-done((bf16[256,2048]{1,0:T(8,128)(2,1)S(1)}, bf16[256,2048]{1,0:T(8,128)(2,1)S(1)}, u32[]{:S(2)}, u32[]{:S(2)}) %collective-permute-start.10) | collective-permute-done | bytes 1048608 | tf_op jit(solution)/shard_map/ppermute | solution.py:244
  80.8 0.0 collective-permute-done.12.refs_1_
  80.8 1.1 collective-permute-done.13.refs_2_
  81.9 0.2 join_grads.1
  82.1 2.5 %collective-permute-start.17 = (bf16[272,512]{1,0:T(8,128)(2,1)S(1)}, bf16[272,512]{1,0:T(8,128)(2,1)S(1)}, u32[]{:S(2)}, u32[]{:S(2)}) collective-permute-start(bf16[272,512]{1,0:T(8,128)(2,1)S(1)} %get-tuple-element.130), channel_id=1, source_target_pairs={{0,16},{8,24},{16,0},{24,8},{32,48},{40,56},{48,32},{56,40},{64,80... | collective-permute-start | bytes 835592 | tf_op jit(solution)/shard_map/ppermute | solution.py:245
  84.6 0.0 collective-permute-start.14
  84.6 3.0 %collective-permute-start.15 = (bf16[96,2048]{1,0:T(8,128)(2,1)S(1)}, bf16[96,2048]{1,0:T(8,128)(2,1)S(1)}, u32[]{:S(2)}, u32[]{:S(2)}) collective-permute-start(bf16[96,2048]{1,0:T(8,128)(2,1)S(1)} %get-tuple-element.127), channel_id=1, source_target_pairs={{0,4},{1,5},{2,6},{3,7},{4,0},{5,1},{6,2},{7,3},{8,12},{9,13},{10,... | collective-permute-start | bytes 1179656 | tf_op jit(solution)/shard_map/ppermute | solution.py:244
  87.6 2.6 %collective-permute-start.16 = (bf16[96,2048]{1,0:T(8,128)(2,1)S(1)}, bf16[96,2048]{1,0:T(8,128)(2,1)S(1)}, u32[]{:S(2)}, u32[]{:S(2)}) collective-permute-start(bf16[96,2048]{1,0:T(8,128)(2,1)S(1)} %get-tuple-element.128), channel_id=1, source_target_pairs={{0,6},{1,7},{2,0},{3,1},{4,2},{5,3},{6,4},{7,5},{8,14},{9,15},{10,... | collective-permute-start | bytes 1179656 | tf_op jit(solution)/shard_map/ppermute | solution.py:244
  90.2 6.3 %collective-permute-done.17.recv = bf16[272,512]{1,0:T(8,128)(2,1)S(1)} collective-permute-done((bf16[272,512]{1,0:T(8,128)(2,1)S(1)}, bf16[272,512]{1,0:T(8,128)(2,1)S(1)}, u32[]{:S(2)}, u32[]{:S(2)}) %collective-permute-start.17) | collective-permute-done | bytes 278560 | tf_op jit(solution)/shard_map/ppermute | solution.py:245
  96.5 0.1 halve_z.1
  96.6 0.0 copy-start.3
  96.6 0.0 copy-start.4
  96.6 3.4 %collective-permute-start.18 = (bf16[272,256]{1,0:T(8,128)(2,1)S(1)}, bf16[272,256]{1,0:T(8,128)(2,1)S(1)}, u32[]{:S(2)}, u32[]{:S(2)}) collective-permute-start(bf16[272,256]{1,0:T(8,128)(2,1)S(1)} %get-tuple-element.132), channel_id=1, source_target_pairs={{0,48},{8,56},{16,32},{24,40},{32,16},{40,24},{48,0},{56,8},{64,11... | collective-permute-start | bytes 417800 | tf_op jit(solution)/shard_map/ppermute | solution.py:245
  100.0 0.0 collective-permute-done.19.refs_3_
  100.0 1.3 %unpack_input_grad.1 = bf16[128,8192]{1,0:T(8,128)(2,1)} custom-call(bf16[128,2048]{1,0:T(8,128)(2,1)S(1)} %get-tuple-element.142.refs_0_, bf16[128,2048]{1,0:T(8,128)(2,1)S(1)} %collective-permute-done.12.refs_1_, bf16[128,2048]{1,0:T(8,128)(2,1)S(1)} %collective-permute-done.13.refs_2_, bf16[128,2048]{1,0:T(8,128)(2,1)S(1)} %collective-permute-done.19.refs_3_), custom_call_target="tpu_custom_call" | custom-call | tf_op jit(solution)/shard_map/unpack_input_grad/pallas_call | solution.py:41
  101.4 4.3 %collective-permute-done.18.refs_1_ = bf16[272,256]{1,0:T(8,128)(2,1)S(1)} collective-permute-done((bf16[272,256]{1,0:T(8,128)(2,1)S(1)}, bf16[272,256]{1,0:T(8,128)(2,1)S(1)}, u32[]{:S(2)}, u32[]{:S(2)}) %collective-permute-start.18) | collective-permute-done | bytes 139296 | tf_op jit(solution)/shard_map/ppermute | solution.py:245
  105.7 0.0 copy-done.3
  105.7 0.0 copy-done.4
  105.7 0.9 outer_step.1
  106.5 0.0 collective-permute-done.14.refs_1_
  106.5 0.0 collective-permute-done.15.refs_2_
  106.6 0.0 collective-permute-done.16.refs_3_
  106.6 1.1 %finish.1 = (bf16[64,8192]{1,0:T(8,128)(2,1)}, bf16[128,512]{1,0:T(8,128)(2,1)}) custom-call(bf16[96,2048]{1,0:T(8,128)(2,1)S(1)} %get-tuple-element.137.refs_0_, bf16[96,2048]{1,0:T(8,128)(2,1)S(1)} %collective-permute-done.14.refs_1_, bf16[96,2048]{1,0:T(8,128)(2,1)S(1)} %collective-permute-done.15.refs_2_, ...), custom_call_target="tpu_custom_call" | custom-call | tf_op jit(solution)/shard_map/finish/pallas_call | solution.py:41
  (2 shorter events, 0.0 us)
Async XLA Ops:
  0.6 9.5 %collective-permute-start.7 = (bf16[256,8192]{1,0:T(8,128)(2,1)}, bf16[256,8192]{1,0:T(8,128)(2,1)S(1)}, u32[]{:S(2)}, u32[]{:S(2)}) collective-permute-start(bf16[256,8192]{1,0:T(8,128)(2,1)} %bitcast.3), channel_id=1, source_target_pairs={{0,8},{8,0},{16,24},{24,16},{32,40},{40,32},{48,56},{56,48},{64,72... | collective-permute-start | bytes 12582920 | tf_op jit(solution)/shard_map/ppermute | solution.py:245
  0.7 1.2 %copy-start.2 = (bf16[1,64,8192]{2,1,0:T(8,128)(2,1)S(1)}, bf16[1,64,8192]{2,1,0:T(8,128)(2,1)}, u32[]{:S(2)}) copy-start(bf16[1,64,8192]{2,1,0:T(8,128)(2,1)} %param.12) | copy-start | bytes 3145732
  2.0 0.9 copy-start.5
  3.3 12.4 %collective-permute-start = (bf16[96,2048]{1,0:T(8,128)(2,1)S(1)}, bf16[96,2048]{1,0:T(8,128)(2,1)S(1)}, u32[]{:S(2)}, u32[]{:S(2)}) collective-permute-start(bf16[96,2048]{1,0:T(8,128)(2,1)S(1)} %get-tuple-element.81), channel_id=1, source_target_pairs={{0,2},{1,3},{2,4},{3,5},{4,6},{5,7},{6,0},{7,1},{8,10},{9,11},{10,... | collective-permute-start | bytes 1179656 | tf_op jit(solution)/shard_map/ppermute | solution.py:244
  5.0 13.5 %collective-permute-start.1 = (bf16[96,2048]{1,0:T(8,128)(2,1)S(1)}, bf16[96,2048]{1,0:T(8,128)(2,1)S(1)}, u32[]{:S(2)}, u32[]{:S(2)}) collective-permute-start(bf16[96,2048]{1,0:T(8,128)(2,1)S(1)} %get-tuple-element.82), channel_id=1, source_target_pairs={{0,4},{1,5},{2,6},{3,7},{4,0},{5,1},{6,2},{7,3},{8,12},{9,13},{10,... | collective-permute-start | bytes 1179656 | tf_op jit(solution)/shard_map/ppermute | solution.py:244
  7.7 18.5 %collective-permute-start.2 = (bf16[96,2048]{1,0:T(8,128)(2,1)S(1)}, bf16[96,2048]{1,0:T(8,128)(2,1)S(1)}, u32[]{:S(2)}, u32[]{:S(2)}) collective-permute-start(bf16[96,2048]{1,0:T(8,128)(2,1)S(1)} %get-tuple-element.83), channel_id=1, source_target_pairs={{0,6},{1,7},{2,0},{3,1},{4,2},{5,3},{6,4},{7,5},{8,14},{9,15},{10,... | collective-permute-start | bytes 1179656 | tf_op jit(solution)/shard_map/ppermute | solution.py:244
  9.0 1.2 %collective-permute-start.6 = (f32[1]{0:T(128)}, f32[1]{0:T(128)}, u32[]{:S(2)}, u32[]{:S(2)}) collective-permute-start(f32[1]{0:T(128)} %convert_element_type.3.counts), channel_id=1, source_target_pairs={{0,8},{8,0},{16,24},{24,16},{32,40},{40,32},{48,56},{56,48},{64,72... | collective-permute-start | bytes 20 | tf_op jit(solution)/shard_map/ppermute | solution.py:245
  10.2 2.2 %copy-start = (bf16[1,256,8192]{2,1,0:T(8,128)(2,1)S(1)}, bf16[1,256,8192]{2,1,0:T(8,128)(2,1)}, u32[]{:S(2)}) copy-start(bf16[1,256,8192]{2,1,0:T(8,128)(2,1)} %param.7) | copy-start | bytes 12582916
  12.4 3.2 %copy-start.1 = (bf16[128,8192]{1,0:T(8,128)(2,1)S(1)}, bf16[128,8192]{1,0:T(8,128)(2,1)}, u32[]{:S(2)}) copy-start(bf16[128,8192]{1,0:T(8,128)(2,1)} %x.1) | copy-start | bytes 6291460
  14.0 26.8 %collective-permute-start.8 = (bf16[272,2048]{1,0:T(8,128)(2,1)S(1)}, bf16[272,2048]{1,0:T(8,128)(2,1)S(1)}, u32[]{:S(2)}, u32[]{:S(2)}) collective-permute-start(bf16[272,2048]{1,0:T(8,128)(2,1)S(1)} %get-tuple-element.93), channel_id=1, source_target_pairs={{0,64},{8,72},{16,80},{24,88},{32,96},{40,104},{48,112},{56,120},{... | collective-permute-start | bytes 3342344 | tf_op jit(solution)/shard_map/ppermute | solution.py:245
  26.2 25.2 %collective-permute-start.9 = (bf16[256,2048]{1,0:T(8,128)(2,1)S(1)}, bf16[256,2048]{1,0:T(8,128)(2,1)S(1)}, u32[]{:S(2)}, u32[]{:S(2)}) collective-permute-start(bf16[256,2048]{1,0:T(8,128)(2,1)S(1)} %stack_weight.1), channel_id=1, source_target_pairs={{0,1},{1,0},{2,3},{3,2},{4,5},{5,4},{6,7},{7,6},{8,9},{9,8},{10,11... | collective-permute-start | bytes 3145736 | tf_op jit(solution)/shard_map/ppermute | solution.py:244
  27.5 25.3 %collective-permute-start.3 = (bf16[128,2048]{1,0:T(8,128)(2,1)S(1)}, bf16[128,2048]{1,0:T(8,128)(2,1)S(1)}, u32[]{:S(2)}, u32[]{:S(2)}) collective-permute-start(bf16[128,2048]{1,0:T(8,128)(2,1)S(1)} %get-tuple-element.85), channel_id=1, source_target_pairs={{0,2},{1,3},{2,4},{3,5},{4,6},{5,7},{6,0},{7,1},{8,10},{9,11},{10,... | collective-permute-start | bytes 1572872 | tf_op jit(solution)/shard_map/ppermute | solution.py:244
  28.8 24.0 %collective-permute-start.4 = (bf16[128,2048]{1,0:T(8,128)(2,1)S(1)}, bf16[128,2048]{1,0:T(8,128)(2,1)S(1)}, u32[]{:S(2)}, u32[]{:S(2)}) collective-permute-start(bf16[128,2048]{1,0:T(8,128)(2,1)S(1)} %get-tuple-element.86), channel_id=1, source_target_pairs={{0,4},{1,5},{2,6},{3,7},{4,0},{5,1},{6,2},{7,3},{8,12},{9,13},{10,... | collective-permute-start | bytes 1572872 | tf_op jit(solution)/shard_map/ppermute | solution.py:244
  30.4 23.8 %collective-permute-start.5 = (bf16[128,2048]{1,0:T(8,128)(2,1)S(1)}, bf16[128,2048]{1,0:T(8,128)(2,1)S(1)}, u32[]{:S(2)}, u32[]{:S(2)}) collective-permute-start(bf16[128,2048]{1,0:T(8,128)(2,1)S(1)} %get-tuple-element.87), channel_id=1, source_target_pairs={{0,6},{1,7},{2,0},{3,1},{4,2},{5,3},{6,4},{7,5},{8,14},{9,15},{10,... | collective-permute-start | bytes 1572872 | tf_op jit(solution)/shard_map/ppermute | solution.py:244
  41.0 15.2 %collective-permute-start.11 = (bf16[272,1024]{1,0:T(8,128)(2,1)S(1)}, bf16[272,1024]{1,0:T(8,128)(2,1)S(1)}, u32[]{:S(2)}, u32[]{:S(2)}) collective-permute-start(bf16[272,1024]{1,0:T(8,128)(2,1)S(1)} %get-tuple-element.107), channel_id=1, source_target_pairs={{0,192},{8,200},{16,208},{24,216},{32,224},{40,232},{48,240},{56,2... | collective-permute-start | bytes 1671176 | tf_op jit(solution)/shard_map/ppermute | solution.py:245
  55.6 25.2 %collective-permute-start.10 = (bf16[256,2048]{1,0:T(8,128)(2,1)S(1)}, bf16[256,2048]{1,0:T(8,128)(2,1)S(1)}, u32[]{:S(2)}, u32[]{:S(2)}) collective-permute-start(bf16[256,2048]{1,0:T(8,128)(2,1)S(1)} %get-tuple-element.102), channel_id=1, source_target_pairs={{0,1},{1,0},{2,3},{3,2},{4,5},{5,4},{6,7},{7,6},{8,9},{9,8},{10,11... | collective-permute-start | bytes 3145736 | tf_op jit(solution)/shard_map/ppermute | solution.py:244
  56.2 24.6 %collective-permute-start.12 = (bf16[128,2048]{1,0:T(8,128)(2,1)S(1)}, bf16[128,2048]{1,0:T(8,128)(2,1)S(1)}, u32[]{:S(2)}, u32[]{:S(2)}) collective-permute-start(bf16[128,2048]{1,0:T(8,128)(2,1)S(1)} %get-tuple-element.108), channel_id=1, source_target_pairs={{0,6},{1,7},{2,0},{3,1},{4,2},{5,3},{6,4},{7,5},{8,14},{9,15},{10,... | collective-permute-start | bytes 1572872 | tf_op jit(solution)/shard_map/ppermute | solution.py:244
  57.9 24.0 %collective-permute-start.13 = (bf16[128,2048]{1,0:T(8,128)(2,1)S(1)}, bf16[128,2048]{1,0:T(8,128)(2,1)S(1)}, u32[]{:S(2)}, u32[]{:S(2)}) collective-permute-start(bf16[128,2048]{1,0:T(8,128)(2,1)S(1)} %get-tuple-element.109), channel_id=1, source_target_pairs={{0,4},{1,5},{2,6},{3,7},{4,0},{5,1},{6,2},{7,3},{8,12},{9,13},{10,... | collective-permute-start | bytes 1572872 | tf_op jit(solution)/shard_map/ppermute | solution.py:244
  59.1 41.0 %collective-permute-start.19 = (bf16[128,2048]{1,0:T(8,128)(2,1)S(1)}, bf16[128,2048]{1,0:T(8,128)(2,1)S(1)}, u32[]{:S(2)}, u32[]{:S(2)}) collective-permute-start(bf16[128,2048]{1,0:T(8,128)(2,1)S(1)} %get-tuple-element.145), channel_id=1, source_target_pairs={{0,2},{1,3},{2,4},{3,5},{4,6},{5,7},{6,0},{7,1},{8,10},{9,11},{10,... | collective-permute-start | bytes 1572872 | tf_op jit(solution)/shard_map/ppermute | solution.py:244
  82.1 14.4 %collective-permute-start.17 = (bf16[272,512]{1,0:T(8,128)(2,1)S(1)}, bf16[272,512]{1,0:T(8,128)(2,1)S(1)}, u32[]{:S(2)}, u32[]{:S(2)}) collective-permute-start(bf16[272,512]{1,0:T(8,128)(2,1)S(1)} %get-tuple-element.130), channel_id=1, source_target_pairs={{0,16},{8,24},{16,0},{24,8},{32,48},{40,56},{48,32},{56,40},{64,80... | collective-permute-start | bytes 835592 | tf_op jit(solution)/shard_map/ppermute | solution.py:245
  84.6 21.9 %collective-permute-start.14 = (bf16[96,2048]{1,0:T(8,128)(2,1)S(1)}, bf16[96,2048]{1,0:T(8,128)(2,1)S(1)}, u32[]{:S(2)}, u32[]{:S(2)}) collective-permute-start(bf16[96,2048]{1,0:T(8,128)(2,1)S(1)} %get-tuple-element.126), channel_id=1, source_target_pairs={{0,2},{1,3},{2,4},{3,5},{4,6},{5,7},{6,0},{7,1},{8,10},{9,11},{10,... | collective-permute-start | bytes 1179656 | tf_op jit(solution)/shard_map/ppermute | solution.py:244
  84.6 21.9 %collective-permute-start.15 = (bf16[96,2048]{1,0:T(8,128)(2,1)S(1)}, bf16[96,2048]{1,0:T(8,128)(2,1)S(1)}, u32[]{:S(2)}, u32[]{:S(2)}) collective-permute-start(bf16[96,2048]{1,0:T(8,128)(2,1)S(1)} %get-tuple-element.127), channel_id=1, source_target_pairs={{0,4},{1,5},{2,6},{3,7},{4,0},{5,1},{6,2},{7,3},{8,12},{9,13},{10,... | collective-permute-start | bytes 1179656 | tf_op jit(solution)/shard_map/ppermute | solution.py:244
  87.6 19.0 %collective-permute-start.16 = (bf16[96,2048]{1,0:T(8,128)(2,1)S(1)}, bf16[96,2048]{1,0:T(8,128)(2,1)S(1)}, u32[]{:S(2)}, u32[]{:S(2)}) collective-permute-start(bf16[96,2048]{1,0:T(8,128)(2,1)S(1)} %get-tuple-element.128), channel_id=1, source_target_pairs={{0,6},{1,7},{2,0},{3,1},{4,2},{5,3},{6,4},{7,5},{8,14},{9,15},{10,... | collective-permute-start | bytes 1179656 | tf_op jit(solution)/shard_map/ppermute | solution.py:244
  96.6 9.1 %copy-start.3 = (f32[256,256]{1,0:T(8,128)S(1)}, f32[256,256]{1,0:T(8,128)}, u32[]{:S(2)}) copy-start(f32[256,256]{1,0:T(8,128)} %refs_2_.1) | copy-start | bytes 786436
  96.6 9.1 %copy-start.4 = (f32[256,256]{1,0:T(8,128)S(1)}, f32[256,256]{1,0:T(8,128)}, u32[]{:S(2)}) copy-start(f32[256,256]{1,0:T(8,128)} %refs_3_.1) | copy-start | bytes 786436
  96.6 9.0 %collective-permute-start.18 = (bf16[272,256]{1,0:T(8,128)(2,1)S(1)}, bf16[272,256]{1,0:T(8,128)(2,1)S(1)}, u32[]{:S(2)}, u32[]{:S(2)}) collective-permute-start(bf16[272,256]{1,0:T(8,128)(2,1)S(1)} %get-tuple-element.132), channel_id=1, source_target_pairs={{0,48},{8,56},{16,32},{24,40},{32,16},{40,24},{48,0},{56,8},{64,11... | collective-permute-start | bytes 417800 | tf_op jit(solution)/shard_map/ppermute | solution.py:245
